TPU v7x, 32 devices: a whole 2x2x4 slice. The times are simulated.
32 devices in a mesh: crop: 2 (over core), axial: 16 (over z, y, x).
Axes of the slice: x: 2, y: 2, z: 4, core: 2. Of those that a mesh axis runs over, the one named last changes fastest.
Arguments:
- pair: bfloat16 [2, 64, 64, 128], P('crop', 'axial'), may hold values from -6 to 6
- crop_mask: int32 [2, 64], P('crop'), may hold values 0 or 1
- weights: bfloat16 [128, 768], replicated, may hold values from -0.5 to 0.5
- probe_signs: int32 [128, 768], replicated, may hold values from 0 to 1
Outputs:
- pair_out: bfloat16 [2, 64, 64, 128], P('crop', 'axial')
- curvature: float32 [128, 768], replicated
All inputs are finite; a program needn't handle non-finite values. No bound on the sum of `crop_mask` on one device may be relied on, other than what follows from the above.
Results may differ from a plain program's by a relative error of at most 0.006.
Values may be sent and summed in bfloat16 or wider, within the bound.
No kernel may reach another device: no remote copies, remote signals or barrier semaphores. Data moves between devices by JAX's collectives and lax.ppermute only.
A program may use at most 64 MiB of HBM per device.

v0:
```python
import jax
import jax.numpy as jnp
from jax import lax
from jax.sharding import PartitionSpec as P


def norm_axis(value, axis):
    mean = jnp.mean(value, axis=axis, keepdims=True)
    centered = value - mean
    var = jnp.mean(centered * centered, axis=axis, keepdims=True)
    return centered * lax.rsqrt(var + 1e-05)


def project_in(w_in, zn_bf, mask_pair):
    proj = jnp.einsum(
        "rnc,cd->drn", zn_bf, w_in.astype(jnp.bfloat16), preferred_element_type=jnp.float32
    )
    hid = proj.shape[0] // 4
    a_full = jax.nn.sigmoid(proj[hid : 2 * hid]) * proj[:hid] * mask_pair
    b_full = jax.nn.sigmoid(proj[3 * hid :]) * proj[2 * hid : 3 * hid] * mask_pair
    return (a_full, b_full)


def head(w_head, x_full, zn_bf):
    chans = zn_bf.shape[2]
    w_gate = w_head[:, :chans].astype(jnp.bfloat16)
    w_out = w_head[:, chans:].astype(jnp.bfloat16)
    x_norm = norm_axis(x_full, 0).astype(jnp.bfloat16)
    out_proj = jnp.einsum("hrn,hc->rnc", x_norm, w_out, preferred_element_type=jnp.float32)
    gating = jax.nn.sigmoid(
        jnp.einsum("rnc,cd->rnd", zn_bf, w_gate, preferred_element_type=jnp.float32)
    )
    return gating * out_proj


def tri_out(left, right):
    return jnp.einsum("cik,cjk->cij", left, right, preferred_element_type=jnp.float32)


def slab_products(slabs):
    a_ch, b_ch, ta_ch, tb_ch = slabs
    x_ch = tri_out(a_ch, b_ch).astype(jnp.bfloat16)
    tx_ch = (tri_out(ta_ch, b_ch) + tri_out(a_ch, tb_ch)).astype(jnp.bfloat16)
    return (x_ch, tx_ch, a_ch, b_ch)


def shards(pair, crop_mask, weights, probe_signs):
    pair_rows = pair[0]
    rows = pair_rows.shape[0]
    width = pair_rows.shape[1]
    chans = weights.shape[0]
    h4 = weights.shape[1] - 2 * chans
    mask = crop_mask[0].astype(jnp.float32)
    start = lax.axis_index("axial") * rows
    mask_rows = lax.dynamic_slice_in_dim(mask, start, rows, 0)
    mask_pair = mask_rows[:, None] * mask[None, :]
    zn = norm_axis(pair_rows.astype(jnp.float32), 2).astype(jnp.bfloat16)
    w_all = weights.astype(jnp.float32)
    probe = (2 * probe_signs - 1).astype(jnp.float32) * (1.0 / jnp.sqrt(jnp.float32(chans)))
    w_in, w_head = (w_all[:, :h4], w_all[:, h4:])
    v_in, v_head = (probe[:, :h4], probe[:, h4:])
    fin = lambda w: project_in(w, zn, mask_pair)
    (a_f, b_f), pull_in = jax.vjp(fin, w_in)
    _, (ta_f, tb_f) = jax.jvp(fin, (w_in,), (v_in,))
    a_bf, b_bf = (a_f.astype(jnp.bfloat16), b_f.astype(jnp.bfloat16))
    ta_bf, tb_bf = (ta_f.astype(jnp.bfloat16), tb_f.astype(jnp.bfloat16))
    a_ch, b_ch = (
        lax.all_to_all(a_bf, "axial", split_axis=0, concat_axis=1, tiled=True),
        lax.all_to_all(b_bf, "axial", split_axis=0, concat_axis=1, tiled=True),
    )
    ta_ch, tb_ch = (
        lax.all_to_all(ta_bf, "axial", split_axis=0, concat_axis=1, tiled=True),
        lax.all_to_all(tb_bf, "axial", split_axis=0, concat_axis=1, tiled=True),
    )
    x_ch, tx_ch, a_ch, b_ch = slab_products((a_ch, b_ch, ta_ch, tb_ch))
    x_bf, tx_bf = (
        lax.all_to_all(x_ch, "axial", split_axis=1, concat_axis=0, tiled=True),
        lax.all_to_all(tx_ch, "axial", split_axis=1, concat_axis=0, tiled=True),
    )
    fhead = lambda w, xx: head(w, xx, zn)
    out, pull_head = jax.vjp(fhead, w_head, x_bf.astype(jnp.float32))
    _, t_out = jax.jvp(
        fhead, (w_head, x_bf.astype(jnp.float32)), (v_head, tx_bf.astype(jnp.float32))
    )
    total = lax.axis_size("crop") * width * width
    cot = t_out * (1.0 / total)
    g_head, x_bar = pull_head(cot)
    xb_ch = lax.all_to_all(
        x_bar.astype(jnp.bfloat16), "axial", split_axis=0, concat_axis=1, tiled=True
    )
    a_bar = jnp.einsum("cij,cjk->cik", xb_ch, b_ch, preferred_element_type=jnp.float32).astype(
        jnp.bfloat16
    )
    b_bar = jnp.einsum("cij,cik->cjk", xb_ch, a_ch, preferred_element_type=jnp.float32).astype(
        jnp.bfloat16
    )
    a_back, b_back = (
        lax.all_to_all(a_bar, "axial", split_axis=1, concat_axis=0, tiled=True),
        lax.all_to_all(b_bar, "axial", split_axis=1, concat_axis=0, tiled=True),
    )
    g_in = pull_in((a_back.astype(jnp.float32), b_back.astype(jnp.float32)))[0]
    curvature = lax.psum(jnp.concatenate([g_in, g_head], axis=1), ("crop", "axial"))
    new_pair = (pair_rows.astype(jnp.float32) + out).astype(jnp.bfloat16)
    return (new_pair[None], curvature)


def solution(mesh):
    placed = (P("crop", "axial", None, None), P("crop", None), P(), P())
    return jax.shard_map(
        shards,
        mesh=mesh,
        in_specs=placed,
        out_specs=(P("crop", "axial", None, None), P()),
        check_vma=False,
    )
```

profile of v0, /device:TPU:0, one launch (start us, length us, event | category | flops | bytes accessed | tf_op | source)
XLA Modules:
  0.0 259.6 jit_solution(5478297715194779967)
XLA Ops:
  7.2 1.0 convert_reduce_fusion
  8.4 1.1 multiply_convert_fusion
  9.5 0.3 fusion.39
  9.8 0.6 copy-done.1
  10.4 0.3 convolution_bitcast_fusion
  10.7 0.6 copy-done.2
  11.8 0.8 reshape.126
  12.6 8.3 %all-to-all-start.1 = ((bf16[16,2,1024]{2,1,0:T(2,128)(2,1)}), bf16[16,2,1024]{2,1,0:T(2,128)(2,1)S(1)}, u32[]{:S(2)}, u32[]{:S(2)}) async-start(bf16[16,2,1024]{2,1,0:T(2,128)(2,1)} %reshape.126), calls=%async_computation.1 | async-start | bytes 131072 | tf_op jit(solution)/shard_map/all_to_all | solution.py:69
  21.0 0.8 reshape.130
  21.8 6.6 %all-to-all-done.1 = bf16[16,2,1024]{2,1,0:T(2,128)(2,1)S(1)} async-done(((bf16[16,2,1024]{2,1,0:T(2,128)(2,1)}), bf16[16,2,1024]{2,1,0:T(2,128)(2,1)S(1)}, u32[]{:S(2)}, u32[]{:S(2)}) %all-to-all-start.1) | async-done | bytes 65568 | tf_op jit(solution)/shard_map/all_to_all | solution.py:69
  28.4 3.5 %all-to-all-start.3 = ((bf16[16,2,1024]{2,1,0:T(2,128)(2,1)}), bf16[16,2,1024]{2,1,0:T(2,128)(2,1)S(1)}, u32[]{:S(2)}, u32[]{:S(2)}) async-start(bf16[16,2,1024]{2,1,0:T(2,128)(2,1)} %reshape.130), calls=%async_computation.3 | async-start | bytes 131072 | tf_op jit(solution)/shard_map/all_to_all | solution.py:72
  32.1 0.8 reshape.124
  32.9 6.6 %all-to-all-done.3 = bf16[16,2,1024]{2,1,0:T(2,128)(2,1)S(1)} async-done(((bf16[16,2,1024]{2,1,0:T(2,128)(2,1)}), bf16[16,2,1024]{2,1,0:T(2,128)(2,1)S(1)}, u32[]{:S(2)}, u32[]{:S(2)}) %all-to-all-start.3) | async-done | bytes 65568 | tf_op jit(solution)/shard_map/all_to_all | solution.py:72
  39.4 3.5 %all-to-all-start = ((bf16[16,2,1024]{2,1,0:T(2,128)(2,1)}), bf16[16,2,1024]{2,1,0:T(2,128)(2,1)S(1)}, u32[]{:S(2)}, u32[]{:S(2)}) async-start(bf16[16,2,1024]{2,1,0:T(2,128)(2,1)} %reshape.124), calls=%async_computation | async-start | bytes 131072 | tf_op jit(solution)/shard_map/all_to_all | solution.py:68
  43.1 0.8 reshape.132
  43.9 6.6 %all-to-all-done = bf16[16,2,1024]{2,1,0:T(2,128)(2,1)S(1)} async-done(((bf16[16,2,1024]{2,1,0:T(2,128)(2,1)}), bf16[16,2,1024]{2,1,0:T(2,128)(2,1)S(1)}, u32[]{:S(2)}, u32[]{:S(2)}) %all-to-all-start) | async-done | bytes 65568 | tf_op jit(solution)/shard_map/all_to_all | solution.py:68
  50.5 3.5 %all-to-all-start.4 = ((bf16[16,2,1024]{2,1,0:T(2,128)(2,1)}), bf16[16,2,1024]{2,1,0:T(2,128)(2,1)S(1)}, u32[]{:S(2)}, u32[]{:S(2)}) async-start(bf16[16,2,1024]{2,1,0:T(2,128)(2,1)} %reshape.132), calls=%async_computation.4 | async-start | bytes 131072 | tf_op jit(solution)/shard_map/all_to_all | solution.py:73
  54.0 0.3 fusion.5
  55.1 6.4 %all-to-all-done.4 = bf16[16,2,1024]{2,1,0:T(2,128)(2,1)S(1)} async-done(((bf16[16,2,1024]{2,1,0:T(2,128)(2,1)}), bf16[16,2,1024]{2,1,0:T(2,128)(2,1)S(1)}, u32[]{:S(2)}, u32[]{:S(2)}) %all-to-all-start.4) | async-done | bytes 65568 | tf_op jit(solution)/shard_map/all_to_all | solution.py:73
  61.9 0.2 fusion
  62.3 0.8 reshape.134
  63.0 3.5 %all-to-all-start.5 = ((bf16[16,2,1024]{2,1,0:T(2,128)(2,1)}), bf16[16,2,1024]{2,1,0:T(2,128)(2,1)S(1)}, u32[]{:S(2)}, u32[]{:S(2)}) async-start(bf16[16,2,1024]{2,1,0:T(2,128)(2,1)} %reshape.134), calls=%async_computation.5 | async-start | bytes 131072 | tf_op jit(solution)/shard_map/all_to_all | solution.py:78
  66.8 0.8 reshape.128
  67.6 6.4 %all-to-all-done.5 = bf16[16,2,1024]{2,1,0:T(2,128)(2,1)S(1)} async-done(((bf16[16,2,1024]{2,1,0:T(2,128)(2,1)}), bf16[16,2,1024]{2,1,0:T(2,128)(2,1)S(1)}, u32[]{:S(2)}, u32[]{:S(2)}) %all-to-all-start.5) | async-done | bytes 65568 | tf_op jit(solution)/shard_map/all_to_all | solution.py:78
  74.0 3.5 %all-to-all-start.2 = ((bf16[16,2,1024]{2,1,0:T(2,128)(2,1)}), bf16[16,2,1024]{2,1,0:T(2,128)(2,1)S(1)}, u32[]{:S(2)}, u32[]{:S(2)}) async-start(bf16[16,2,1024]{2,1,0:T(2,128)(2,1)} %reshape.128), calls=%async_computation.2 | async-start | bytes 131072 | tf_op jit(solution)/shard_map/all_to_all | solution.py:77
  77.8 7.3 %all-to-all-done.2 = bf16[16,2,1024]{2,1,0:T(2,128)(2,1)S(1)} async-done(((bf16[16,2,1024]{2,1,0:T(2,128)(2,1)}), bf16[16,2,1024]{2,1,0:T(2,128)(2,1)S(1)}, u32[]{:S(2)}, u32[]{:S(2)}) %all-to-all-start.2) | async-done | bytes 65568 | tf_op jit(solution)/shard_map/all_to_all | solution.py:77
  86.0 0.3 fusion.52
  86.3 0.3 fusion.9
  86.7 0.3 multiply_reduce_fusion.1
  87.0 0.3 fusion.13
  87.3 0.3 fusion.70
  87.6 0.2 add_convert_fusion
  88.0 0.8 reshape.136
  88.7 3.5 %all-to-all-start.6 = ((bf16[16,2,1024]{2,1,0:T(2,128)(2,1)}), bf16[16,2,1024]{2,1,0:T(2,128)(2,1)S(1)}, u32[]{:S(2)}, u32[]{:S(2)}) async-start(bf16[16,2,1024]{2,1,0:T(2,128)(2,1)} %reshape.136), calls=%async_computation.6 | async-start | bytes 131072 | tf_op jit(solution)/shard_map/all_to_all | solution.py:88
  92.2 0.2 fusion.12
  92.4 7.3 %all-to-all-done.6 = bf16[16,2,1024]{2,1,0:T(2,128)(2,1)S(1)} async-done(((bf16[16,2,1024]{2,1,0:T(2,128)(2,1)}), bf16[16,2,1024]{2,1,0:T(2,128)(2,1)S(1)}, u32[]{:S(2)}, u32[]{:S(2)}) %all-to-all-start.6) | async-done | bytes 65568 | tf_op jit(solution)/shard_map/all_to_all | solution.py:88
  100.2 0.8 reshape.138
  101.0 3.5 %all-to-all-start.8 = ((bf16[16,2,1024]{2,1,0:T(2,128)(2,1)}), bf16[16,2,1024]{2,1,0:T(2,128)(2,1)S(1)}, u32[]{:S(2)}, u32[]{:S(2)}) async-start(bf16[16,2,1024]{2,1,0:T(2,128)(2,1)} %reshape.138), calls=%async_computation.8 | async-start | bytes 131072 | tf_op jit(solution)/shard_map/all_to_all | solution.py:98
  104.5 0.2 convolution_convert_fusion.1
  104.8 0.8 reshape.140
  105.6 6.4 %all-to-all-done.8 = bf16[16,2,1024]{2,1,0:T(2,128)(2,1)S(1)} async-done(((bf16[16,2,1024]{2,1,0:T(2,128)(2,1)}), bf16[16,2,1024]{2,1,0:T(2,128)(2,1)S(1)}, u32[]{:S(2)}, u32[]{:S(2)}) %all-to-all-start.8) | async-done | bytes 65568 | tf_op jit(solution)/shard_map/all_to_all | solution.py:98
  112.0 3.5 %all-to-all-start.7 = ((bf16[16,2,1024]{2,1,0:T(2,128)(2,1)}), bf16[16,2,1024]{2,1,0:T(2,128)(2,1)S(1)}, u32[]{:S(2)}, u32[]{:S(2)}) async-start(bf16[16,2,1024]{2,1,0:T(2,128)(2,1)} %reshape.140), calls=%async_computation.7 | async-start | bytes 131072 | tf_op jit(solution)/shard_map/all_to_all | solution.py:99
  115.8 7.2 %all-to-all-done.7 = bf16[16,2,1024]{2,1,0:T(2,128)(2,1)S(1)} async-done(((bf16[16,2,1024]{2,1,0:T(2,128)(2,1)}), bf16[16,2,1024]{2,1,0:T(2,128)(2,1)S(1)}, u32[]{:S(2)}, u32[]{:S(2)}) %all-to-all-start.7) | async-done | bytes 65568 | tf_op jit(solution)/shard_map/all_to_all | solution.py:99
  123.4 0.3 fusion.2
  123.8 0.8 pad_maximum_fusion
  124.6 0.7 fusion.53
  125.2 125.8 %all-reduce.8.cloned.1.call-done = f32[128,768]{1,0:T(8,128)} async-done(((f32[128,768]{1,0:T(8,128)}), f32[128,768]{1,0:T(8,128)}) %all-reduce.8.cloned.1.call-update) | async-done | bytes 393232 | tf_op jit(solution)/shard_map/psum | solution.py:102
  251.0 1.8 copy.107
  (66 shorter events, 5.3 us)
Async XLA Ops:
  7.2 1.0 copy-start
  9.5 0.9 copy-start.1
  10.7 0.7 copy-start.2
  12.6 15.9 %all-to-all-start.1 = ((bf16[16,2,1024]{2,1,0:T(2,128)(2,1)}), bf16[16,2,1024]{2,1,0:T(2,128)(2,1)S(1)}, u32[]{:S(2)}, u32[]{:S(2)}) async-start(bf16[16,2,1024]{2,1,0:T(2,128)(2,1)} %reshape.126), calls=%async_computation.1 | async-start | bytes 131072 | tf_op jit(solution)/shard_map/all_to_all | solution.py:69
  28.4 11.0 %all-to-all-start.3 = ((bf16[16,2,1024]{2,1,0:T(2,128)(2,1)}), bf16[16,2,1024]{2,1,0:T(2,128)(2,1)S(1)}, u32[]{:S(2)}, u32[]{:S(2)}) async-start(bf16[16,2,1024]{2,1,0:T(2,128)(2,1)} %reshape.130), calls=%async_computation.3 | async-start | bytes 131072 | tf_op jit(solution)/shard_map/all_to_all | solution.py:72
  39.4 11.0 %all-to-all-start = ((bf16[16,2,1024]{2,1,0:T(2,128)(2,1)}), bf16[16,2,1024]{2,1,0:T(2,128)(2,1)S(1)}, u32[]{:S(2)}, u32[]{:S(2)}) async-start(bf16[16,2,1024]{2,1,0:T(2,128)(2,1)} %reshape.124), calls=%async_computation | async-start | bytes 131072 | tf_op jit(solution)/shard_map/all_to_all | solution.py:68
  50.5 11.0 %all-to-all-start.4 = ((bf16[16,2,1024]{2,1,0:T(2,128)(2,1)}), bf16[16,2,1024]{2,1,0:T(2,128)(2,1)S(1)}, u32[]{:S(2)}, u32[]{:S(2)}) async-start(bf16[16,2,1024]{2,1,0:T(2,128)(2,1)} %reshape.132), calls=%async_computation.4 | async-start | bytes 131072 | tf_op jit(solution)/shard_map/all_to_all | solution.py:73
  63.0 11.0 %all-to-all-start.5 = ((bf16[16,2,1024]{2,1,0:T(2,128)(2,1)}), bf16[16,2,1024]{2,1,0:T(2,128)(2,1)S(1)}, u32[]{:S(2)}, u32[]{:S(2)}) async-start(bf16[16,2,1024]{2,1,0:T(2,128)(2,1)} %reshape.134), calls=%async_computation.5 | async-start | bytes 131072 | tf_op jit(solution)/shard_map/all_to_all | solution.py:78
  74.0 11.0 %all-to-all-start.2 = ((bf16[16,2,1024]{2,1,0:T(2,128)(2,1)}), bf16[16,2,1024]{2,1,0:T(2,128)(2,1)S(1)}, u32[]{:S(2)}, u32[]{:S(2)}) async-start(bf16[16,2,1024]{2,1,0:T(2,128)(2,1)} %reshape.128), calls=%async_computation.2 | async-start | bytes 131072 | tf_op jit(solution)/shard_map/all_to_all | solution.py:77
  88.7 11.0 %all-to-all-start.6 = ((bf16[16,2,1024]{2,1,0:T(2,128)(2,1)}), bf16[16,2,1024]{2,1,0:T(2,128)(2,1)S(1)}, u32[]{:S(2)}, u32[]{:S(2)}) async-start(bf16[16,2,1024]{2,1,0:T(2,128)(2,1)} %reshape.136), calls=%async_computation.6 | async-start | bytes 131072 | tf_op jit(solution)/shard_map/all_to_all | solution.py:88
  101.0 11.0 %all-to-all-start.8 = ((bf16[16,2,1024]{2,1,0:T(2,128)(2,1)}), bf16[16,2,1024]{2,1,0:T(2,128)(2,1)S(1)}, u32[]{:S(2)}, u32[]{:S(2)}) async-start(bf16[16,2,1024]{2,1,0:T(2,128)(2,1)} %reshape.138), calls=%async_computation.8 | async-start | bytes 131072 | tf_op jit(solution)/shard_map/all_to_all | solution.py:98
  112.0 11.0 %all-to-all-start.7 = ((bf16[16,2,1024]{2,1,0:T(2,128)(2,1)}), bf16[16,2,1024]{2,1,0:T(2,128)(2,1)S(1)}, u32[]{:S(2)}, u32[]{:S(2)}) async-start(bf16[16,2,1024]{2,1,0:T(2,128)(2,1)} %reshape.140), calls=%async_computation.7 | async-start | bytes 131072 | tf_op jit(solution)/shard_map/all_to_all | solution.py:99
  115.5 135.5 %all-reduce.8.cloned.1.call-start = ((), (), s32[]{:S(2)}) async-start(), calls=%async_computation.9 | async-start | bytes 786432 | tf_op jit(solution)/shard_map/psum | solution.py:102
Sparse Core Ops, SparseCore 0:
  124.7 126.2 all-reduce.7
where the time goes:
time: 260 us
  waiting for transfers between devices  187 us (72%)
  starting transfers between devices  36.4 us (14%)
  between operations  14.6 us (6%)
  local copies, waits for them, and re-layouts  13.4 us (5%)
  other arithmetic  4.99 us (2%)
  matrix products  3.75 us (1%)
    psum x1, waiting for transfers between devices, shards(): lax.psum(jnp.concatenate([g_in, g_head], axis=1), ('crop', 'axial'))  126 us
    unnamed x25, local copies, waits for them, and re-layouts  11.2 us
    all_to_all x1, starting transfers between devices, shards(): lax.all_to_all(b_bf, 'axial', split_axis=0, concat_axis=1, tiled=True)  8.31 us
    all_to_all x1, waiting for transfers between devices, shards(): lax.all_to_all(x_ch, 'axial', split_axis=1, concat_axis=0, tiled=True)  7.3 us
    all_to_all x1, waiting for transfers between devices, shards(): lax.all_to_all(x_bar.astype(jnp.bfloat16), 'axial', split_axis=0, concat_...  7.28 us
    all_to_all x1, waiting for transfers between devices, shards(): lax.all_to_all(b_bar, 'axial', split_axis=1, concat_axis=0, tiled=True)  7.16 us
    all_to_all x1, waiting for transfers between devices, shards(): lax.all_to_all(b_bf, 'axial', split_axis=0, concat_axis=1, tiled=True)  6.62 us
    all_to_all x1, waiting for transfers between devices, shards(): lax.all_to_all(ta_bf, 'axial', split_axis=0, concat_axis=1, tiled=True)  6.59 us
  transfers between devices with their start and end apart: 10, of which 10 were waited for; matrix products, arithmetic and copies ran while one was open for 3% of the time, Pallas kernels for 0%

commit v1 on v0

v1 whole, which is shorter than its diff:
```python
import functools

import jax
import jax.numpy as jnp
import numpy as np
from jax import lax
from jax.experimental import pallas as pl
from jax.experimental.pallas import tpu as pltpu
from jax.sharding import PartitionSpec as P

BF = jnp.bfloat16
F32 = jnp.float32
VMEM = pl.BlockSpec(memory_space=pltpu.VMEM)
SMEM = pl.BlockSpec(memory_space=pltpu.SMEM)


def dot(left, right, dims=((1,), (0,))):
    return lax.dot_general(left, right, (dims, ((), ())), preferred_element_type=F32)


def log2(value):
    power = value.bit_length() - 1
    assert 1 << power == value
    return power


def centre(value):
    return value - jnp.mean(value, axis=1, keepdims=True)


def scale_of(centered):
    return lax.rsqrt(jnp.mean(centered * centered, axis=1, keepdims=True) + 1e-05)


def sigmoid(value):
    return 0.5 * jnp.tanh(0.5 * value) + 0.5


def block_kernel(cfg, place, mask_s, mask_v, w_ref, signs_ref, own_ref, *rest):
    g1, g2, rows, width, chans, total = cfg
    i_refs = (own_ref,) + rest[: g1 - 1]
    j_refs = (own_ref,) + rest[g1 - 1 : g1 + g2 - 2]
    (keep_ref, send_ref, y_ref, v_s, zi_s, zj_s, a_s, ta_s, sa_s, ga_s, b_s, tb_s, sb_s, gb_s,
     zp_s, px_s, pt_s, x_s, tx_s, xb_s, g_s) = rest[g1 + g2 - 2 :]
    n_i, n_j = g1 * rows, g2 * rows
    blk = rows * width
    me, core = place[0], place[1]
    unit = 1.0 / np.sqrt(np.float32(chans))
    v_s[...] = ((2 * signs_ref[...] - 1).astype(F32) * unit).astype(BF)

    def side(refs, step, first, z_s, val_s, tan_s, sig_s, gate_s):
        for m, ref in enumerate(refs):
            value = centre(ref[...].reshape(blk, chans).astype(F32))
            zn = (value * scale_of(value)).astype(BF)
            z_s[m * blk : (m + 1) * blk, :] = zn
            proj = dot(zn, w_ref[:, first : first + 2 * chans])
            tang = dot(zn, v_s[:, first : first + 2 * chans])
            base = jnp.bitwise_xor(me, m * step) * rows
            cover = jnp.concatenate(
                [mask_v[...] * mask_s[0, base + r].astype(F32) for r in range(rows)], axis=0
            )
            sig = sigmoid(proj[:, chans:])
            held = cover * sig
            val = held * proj[:, :chans]
            gate = val - val * sig
            here = slice(m * blk, (m + 1) * blk)
            val_s[here, :] = val
            tan_s[here, :] = held * tang[:, :chans] + gate * tang[:, chans:]
            sig_s[here, :] = held.astype(sig_s.dtype)
            gate_s[here, :] = gate.astype(gate_s.dtype)

    side(i_refs, 1, 0, zi_s, a_s, ta_s, sa_s, ga_s)
    side(j_refs, g1, 2 * chans, zj_s, b_s, tb_s, sb_s, gb_s)

    spot = lax.broadcasted_iota(jnp.int32, (n_j, width), 0)
    col = lax.broadcasted_iota(jnp.int32, (n_j, width), 1)
    owner = jnp.bitwise_xor(me, (spot >> log2(rows)) * g1)
    pick = jnp.where(col == owner * rows + (spot & (rows - 1)), 1.0, 0.0).astype(BF)
    for i in range(n_i):
        zp_s[i * n_j : (i + 1) * n_j, :] = dot(pick, zi_s[i * width : (i + 1) * width, :]).astype(BF)

    def fold(value):
        return jnp.sum(value.reshape(width // 8, 8, chans), axis=0)

    def tri(i, carry):
        at = pl.ds(pl.multiple_of(i * width, width), width)
        a, ta = a_s[at, :], ta_s[at, :]
        for j in range(n_j):
            here = slice(j * width, (j + 1) * width)
            b, tb = b_s[here, :], tb_s[here, :]
            to = pl.ds(pl.multiple_of(i * (n_j * 8), 8) + j * 8, 8)
            px_s[to, :] = fold(a * b)
            pt_s[to, :] = fold(ta * b + a * tb)
        return carry

    lax.fori_loop(0, n_i, tri, 0)
    pairs = n_i * n_j
    x_s[...] = sum(px_s[pl.ds(s, pairs, stride=8), :] for s in range(8)).astype(BF).astype(F32)
    tx_s[...] = sum(pt_s[pl.ds(s, pairs, stride=8), :] for s in range(8)).astype(BF).astype(F32)

    w_gate, w_out = w_ref[:, 4 * chans : 5 * chans], w_ref[:, 5 * chans :]
    v_gate, v_out = v_s[:, 4 * chans : 5 * chans], v_s[:, 5 * chans :]
    step = min(pairs, 256)
    for at in range(0, pairs, step):
        here = slice(at, at + step)
        zp = zp_s[here, :]
        xc = centre(x_s[here, :])
        inv = scale_of(xc)
        xhat = xc * inv
        xn = xhat.astype(BF)
        tc = centre(tx_s[here, :])
        txn = (inv * (tc - xhat * jnp.mean(xhat * tc, axis=1, keepdims=True))).astype(BF)
        out = dot(xn, w_out)
        t_out = dot(txn, w_out) + dot(xn, v_out)
        sig = sigmoid(dot(zp, w_gate))
        slope = sig * (1.0 - sig) * out
        y_ref[here, :] = (sig * out).astype(BF)
        bar = (sig * t_out + slope * dot(zp, v_gate)) * (1.0 / total)
        d_out = (bar * sig).astype(BF)
        d_gate = (bar * slope).astype(BF)
        part_gate = dot(zp, d_gate, ((0,), (0,)))
        part_out = dot(xn, d_out, ((0,), (0,)))
        if at == 0:
            g_s[1, chans : 2 * chans, :] = part_gate
            g_s[1, 2 * chans :, :] = part_out
        else:
            g_s[1, chans : 2 * chans, :] += part_gate
            g_s[1, 2 * chans :, :] += part_out
        dxn = dot(d_out, w_out, ((1,), (1,)))
        dc = centre(dxn)
        xb_s[here, :] = inv * (dc - xhat * jnp.mean(xhat * dxn, axis=1, keepdims=True))

    chunk = min(width, 64)

    def back(count, others, row_of, val_s, sig_s, gate_s, z_s, spots):
        def one(m, carry):
            bars = []
            for r in range(rows):
                for kc in range(0, width, chunk):
                    acc = None
                    for o in range(others):
                        row = xb_s[pl.ds(row_of(m * rows + r, o), 1), :]
                        term = row * val_s[o * width + kc : o * width + kc + chunk, :]
                        acc = term if acc is None else acc + term
                    bars.append(acc)
            at = pl.ds(pl.multiple_of(m * blk, blk), blk)
            bar = jnp.concatenate(bars, axis=0)
            both = jnp.concatenate(
                [(bar * sig_s[at, :].astype(F32)).astype(BF), (bar * gate_s[at, :].astype(F32)).astype(BF)], axis=1
            )
            part = dot(z_s[at, :], both, ((0,), (0,)))
            for n, (half, top) in enumerate(spots):
                g_s[half, top : top + chans, :] += part[:, n * chans : (n + 1) * chans]
            return carry

        for half, top in spots:
            g_s[half, top : top + chans, :] = jnp.zeros((chans, chans), F32)
        lax.fori_loop(0, count, one, 0)

    back(g1, n_j, lambda i, j: i * n_j + j, b_s, sa_s, ga_s, zi_s, ((0, 0), (0, chans)))
    back(g2, n_i, lambda j, i: i * n_j + j, a_s, sb_s, gb_s, zj_s, ((0, 2 * chans), (1, 0)))
    keep_ref[...] = g_s[core].astype(BF)
    send_ref[...] = g_s[1 - core].astype(BF)


def last_kernel(cfg, place, pair_ref, y_ref, mine_ref, other_ref, new_ref, curv_ref, g_s):
    g1, g2, rows, width, chans, _ = cfg
    me, core = place[0], place[1]
    n_j = g2 * rows
    col = lax.broadcasted_iota(jnp.int32, (width, width), 0)
    spot = lax.broadcasted_iota(jnp.int32, (width, width), 1)
    n = (spot >> log2(rows)) & (g2 - 1)
    owner = jnp.bitwise_xor(jnp.bitwise_xor(me, n * g1), spot >> log2(n_j))
    put = jnp.where(col == owner * rows + (spot & (rows - 1)), 1.0, 0.0).astype(BF)
    for r in range(rows):
        y = jnp.concatenate([y_ref[s, r * n_j : (r + 1) * n_j, :] for s in range(g1)], axis=0)
        new_ref[r] = (pair_ref[r].astype(F32) + dot(put, y)).astype(BF)
    g_s[core] = mine_ref[...].astype(F32)
    g_s[1 - core] = other_ref[...].astype(F32)
    for b in range(6):
        top = (b % 3) * chans
        curv_ref[:, b * chans : (b + 1) * chans] = g_s[b // 3, top : top + chans, :]


def shards(pair, crop_mask, weights, probe_signs):
    own = pair[0]
    rows, width, chans = own.shape
    n_axial, n_crop = lax.axis_size("axial"), lax.axis_size("crop")
    g1 = 1 << (log2(n_axial) // 2)
    g2 = n_axial // g1
    n_i, n_j = g1 * rows, g2 * rows
    cfg = (g1, g2, rows, width, chans, n_crop * width * width)

    def swap(value, axis, bit):
        return lax.ppermute(value, axis, [(i, i ^ bit) for i in range(lax.axis_size(axis))])

    along = [swap(own, "axial", m * g1) for m in range(1, g2)]
    plane = [swap(own, "axial", m) for m in range(1, g1)]
    place = jnp.stack([lax.axis_index("axial"), lax.axis_index("crop") & 1]).astype(jnp.int32)
    mask_v = jnp.broadcast_to(crop_mask[0].astype(F32)[:, None], (width, chans))
    kept = F32 if width <= 64 else BF
    wide = lambda n, dtype=F32: pltpu.VMEM((n * width, chans), dtype)
    half = jax.ShapeDtypeStruct((3 * chans, chans), BF)
    keep, send, y = pl.pallas_call(
        functools.partial(block_kernel, cfg),
        out_shape=(half, half, jax.ShapeDtypeStruct((n_i * n_j, chans), BF)),
        in_specs=[SMEM, SMEM] + [VMEM] * (2 + g1 + g2),
        out_specs=(VMEM, VMEM, VMEM),
        scratch_shapes=[
            pltpu.VMEM(weights.shape, BF),
            wide(n_i, BF), wide(n_j, BF),
            wide(n_i), wide(n_i), wide(n_i, kept), wide(n_i, kept),
            wide(n_j), wide(n_j), wide(n_j, kept), wide(n_j, kept),
            pltpu.VMEM((n_i * n_j, chans), BF),
            pltpu.VMEM((n_i * n_j * 8, chans), F32), pltpu.VMEM((n_i * n_j * 8, chans), F32),
            pltpu.VMEM((n_i * n_j, chans), F32), pltpu.VMEM((n_i * n_j, chans), F32),
            pltpu.VMEM((n_i * n_j, chans), F32),
            pltpu.VMEM((2, 3 * chans, chans), F32),
        ],
        compiler_params=pltpu.CompilerParams(vmem_limit_bytes=(40 if width <= 64 else 58) << 20),
        name="block",
    )(place, crop_mask, mask_v, weights, probe_signs, own, *plane, *along)

    def plus(one, two):
        return (one.astype(F32) + two.astype(F32)).astype(BF)

    g = plus(keep, swap(send, "crop", 1))
    bit = 2
    while bit < n_crop:
        g = plus(g, swap(g, "crop", bit))
        bit *= 2
    y = y.reshape(g1, 1, rows * n_j, chans)
    bit = 1
    while bit < g1:
        parts = y.reshape((y.shape[0] // 2, 2) + y.shape[1:])
        out = parts[:, 1].reshape(-1, chans)
        got = swap(jnp.concatenate([g, out], axis=0), "axial", bit)
        g = plus(g, got[: 3 * chans])
        y = jnp.concatenate([parts[:, 0], got[3 * chans :].reshape(parts[:, 1].shape)], axis=1)
        bit *= 2
    while bit < n_axial:
        g = plus(g, swap(g, "axial", bit))
        bit *= 2
    other = swap(g, "crop", 1)
    new_pair, curvature = pl.pallas_call(
        functools.partial(last_kernel, cfg),
        out_shape=(jax.ShapeDtypeStruct(own.shape, BF), jax.ShapeDtypeStruct(weights.shape, F32)),
        in_specs=[SMEM] + [VMEM] * 4,
        out_specs=(VMEM, VMEM),
        scratch_shapes=[pltpu.VMEM((2, 3 * chans, chans), F32)],
        compiler_params=pltpu.CompilerParams(vmem_limit_bytes=32 << 20),
        name="last",
    )(place, own, y[0], g, other)
    return (new_pair[None], curvature)


def solution(mesh):
    placed = (P("crop", "axial", None, None), P("crop", None), P(), P())
    return jax.shard_map(
        shards,
        mesh=mesh,
        in_specs=placed,
        out_specs=(P("crop", "axial", None, None), P()),
        check_vma=False,
    )
```

time: 260 us -> 49.7 us (0.19)
  waiting for transfers between devices: 187 us -> 19.9 us
  starting transfers between devices: 36.4 us -> 17 us
  between operations: 14.6 us -> 0.75 us
  local copies, waits for them, and re-layouts: 13.4 us -> 2.86 us
  Pallas kernels: 0 us -> 8.5 us
  other arithmetic: 4.99 us -> 0.26 us
  matrix products: 3.75 us -> 0 us
    psum x1 -> x0, waiting for transfers between devices: 126 us -> none  [shards(): lax.psum(jnp.concatenate([g_in, g_head], axis=1), ('crop', 'axial'))]
    all_to_all x9 -> x0, waiting for transfers between devices: 60.7 us -> none  [the longest x1 7.3 us: shards(): lax.all_to_all(x_ch, 'axial', split_axis=1, concat_axis=0, tiled=True)]
    all_to_all x9 -> x0, starting transfers between devices: 36.3 us -> none  [the longest x1 8.31 us: shards(): lax.all_to_all(b_bf, 'axial', split_axis=0, concat_axis=1, tiled=True)]
    ppermute x0 -> x12, waiting for transfers between devices: none -> 19.9 us  [swap(): lax.ppermute(value, axis, [(i, i ^ bit) for i in range(lax.axis_size(axis...]
    ppermute x0 -> x12, starting transfers between devices: none -> 17 us  [swap(): lax.ppermute(value, axis, [(i, i ^ bit) for i in range(lax.axis_size(axis...]
    pallas_call x0 -> x2, Pallas kernels: none -> 8.5 us  [the longest x1 7.12 us: shards(): pl.pallas_call(functools.partial(block_kernel, cfg), out_shape=(half, hal...]
    unnamed x25 -> x10, local copies, waits for them, and re-layouts: 11.2 us -> 2.77 us
    dot_general x16 -> x0, matrix products: 3.75 us -> none  [the longest x5 1.08 us: head(): jnp.einsum('hrn,hc->rnc', x_norm, w_out, preferred_element_type=jnp.float32)]
  transfers between devices with their start and end apart: 10 -> 12, of which waited for: 10 -> 10; matrix products, arithmetic and copies ran while one was open for 3% -> 0% of each run, Pallas kernels for 0% -> 0%
where the time goes in v1:
time: 49.7 us; the launch traced here: 49.3 us
  waiting for transfers between devices  19.9 us (40%)
  starting transfers between devices  17 us (34%)
  Pallas kernels  8.5 us (17%)
  local copies, waits for them, and re-layouts  2.86 us (6%)
  between operations  0.75 us (2%)
    ppermute x12, waiting for transfers between devices, swap(): lax.ppermute(value, axis, [(i, i ^ bit) for i in range(lax.axis_size(axis...  19.9 us
    ppermute x12, starting transfers between devices, swap(): lax.ppermute(value, axis, [(i, i ^ bit) for i in range(lax.axis_size(axis...  17 us
    pallas_call x1, Pallas kernels, shards(): pl.pallas_call(functools.partial(block_kernel, cfg), out_shape=(half, hal...  7.12 us
    unnamed x10, local copies, waits for them, and re-layouts  2.77 us
    pallas_call x1, Pallas kernels, shards(): pl.pallas_call(functools.partial(last_kernel, cfg), out_shape=(jax.ShapeD...  1.38 us
  transfers between devices with their start and end apart: 12, of which 10 were waited for; matrix products, arithmetic and copies ran while one was open for 0% of the time, Pallas kernels for 0%

profile of v1, /device:TPU:0, one launch (start us, length us, event | category | flops | bytes accessed | tf_op | source)
XLA Modules:
  0.0 49.3 jit_solution(9640095227933170234)
XLA Ops:
  0.6 0.0 copy-start.3
  0.6 5.1 %collective-permute-start.5 = (bf16[4,64,128]{2,1,0:T(8,128)(2,1)}, bf16[4,64,128]{2,1,0:T(8,128)(2,1)S(1)}, u32[]{:S(2)}, u32[]{:S(2)}) collective-permute-start(bf16[4,64,128]{2,1,0:T(8,128)(2,1)} %bitcast.23), channel_id=1, source_target_pairs={{0,12},{1,13},{2,14},{3,15},{4,8},{5,9},{6,10},{7,11},{8,4},{9,5},... | collective-permute-start | bytes 196616 | tf_op jit(solution)/shard_map/ppermute | solution.py:195
  5.8 0.0 collective-permute-start.4
  5.8 0.6 %collective-permute-start.3 = (bf16[4,64,128]{2,1,0:T(8,128)(2,1)}, bf16[4,64,128]{2,1,0:T(8,128)(2,1)S(1)}, u32[]{:S(2)}, u32[]{:S(2)}) collective-permute-start(bf16[4,64,128]{2,1,0:T(8,128)(2,1)} %bitcast.25), channel_id=1, source_target_pairs={{0,4},{1,5},{2,6},{3,7},{4,0},{5,1},{6,2},{7,3},{8,12},{9,13},{10,... | collective-permute-start | bytes 196616 | tf_op jit(solution)/shard_map/ppermute | solution.py:195
  6.4 2.6 %collective-permute-start.2 = (bf16[4,64,128]{2,1,0:T(8,128)(2,1)}, bf16[4,64,128]{2,1,0:T(8,128)(2,1)S(1)}, u32[]{:S(2)}, u32[]{:S(2)}) collective-permute-start(bf16[4,64,128]{2,1,0:T(8,128)(2,1)} %bitcast.26), channel_id=1, source_target_pairs={{0,3},{1,2},{2,1},{3,0},{4,7},{5,6},{6,5},{7,4},{8,11},{9,10},{10,... | collective-permute-start | bytes 196616 | tf_op jit(solution)/shard_map/ppermute | solution.py:195
  9.0 0.5 %collective-permute-start.1 = (bf16[4,64,128]{2,1,0:T(8,128)(2,1)}, bf16[4,64,128]{2,1,0:T(8,128)(2,1)S(1)}, u32[]{:S(2)}, u32[]{:S(2)}) collective-permute-start(bf16[4,64,128]{2,1,0:T(8,128)(2,1)} %bitcast.27), channel_id=1, source_target_pairs={{0,2},{1,3},{2,0},{3,1},{4,6},{5,7},{6,4},{7,5},{8,10},{9,11},{10,... | collective-permute-start | bytes 196616 | tf_op jit(solution)/shard_map/ppermute | solution.py:195
  9.5 0.0 copy-done.3
  9.5 0.0 collective-permute-done.5.rest_5_
  9.5 0.9 %collective-permute-start = (bf16[4,64,128]{2,1,0:T(8,128)(2,1)}, bf16[4,64,128]{2,1,0:T(8,128)(2,1)S(1)}, u32[]{:S(2)}, u32[]{:S(2)}) collective-permute-start(bf16[4,64,128]{2,1,0:T(8,128)(2,1)} %bitcast.28), channel_id=1, source_target_pairs={{0,1},{1,0},{2,3},{3,2},{4,5},{5,4},{6,7},{7,6},{8,9},{9,8},{10,11... | collective-permute-start | bytes 196616 | tf_op jit(solution)/shard_map/ppermute | solution.py:195
  10.4 0.1 pad_add_fusion.place
  10.5 1.1 %collective-permute-done.4.rest_4_ = bf16[4,64,128]{2,1,0:T(8,128)(2,1)S(1)} collective-permute-done((bf16[4,64,128]{2,1,0:T(8,128)(2,1)}, bf16[4,64,128]{2,1,0:T(8,128)(2,1)S(1)}, u32[]{:S(2)}, u32[]{:S(2)}) %collective-permute-start.4) | collective-permute-done | bytes 65568 | tf_op jit(solution)/shard_map/ppermute | solution.py:195
  11.6 0.0 collective-permute-done.3.rest_3_
  11.6 0.3 collective-permute-done.2.rest_2_
  11.9 1.6 %collective-permute-done.1.rest_1_ = bf16[4,64,128]{2,1,0:T(8,128)(2,1)S(1)} collective-permute-done((bf16[4,64,128]{2,1,0:T(8,128)(2,1)}, bf16[4,64,128]{2,1,0:T(8,128)(2,1)S(1)}, u32[]{:S(2)}, u32[]{:S(2)}) %collective-permute-start.1) | collective-permute-done | bytes 65568 | tf_op jit(solution)/shard_map/ppermute | solution.py:195
  13.5 0.6 %collective-permute-done.rest_0_ = bf16[4,64,128]{2,1,0:T(8,128)(2,1)S(1)} collective-permute-done((bf16[4,64,128]{2,1,0:T(8,128)(2,1)}, bf16[4,64,128]{2,1,0:T(8,128)(2,1)S(1)}, u32[]{:S(2)}, u32[]{:S(2)}) %collective-permute-start) | collective-permute-done | bytes 65568 | tf_op jit(solution)/shard_map/ppermute | solution.py:195
  14.0 0.1 broadcast_in_dim.4.mask_v
  14.1 0.0 copy-start
  14.1 1.0 %copy-done = s32[128,768]{1,0:T(8,128)S(1)} copy-done((s32[128,768]{1,0:T(8,128)S(1)}, s32[128,768]{1,0:T(8,128)}, u32[]{:S(2)}) %copy-start) | copy-done | bytes 393240
  15.1 0.0 copy-start.1
  15.1 0.8 %copy-done.1 = bf16[1,4,64,128]{3,2,1,0:T(8,128)(2,1)S(1)} copy-done((bf16[1,4,64,128]{3,2,1,0:T(8,128)(2,1)S(1)}, bf16[1,4,64,128]{3,2,1,0:T(8,128)(2,1)}, u32[]{:S(2)}) %copy-start.1) | copy-done | bytes 65560
  16.0 0.0 copy-start.2
  16.0 0.9 %copy-done.2 = bf16[128,768]{1,0:T(8,128)(2,1)S(1)} copy-done((bf16[128,768]{1,0:T(8,128)(2,1)S(1)}, bf16[128,768]{1,0:T(8,128)(2,1)}, u32[]{:S(2)}) %copy-start.2) | copy-done | bytes 196632
  16.9 7.1 %block.1 = (bf16[384,128]{1,0:T(8,128)(2,1)S(1)}, bf16[384,128]{1,0:T(8,128)(2,1)S(1)}, bf16[256,128]{1,0:T(8,128)(2,1)S(1)}) custom-call(s32[2]{0:T(128)S(1)} %pad_add_fusion.place, s32[1,64]{1,0:T(1,128)S(1)} %copy-done.3, f32[64,128]{1,0:T(8,128)S(1)} %broadcast_in_dim.4.mask_v, bf16[128,768]{1,0:T(8,128)(2,1)S(1)} %copy-done.2, s32[128,768]{1,0:T(8,128)S(1)} %copy-done, ...), custom_call_target="tpu_custom_call" | custom-call | tf_op jit(solution)/shard_map/block/pallas_call | solution.py:204
  24.0 0.1 collective-permute-start.6
  24.1 1.3 %collective-permute-done.6 = bf16[384,128]{1,0:T(8,128)(2,1)S(1)} collective-permute-done((bf16[384,128]{1,0:T(8,128)(2,1)S(1)}, bf16[384,128]{1,0:T(8,128)(2,1)S(1)}, u32[]{:S(2)}, u32[]{:S(2)}) %collective-permute-start.6) | collective-permute-done | bytes 98336 | tf_op jit(solution)/shard_map/ppermute | solution.py:195
  25.4 0.9 %collective-permute-start.7 = (bf16[512,128]{1,0:T(8,128)(2,1)S(1)}, bf16[512,128]{1,0:T(8,128)(2,1)S(1)}, u32[]{:S(2)}, u32[]{:S(2)}) collective-permute-start(bf16[512,128]{1,0:T(8,128)(2,1)S(1)} %pad_maximum_fusion), channel_id=1, source_target_pairs={{0,1},{1,0},{2,3},{3,2},{4,5},{5,4},{6,7},{7,6},{8,9},{9,8},{10,11... | collective-permute-start | bytes 393224 | tf_op jit(solution)/shard_map/ppermute | solution.py:195
  26.3 4.7 %collective-permute-done.7 = bf16[512,128]{1,0:T(8,128)(2,1)S(1)} collective-permute-done((bf16[512,128]{1,0:T(8,128)(2,1)S(1)}, bf16[512,128]{1,0:T(8,128)(2,1)S(1)}, u32[]{:S(2)}, u32[]{:S(2)}) %collective-permute-start.7) | collective-permute-done | bytes 131104 | tf_op jit(solution)/shard_map/ppermute | solution.py:195
  31.1 1.6 %collective-permute-start.8 = (bf16[512,128]{1,0:T(8,128)(2,1)S(1)}, bf16[512,128]{1,0:T(8,128)(2,1)S(1)}, u32[]{:S(2)}, u32[]{:S(2)}) collective-permute-start(bf16[512,128]{1,0:T(8,128)(2,1)S(1)} %pad_maximum_fusion.1), channel_id=1, source_target_pairs={{0,2},{1,3},{2,0},{3,1},{4,6},{5,7},{6,4},{7,5},{8,10},{9,11},{10,... | collective-permute-start | bytes 393224 | tf_op jit(solution)/shard_map/ppermute | solution.py:195
  32.7 3.4 %collective-permute-done.8 = bf16[512,128]{1,0:T(8,128)(2,1)S(1)} collective-permute-done((bf16[512,128]{1,0:T(8,128)(2,1)S(1)}, bf16[512,128]{1,0:T(8,128)(2,1)S(1)}, u32[]{:S(2)}, u32[]{:S(2)}) %collective-permute-start.8) | collective-permute-done | bytes 131104 | tf_op jit(solution)/shard_map/ppermute | solution.py:195
  36.2 0.0 copy-start.4
  36.2 1.7 %collective-permute-start.9 = (bf16[384,128]{1,0:T(8,128)(2,1)S(1)}, bf16[384,128]{1,0:T(8,128)(2,1)S(1)}, u32[]{:S(2)}, u32[]{:S(2)}) collective-permute-start(bf16[384,128]{1,0:T(8,128)(2,1)S(1)} %add_convert_fusion.2), channel_id=1, source_target_pairs={{0,4},{1,5},{2,6},{3,7},{4,0},{5,1},{6,2},{7,3},{8,12},{9,13},{10,... | collective-permute-start | bytes 294920 | tf_op jit(solution)/shard_map/ppermute | solution.py:195
  37.9 3.0 %collective-permute-done.9 = bf16[384,128]{1,0:T(8,128)(2,1)S(1)} collective-permute-done((bf16[384,128]{1,0:T(8,128)(2,1)S(1)}, bf16[384,128]{1,0:T(8,128)(2,1)S(1)}, u32[]{:S(2)}, u32[]{:S(2)}) %collective-permute-start.9) | collective-permute-done | bytes 98336 | tf_op jit(solution)/shard_map/ppermute | solution.py:195
  40.9 3.0 %collective-permute-start.10 = (bf16[384,128]{1,0:T(8,128)(2,1)S(1)}, bf16[384,128]{1,0:T(8,128)(2,1)S(1)}, u32[]{:S(2)}, u32[]{:S(2)}) collective-permute-start(bf16[384,128]{1,0:T(8,128)(2,1)S(1)} %add_convert_fusion.1), channel_id=1, source_target_pairs={{0,8},{1,9},{2,10},{3,11},{4,12},{5,13},{6,14},{7,15},{8,0},{9,1},... | collective-permute-start | bytes 294920 | tf_op jit(solution)/shard_map/ppermute | solution.py:195
  43.9 0.0 copy-done.4
  43.9 0.0 slice-start
  43.9 2.6 %collective-permute-done.10 = bf16[384,128]{1,0:T(8,128)(2,1)S(1)} collective-permute-done((bf16[384,128]{1,0:T(8,128)(2,1)S(1)}, bf16[384,128]{1,0:T(8,128)(2,1)S(1)}, u32[]{:S(2)}, u32[]{:S(2)}) %collective-permute-start.10) | collective-permute-done | bytes 98336 | tf_op jit(solution)/shard_map/ppermute | solution.py:195
  46.6 0.1 collective-permute-start.11
  46.6 0.0 slice-done
  46.7 1.3 %collective-permute-done.11.other_ref = bf16[384,128]{1,0:T(8,128)(2,1)S(1)} collective-permute-done((bf16[384,128]{1,0:T(8,128)(2,1)S(1)}, bf16[384,128]{1,0:T(8,128)(2,1)S(1)}, u32[]{:S(2)}, u32[]{:S(2)}) %collective-permute-start.11) | collective-permute-done | bytes 98336 | tf_op jit(solution)/shard_map/ppermute | solution.py:195
  47.9 1.4 %last.1 = (bf16[4,64,128]{2,1,0:T(8,128)(2,1)}, f32[128,768]{1,0:T(8,128)}) custom-call(s32[2]{0:T(128)S(1)} %pad_add_fusion.place, bf16[4,64,128]{2,1,0:T(8,128)(2,1)S(1)} %bitcast.30, bf16[4,64,128]{2,1,0:T(8,128)(2,1)S(1)} %maximum_bitcast_fusion.1.y_ref, bf16[384,128]{1,0:T(8,128)(2,1)S(1)} %add_convert_fusion.mine_ref, ...), custom_call_target="tpu_custom_call" | custom-call | tf_op jit(solution)/shard_map/last/pallas_call | solution.py:245
  (13 shorter events, 0.2 us)
Async XLA Ops:
  0.6 8.9 %copy-start.3 = (s32[1,64]{1,0:T(1,128)S(1)}, s32[1,64]{1,0:T(1,128)}, u32[]{:S(2)}) copy-start(s32[1,64]{1,0:T(1,128)} %mask_s.1) | copy-start | bytes 772
  0.6 8.9 %collective-permute-start.5 = (bf16[4,64,128]{2,1,0:T(8,128)(2,1)}, bf16[4,64,128]{2,1,0:T(8,128)(2,1)S(1)}, u32[]{:S(2)}, u32[]{:S(2)}) collective-permute-start(bf16[4,64,128]{2,1,0:T(8,128)(2,1)} %bitcast.23), channel_id=1, source_target_pairs={{0,12},{1,13},{2,14},{3,15},{4,8},{5,9},{6,10},{7,11},{8,4},{9,5},... | collective-permute-start | bytes 196616 | tf_op jit(solution)/shard_map/ppermute | solution.py:195
  5.8 5.8 %collective-permute-start.4 = (bf16[4,64,128]{2,1,0:T(8,128)(2,1)}, bf16[4,64,128]{2,1,0:T(8,128)(2,1)S(1)}, u32[]{:S(2)}, u32[]{:S(2)}) collective-permute-start(bf16[4,64,128]{2,1,0:T(8,128)(2,1)} %bitcast.24), channel_id=1, source_target_pairs={{0,8},{1,9},{2,10},{3,11},{4,12},{5,13},{6,14},{7,15},{8,0},{9,1},... | collective-permute-start | bytes 196616 | tf_op jit(solution)/shard_map/ppermute | solution.py:195
  5.8 5.8 %collective-permute-start.3 = (bf16[4,64,128]{2,1,0:T(8,128)(2,1)}, bf16[4,64,128]{2,1,0:T(8,128)(2,1)S(1)}, u32[]{:S(2)}, u32[]{:S(2)}) collective-permute-start(bf16[4,64,128]{2,1,0:T(8,128)(2,1)} %bitcast.25), channel_id=1, source_target_pairs={{0,4},{1,5},{2,6},{3,7},{4,0},{5,1},{6,2},{7,3},{8,12},{9,13},{10,... | collective-permute-start | bytes 196616 | tf_op jit(solution)/shard_map/ppermute | solution.py:195
  6.4 5.5 %collective-permute-start.2 = (bf16[4,64,128]{2,1,0:T(8,128)(2,1)}, bf16[4,64,128]{2,1,0:T(8,128)(2,1)S(1)}, u32[]{:S(2)}, u32[]{:S(2)}) collective-permute-start(bf16[4,64,128]{2,1,0:T(8,128)(2,1)} %bitcast.26), channel_id=1, source_target_pairs={{0,3},{1,2},{2,1},{3,0},{4,7},{5,6},{6,5},{7,4},{8,11},{9,10},{10,... | collective-permute-start | bytes 196616 | tf_op jit(solution)/shard_map/ppermute | solution.py:195
  9.0 4.5 %collective-permute-start.1 = (bf16[4,64,128]{2,1,0:T(8,128)(2,1)}, bf16[4,64,128]{2,1,0:T(8,128)(2,1)S(1)}, u32[]{:S(2)}, u32[]{:S(2)}) collective-permute-start(bf16[4,64,128]{2,1,0:T(8,128)(2,1)} %bitcast.27), channel_id=1, source_target_pairs={{0,2},{1,3},{2,0},{3,1},{4,6},{5,7},{6,4},{7,5},{8,10},{9,11},{10,... | collective-permute-start | bytes 196616 | tf_op jit(solution)/shard_map/ppermute | solution.py:195
  9.5 4.5 %collective-permute-start = (bf16[4,64,128]{2,1,0:T(8,128)(2,1)}, bf16[4,64,128]{2,1,0:T(8,128)(2,1)S(1)}, u32[]{:S(2)}, u32[]{:S(2)}) collective-permute-start(bf16[4,64,128]{2,1,0:T(8,128)(2,1)} %bitcast.28), channel_id=1, source_target_pairs={{0,1},{1,0},{2,3},{3,2},{4,5},{5,4},{6,7},{7,6},{8,9},{9,8},{10,11... | collective-permute-start | bytes 196616 | tf_op jit(solution)/shard_map/ppermute | solution.py:195
  14.1 1.0 %copy-start = (s32[128,768]{1,0:T(8,128)S(1)}, s32[128,768]{1,0:T(8,128)}, u32[]{:S(2)}) copy-start(s32[128,768]{1,0:T(8,128)} %signs_ref.1) | copy-start | bytes 1179652
  15.1 0.8 %copy-start.1 = (bf16[1,4,64,128]{3,2,1,0:T(8,128)(2,1)S(1)}, bf16[1,4,64,128]{3,2,1,0:T(8,128)(2,1)}, u32[]{:S(2)}) copy-start(bf16[1,4,64,128]{3,2,1,0:T(8,128)(2,1)} %param.4) | copy-start | bytes 196612
  16.0 0.9 %copy-start.2 = (bf16[128,768]{1,0:T(8,128)(2,1)S(1)}, bf16[128,768]{1,0:T(8,128)(2,1)}, u32[]{:S(2)}) copy-start(bf16[128,768]{1,0:T(8,128)(2,1)} %w_ref.1) | copy-start | bytes 589828
  24.0 1.4 %collective-permute-start.6 = (bf16[384,128]{1,0:T(8,128)(2,1)S(1)}, bf16[384,128]{1,0:T(8,128)(2,1)S(1)}, u32[]{:S(2)}, u32[]{:S(2)}) collective-permute-start(bf16[384,128]{1,0:T(8,128)(2,1)S(1)} %get-tuple-element.9), channel_id=1, source_target_pairs={{0,16},{16,0},{1,17},{17,1},{2,18},{18,2},{3,19},{19,3},{4,20},{20... | collective-permute-start | bytes 294920 | tf_op jit(solution)/shard_map/ppermute | solution.py:195
  25.4 5.6 %collective-permute-start.7 = (bf16[512,128]{1,0:T(8,128)(2,1)S(1)}, bf16[512,128]{1,0:T(8,128)(2,1)S(1)}, u32[]{:S(2)}, u32[]{:S(2)}) collective-permute-start(bf16[512,128]{1,0:T(8,128)(2,1)S(1)} %pad_maximum_fusion), channel_id=1, source_target_pairs={{0,1},{1,0},{2,3},{3,2},{4,5},{5,4},{6,7},{7,6},{8,9},{9,8},{10,11... | collective-permute-start | bytes 393224 | tf_op jit(solution)/shard_map/ppermute | solution.py:195
  31.1 5.0 %collective-permute-start.8 = (bf16[512,128]{1,0:T(8,128)(2,1)S(1)}, bf16[512,128]{1,0:T(8,128)(2,1)S(1)}, u32[]{:S(2)}, u32[]{:S(2)}) collective-permute-start(bf16[512,128]{1,0:T(8,128)(2,1)S(1)} %pad_maximum_fusion.1), channel_id=1, source_target_pairs={{0,2},{1,3},{2,0},{3,1},{4,6},{5,7},{6,4},{7,5},{8,10},{9,11},{10,... | collective-permute-start | bytes 393224 | tf_op jit(solution)/shard_map/ppermute | solution.py:195
  36.2 7.7 %copy-start.4 = (bf16[512,128]{1,0:T(8,128)(2,1)}, bf16[512,128]{1,0:T(8,128)(2,1)S(1)}, u32[]{:S(2)}) copy-start(bf16[512,128]{1,0:T(8,128)(2,1)S(1)} %collective-permute-done.8) | copy-start | bytes 393220
  36.2 4.7 %collective-permute-start.9 = (bf16[384,128]{1,0:T(8,128)(2,1)S(1)}, bf16[384,128]{1,0:T(8,128)(2,1)S(1)}, u32[]{:S(2)}, u32[]{:S(2)}) collective-permute-start(bf16[384,128]{1,0:T(8,128)(2,1)S(1)} %add_convert_fusion.2), channel_id=1, source_target_pairs={{0,4},{1,5},{2,6},{3,7},{4,0},{5,1},{6,2},{7,3},{8,12},{9,13},{10,... | collective-permute-start | bytes 294920 | tf_op jit(solution)/shard_map/ppermute | solution.py:195
  40.9 5.6 %collective-permute-start.10 = (bf16[384,128]{1,0:T(8,128)(2,1)S(1)}, bf16[384,128]{1,0:T(8,128)(2,1)S(1)}, u32[]{:S(2)}, u32[]{:S(2)}) collective-permute-start(bf16[384,128]{1,0:T(8,128)(2,1)S(1)} %add_convert_fusion.1), channel_id=1, source_target_pairs={{0,8},{1,9},{2,10},{3,11},{4,12},{5,13},{6,14},{7,15},{8,0},{9,1},... | collective-permute-start | bytes 294920 | tf_op jit(solution)/shard_map/ppermute | solution.py:195
  43.9 2.8 %slice-start = ((bf16[512,128]{1,0:T(8,128)(2,1)}), bf16[128,128]{1,0:T(8,128)(2,1)S(1)}, s32[]{:S(2)}) async-start(bf16[512,128]{1,0:T(8,128)(2,1)} %copy-done.4), calls=%async_computation | async-start | bytes 65536 | tf_op jit(solution)/shard_map/slice | solution.py:239
  46.6 1.4 %collective-permute-start.11 = (bf16[384,128]{1,0:T(8,128)(2,1)S(1)}, bf16[384,128]{1,0:T(8,128)(2,1)S(1)}, u32[]{:S(2)}, u32[]{:S(2)}) collective-permute-start(bf16[384,128]{1,0:T(8,128)(2,1)S(1)} %add_convert_fusion.mine_ref), channel_id=1, source_target_pairs={{0,16},{16,0},{1,17},{17,1},{2,18},{18,2},{3,19},{19,3},{4,20},{20... | collective-permute-start | bytes 294920 | tf_op jit(solution)/shard_map/ppermute | solution.py:195

commit v2 on v1

v2 whole, which is shorter than its diff:
```python
import functools

import jax
import jax.numpy as jnp
import numpy as np
from jax import lax
from jax.experimental import pallas as pl
from jax.experimental.pallas import tpu as pltpu
from jax.sharding import PartitionSpec as P

BF = jnp.bfloat16
F32 = jnp.float32
VMEM = pl.BlockSpec(memory_space=pltpu.VMEM)
SMEM = pl.BlockSpec(memory_space=pltpu.SMEM)


def dot(left, right, dims=((1,), (0,))):
    return lax.dot_general(left, right, (dims, ((), ())), preferred_element_type=F32)


def log2(value):
    power = value.bit_length() - 1
    assert 1 << power == value
    return power


def centre(value):
    return value - jnp.mean(value, axis=1, keepdims=True)


def scale_of(centered):
    return lax.rsqrt(jnp.mean(centered * centered, axis=1, keepdims=True) + 1e-05)


def sigmoid(value):
    return 0.5 * jnp.tanh(0.5 * value) + 0.5


def flip(value, bits):
    return sum(((value >> b) & 1) << (bits - 1 - b) for b in range(bits))


def turned(core, value, bits):
    return jnp.where(core == 0, value, flip(value, bits))


def picker(cfg, place):
    g1, g2, rows, width, _, _ = cfg
    shape = (g2 * rows, width)
    spot = lax.broadcasted_iota(jnp.int32, shape, 0)
    col = lax.broadcasted_iota(jnp.int32, shape, 1)
    owner = jnp.bitwise_xor(place[0], turned(place[1], spot >> log2(rows), log2(g2)) * g1)
    return jnp.where(col == owner * rows + (spot & (rows - 1)), 1.0, 0.0).astype(BF)


def fill_side(cfg, place, mask_s, mask_v, w_ref, v_ref, blocks, step, first, outs):
    g1, g2, rows, width, chans, _ = cfg
    z_s, val_s, tan_s, sig_s, gate_s, *zp_s = outs
    if zp_s:
        pick = picker(cfg, place)
    blk = rows * width
    bits = log2(g1 if step == 1 else g2)
    for m, ref in blocks:
        here = slice(m * blk, (m + 1) * blk)
        value = centre(ref[...].reshape(blk, chans).astype(F32))
        zn = (value * scale_of(value)).astype(BF)
        z_s[:, here] = zn.T
        for r in range(rows if zp_s else 0):
            i = m * rows + r
            pairs = dot(pick, zn[r * width : (r + 1) * width]).astype(BF)
            zp_s[0][i * g2 * rows : (i + 1) * g2 * rows, :] = pairs
        proj = dot(zn, w_ref[:, first : first + 2 * chans])
        tang = dot(zn, v_ref[:, first : first + 2 * chans])
        base = jnp.bitwise_xor(place[0], turned(place[1], m, bits) * step) * rows
        cover = jnp.concatenate(
            [mask_v[...] * mask_s[0, base + r].astype(F32) for r in range(rows)], axis=0
        )
        sig = sigmoid(proj[:, chans:])
        held = cover * sig
        val = held * proj[:, :chans]
        gate = val - val * sig
        val_s[here, :] = val.astype(val_s.dtype)
        tan_s[here, :] = (held * tang[:, :chans] + gate * tang[:, chans:]).astype(tan_s.dtype)
        sig_s[here, :] = held.astype(sig_s.dtype)
        gate_s[here, :] = gate.astype(gate_s.dtype)


def own_kernel(cfg, place, mask_s, mask_v, w_ref, v_ref, own_ref, *outs):
    g1, chans = cfg[0], cfg[4]
    fill_side(cfg, place, mask_s, mask_v, w_ref, v_ref, [(0, own_ref)], 1, 0, outs[:6])
    fill_side(cfg, place, mask_s, mask_v, w_ref, v_ref, [(0, own_ref)], g1, 2 * chans, outs[6:])


def rows_kernel(cfg, place, mask_s, mask_v, w_ref, v_ref, *rest):
    g1, g2, chans = cfg[0], cfg[1], cfg[4]
    count = g1 + g2 - 3
    refs, outs = rest[:count], rest[count + 11 :]
    fill_side(cfg, place, mask_s, mask_v, w_ref, v_ref,
              [(m + 1, refs[g1 - 2 + m]) for m in range(g2 - 1)], g1, 2 * chans, outs[6:])
    fill_side(cfg, place, mask_s, mask_v, w_ref, v_ref,
              [(m + 2, refs[m]) for m in range(g1 - 2)], 1, 0, outs[:6])


def block_kernel(cfg, place, mask_s, mask_v, w_ref, v_s, zj_s, b_s, tb_s, sb_s, gb_s, late_ref, *rest):
    g1, g2, rows, width, chans, total = cfg
    (keep_ref, send_ref, y_ref, zi_s, a_s, ta_s, sa_s, ga_s, zp_s,
     px_s, pt_s, x_s, tx_s, xb_s, d_s, g_s) = rest[6:]
    n_i, n_j = g1 * rows, g2 * rows
    blk = rows * width
    core = place[1]
    fill_side(cfg, place, mask_s, mask_v, w_ref, v_s, [(1, late_ref)], 1, 0,
              (zi_s, a_s, ta_s, sa_s, ga_s, zp_s))

    def fold(value):
        return jnp.sum(value.reshape(width // 8, 8, chans), axis=0)

    def tri(i, carry):
        at = pl.ds(pl.multiple_of(i * width, width), width)
        a, ta = a_s[at, :].astype(F32), ta_s[at, :].astype(F32)
        for j in range(n_j):
            here = slice(j * width, (j + 1) * width)
            b, tb = b_s[here, :].astype(F32), tb_s[here, :].astype(F32)
            to = pl.ds(pl.multiple_of(i * (n_j * 8), 8) + j * 8, 8)
            px_s[to, :] = fold(a * b)
            pt_s[to, :] = fold(ta * b + a * tb)
        return carry

    lax.fori_loop(0, n_i, tri, 0)
    pairs = n_i * n_j
    x_s[...] = sum(px_s[pl.ds(s, pairs, stride=8), :] for s in range(8)).astype(BF).astype(F32)
    tx_s[...] = sum(pt_s[pl.ds(s, pairs, stride=8), :] for s in range(8)).astype(BF).astype(F32)

    w_gate, w_out = w_ref[:, 4 * chans : 5 * chans], w_ref[:, 5 * chans :]
    v_gate, v_out = v_s[:, 4 * chans : 5 * chans], v_s[:, 5 * chans :]
    step = min(pairs, 256)
    for at in range(0, pairs, step):
        here = slice(at, at + step)
        zp = zp_s[here, :]
        xc = centre(x_s[here, :])
        inv = scale_of(xc)
        xhat = xc * inv
        xn = xhat.astype(BF)
        tc = centre(tx_s[here, :])
        txn = (inv * (tc - xhat * jnp.mean(xhat * tc, axis=1, keepdims=True))).astype(BF)
        out = dot(xn, w_out)
        t_out = dot(txn, w_out) + dot(xn, v_out)
        sig = sigmoid(dot(zp, w_gate))
        slope = sig * (1.0 - sig) * out
        y_ref[here, :] = (sig * out).astype(BF)
        bar = (sig * t_out + slope * dot(zp, v_gate)) * (1.0 / total)
        d_out = (bar * sig).astype(BF)
        d_gate = (bar * slope).astype(BF)
        part_gate = dot(zp, d_gate, ((0,), (0,)))
        part_out = dot(xn, d_out, ((0,), (0,)))
        if at == 0:
            g_s[1, chans : 2 * chans, :] = part_gate
            g_s[1, 2 * chans :, :] = part_out
        else:
            g_s[1, chans : 2 * chans, :] += part_gate
            g_s[1, 2 * chans :, :] += part_out
        dxn = dot(d_out, w_out, ((1,), (1,)))
        dc = centre(dxn)
        xb_s[here, :] = inv * (dc - xhat * jnp.mean(xhat * dxn, axis=1, keepdims=True))

    chunk = min(width, 64)

    def back(count, others, row_of, val_s, sig_s, gate_s, z_s, spots):
        def one(m, carry):
            bars = []
            for r in range(rows):
                for kc in range(0, width, chunk):
                    acc = None
                    for o in range(others):
                        row = xb_s[pl.ds(row_of(m * rows + r, o), 1), :]
                        term = row * val_s[o * width + kc : o * width + kc + chunk, :].astype(F32)
                        acc = term if acc is None else acc + term
                    bars.append(acc)
            at = pl.ds(pl.multiple_of(m * blk, blk), blk)
            bar = jnp.concatenate(bars, axis=0)
            d_s[at, :chans] = (bar * sig_s[at, :].astype(F32)).astype(BF)
            d_s[at, chans:] = (bar * gate_s[at, :].astype(F32)).astype(BF)
            return carry

        lax.fori_loop(0, count, one, 0)
        part = dot(z_s[...], d_s[: count * blk, :])
        for n, (half, top) in enumerate(spots):
            g_s[half, top : top + chans, :] = part[:, n * chans : (n + 1) * chans]

    back(g1, n_j, lambda i, j: i * n_j + j, b_s, sa_s, ga_s, zi_s, ((0, 0), (0, chans)))
    back(g2, n_i, lambda j, i: i * n_j + j, a_s, sb_s, gb_s, zj_s, ((0, 2 * chans), (1, 0)))
    keep_ref[...] = g_s[core].astype(BF)
    send_ref[...] = g_s[1 - core].astype(BF)


def pair_kernel(cfg, place, pair_ref, y_ref, new_ref):
    g1, g2, rows, width, _, _ = cfg
    me, core = place[0], place[1]
    n_j = g2 * rows
    col = lax.broadcasted_iota(jnp.int32, (width, width), 0)
    spot = lax.broadcasted_iota(jnp.int32, (width, width), 1)
    n = turned(core, (spot >> log2(rows)) & (g2 - 1), log2(g2))
    s = turned(core, spot >> log2(n_j), log2(g1))
    owner = jnp.bitwise_xor(jnp.bitwise_xor(me, n * g1), s)
    put = jnp.where(col == owner * rows + (spot & (rows - 1)), 1.0, 0.0).astype(BF)
    for r in range(rows):
        y = jnp.concatenate([y_ref[s, r * n_j : (r + 1) * n_j, :] for s in range(g1)], axis=0)
        new_ref[r] = (pair_ref[r].astype(F32) + dot(put, y)).astype(BF)


def last_kernel(cfg, place, mine_ref, other_ref, curv_ref, g_s):
    chans = cfg[4]
    core = place[1]
    g_s[core] = mine_ref[...].astype(F32)
    g_s[1 - core] = other_ref[...].astype(F32)
    for b in range(6):
        top = (b % 3) * chans
        curv_ref[:, b * chans : (b + 1) * chans] = g_s[b // 3, top : top + chans, :]


def shards(pair, crop_mask, weights, probe_signs):
    own = pair[0]
    rows, width, chans = own.shape
    n_axial, n_crop = lax.axis_size("axial"), lax.axis_size("crop")
    g1 = 1 << (log2(n_axial) // 2)
    g2 = n_axial // g1
    n_i, n_j = g1 * rows, g2 * rows
    cfg = (g1, g2, rows, width, chans, n_crop * width * width)

    def crop_swap(value, bit):
        return lax.ppermute(value, "crop", [(i, i ^ bit) for i in range(n_crop)])

    def swap(value, m, step, mixed=True):
        bits = log2(g1 if step == 1 else g2)
        pairs = []
        for q in range(n_crop):
            there = (flip(m, bits) if mixed and q & 1 else m) * step
            pairs += [(q * n_axial + i, q * n_axial + (i ^ there)) for i in range(n_axial)]
        return lax.ppermute(value, ("crop", "axial"), pairs)

    along = [swap(own, m, g1) for m in range(1, g2)]
    plane = [swap(own, m, 1) for m in range(2, g1)]
    place = jnp.stack([lax.axis_index("axial"), lax.axis_index("crop") & 1]).astype(jnp.int32)
    mask_v = jnp.broadcast_to(crop_mask[0].astype(F32)[:, None], (width, chans))
    kept = F32 if width <= 64 else BF
    shape = jax.ShapeDtypeStruct
    pairs = (n_i * n_j, chans)
    side = lambda n: [shape((chans, n * width), BF)] + [shape((n * width, chans), t) for t in (kept,) * 4]
    side_a, side_b = side(n_i) + [shape(pairs, BF)], side(n_j)
    half = shape((3 * chans, chans), BF)
    params = lambda: pltpu.CompilerParams(vmem_limit_bytes=(40 if width <= 64 else 58) << 20)
    cost = lambda us: pl.CostEstimate(flops=int(us * 1e9), bytes_accessed=0, transcendentals=0)

    unit = 1.0 / np.sqrt(np.float32(chans))
    v = ((2 * probe_signs - 1).astype(F32) * unit).astype(BF)
    later, along[-1], v = lax.optimization_barrier((own, along[-1], v))
    late = swap(later, 1, 1)
    sides = pl.pallas_call(
        functools.partial(own_kernel, cfg),
        out_shape=side_a + side_b,
        in_specs=[SMEM, SMEM] + [VMEM] * 4,
        out_specs=[VMEM] * 11,
        compiler_params=params(),
        cost_estimate=cost(0.01),
        name="own_rows",
    )(place, crop_mask, mask_v, weights, v, own)
    sides = pl.pallas_call(
        functools.partial(rows_kernel, cfg),
        out_shape=side_a + side_b,
        in_specs=[SMEM, SMEM] + [VMEM] * (3 + g1 + g2 - 3 + 11),
        out_specs=[VMEM] * 11,
        input_output_aliases={2 + g1 + g2 + i: i for i in range(11)},
        compiler_params=params(),
        cost_estimate=cost(0.01),
        name="rows",
    )(place, crop_mask, mask_v, weights, v, *plane, *along, *sides)
    keep, send, y, *_ = pl.pallas_call(
        functools.partial(block_kernel, cfg),
        out_shape=[half, half, shape(pairs, BF)] + side_a,
        in_specs=[SMEM, SMEM] + [VMEM] * 15,
        out_specs=[VMEM] * 9,
        input_output_aliases={11 + i: 3 + i for i in range(6)},
        scratch_shapes=[pltpu.VMEM((pairs[0] * 8, chans), F32)] * 2
        + [pltpu.VMEM(pairs, F32)] * 3
        + [pltpu.VMEM((max(n_i, n_j) * width, 2 * chans), BF)]
        + [pltpu.VMEM((2, 3 * chans, chans), F32)],
        compiler_params=params(),
        cost_estimate=cost(5.0),
        name="block",
    )(place, crop_mask, mask_v, weights, v, *sides[6:], late, *sides[:6])

    def plus(one, two):
        return (one.astype(F32) + two.astype(F32)).astype(BF)

    g = plus(keep, crop_swap(send, 1))
    bit = 2
    while bit < n_crop:
        g = plus(g, crop_swap(g, bit))
        bit *= 2
    y = y.reshape(g1, 1, rows * n_j, chans)
    bit = 1
    while bit < g1:
        parts = y.reshape((y.shape[0] // 2, 2) + y.shape[1:])
        out = parts[:, 1].reshape(-1, chans)
        got = swap(jnp.concatenate([g, out], axis=0), bit, 1)
        g = plus(g, got[: 3 * chans])
        y = jnp.concatenate([parts[:, 0], got[3 * chans :].reshape(parts[:, 1].shape)], axis=1)
        bit *= 2
    new_pair = pl.pallas_call(
        functools.partial(pair_kernel, cfg),
        out_shape=shape(own.shape, BF),
        in_specs=[SMEM] + [VMEM] * 2,
        out_specs=VMEM,
        compiler_params=params(),
        cost_estimate=cost(0.5),
        name="new_pair",
    )(place, own, y[0])
    bit = 1
    while bit < g2:
        g = plus(g, swap(g, bit, g1, False))
        g, new_pair = lax.optimization_barrier((g, new_pair))
        bit *= 2
    curvature = pl.pallas_call(
        functools.partial(last_kernel, cfg),
        out_shape=shape(weights.shape, F32),
        in_specs=[SMEM] + [VMEM] * 2,
        out_specs=VMEM,
        scratch_shapes=[pltpu.VMEM((2, 3 * chans, chans), F32)],
        compiler_params=params(),
        cost_estimate=cost(0.5),
        name="halves",
    )(place, g, crop_swap(g, 1))
    return (new_pair[None], curvature)


def solution(mesh):
    placed = (P("crop", "axial", None, None), P("crop", None), P(), P())
    return jax.shard_map(
        shards,
        mesh=mesh,
        in_specs=placed,
        out_specs=(P("crop", "axial", None, None), P()),
        check_vma=False,
    )
```

time: 49.7 us -> 46.2 us (0.930)
  local copies, waits for them, and re-layouts: 2.86 us -> 0.1 us
  waiting for transfers between devices: 19.9 us -> 17.4 us
  Pallas kernels: 8.5 us -> 10.9 us
  starting transfers between devices: 17 us -> 15.6 us
  other arithmetic: 0.26 us -> 1.32 us
    unnamed x10 -> x6, local copies, waits for them, and re-layouts: 2.77 us -> 0.01 us
    ppermute x12, waiting for transfers between devices: 19.9 us -> 17.4 us  [the longest x10 14.8 us: swap(): return lax.ppermute(value, ('crop', 'axial'), pairs)]
    pallas_call x2 -> x5, Pallas kernels: 8.5 us -> 10.9 us  [the longest x1 5.67 us: shards(): pl.pallas_call(functools.partial(block_kernel, cfg), out_shape=[half, hal...]
    ppermute x12, starting transfers between devices: 17 us -> 15.6 us  [the longest x10 15.5 us: swap(): return lax.ppermute(value, ('crop', 'axial'), pairs)]
    convert_element_type x0 -> x1, other arithmetic: none -> 1.05 us  [shards(): v = ((2 * probe_signs - 1).astype(F32) * unit).astype(BF)]
  transfers between devices with their start and end apart: 12 -> 12, of which waited for: 10 -> 9; matrix products, arithmetic and copies ran while one was open for 0% -> 3% of each run, Pallas kernels for 0% -> 8%
where the time goes in v2:
time: 46.2 us; the launch traced here: 46.1 us
  waiting for transfers between devices  17.4 us (38%)
  starting transfers between devices  15.6 us (34%)
  Pallas kernels  10.9 us (24%)
  other arithmetic  1.32 us (3%)
  between operations  0.82 us (2%)
    ppermute x10, starting transfers between devices, swap(): return lax.ppermute(value, ('crop', 'axial'), pairs)  15.5 us
    ppermute x10, waiting for transfers between devices, swap(): return lax.ppermute(value, ('crop', 'axial'), pairs)  14.8 us
    pallas_call x1, Pallas kernels, shards(): pl.pallas_call(functools.partial(block_kernel, cfg), out_shape=[half, hal...  5.67 us
    ppermute x2, waiting for transfers between devices, crop_swap(): return lax.ppermute(value, 'crop', [(i, i ^ bit) for i in range(n_crop)])  2.56 us
    pallas_call x1, Pallas kernels, shards(): pl.pallas_call(functools.partial(rows_kernel, cfg), out_shape=side_a + si...  1.45 us
    pallas_call x1, Pallas kernels, shards(): pl.pallas_call(functools.partial(last_kernel, cfg), out_shape=shape(weigh...  1.34 us
    pallas_call x1, Pallas kernels, shards(): pl.pallas_call(functools.partial(pair_kernel, cfg), out_shape=shape(own.s...  1.32 us
    pallas_call x1, Pallas kernels, shards(): pl.pallas_call(functools.partial(own_kernel, cfg), out_shape=side_a + sid...  1.07 us
  transfers between devices with their start and end apart: 12, of which 9 were waited for; matrix products, arithmetic and copies ran while one was open for 3% of the time, Pallas kernels for 8%

profile of v2, /device:TPU:0, one launch (start us, length us, event | category | flops | bytes accessed | tf_op | source)
XLA Modules:
  0.0 46.1 jit_solution(8884625229489454615)
XLA Ops:
  0.6 0.0 copy-start.2
  0.6 0.0 copy-start.1
  0.7 0.0 copy-start
  0.7 5.1 %collective-permute-start = (bf16[4,64,128]{2,1,0:T(8,128)(2,1)}, bf16[4,64,128]{2,1,0:T(8,128)(2,1)S(1)}, u32[]{:S(2)}, u32[]{:S(2)}) collective-permute-start(bf16[4,64,128]{2,1,0:T(8,128)(2,1)} %bitcast.23), channel_id=1, source_target_pairs={{0,12},{1,13},{2,14},{3,15},{4,8},{5,9},{6,10},{7,11},{8,4},{9,5},... | collective-permute-start | bytes 196616 | tf_op jit(solution)/shard_map/ppermute | solution.py:238
  5.8 1.5 %collective-permute-start.1 = (bf16[4,64,128]{2,1,0:T(8,128)(2,1)}, bf16[4,64,128]{2,1,0:T(8,128)(2,1)S(1)}, u32[]{:S(2)}, u32[]{:S(2)}) collective-permute-start(bf16[4,64,128]{2,1,0:T(8,128)(2,1)} %bitcast.24), channel_id=1, source_target_pairs={{0,2},{1,3},{2,0},{3,1},{4,6},{5,7},{6,4},{7,5},{8,10},{9,11},{10,... | collective-permute-start | bytes 196616 | tf_op jit(solution)/shard_map/ppermute | solution.py:238
  7.3 1.4 %collective-permute-start.2 = (bf16[4,64,128]{2,1,0:T(8,128)(2,1)}, bf16[4,64,128]{2,1,0:T(8,128)(2,1)S(1)}, u32[]{:S(2)}, u32[]{:S(2)}) collective-permute-start(bf16[4,64,128]{2,1,0:T(8,128)(2,1)} %bitcast.25), channel_id=1, source_target_pairs={{0,3},{1,2},{2,1},{3,0},{4,7},{5,6},{6,5},{7,4},{8,11},{9,10},{10,... | collective-permute-start | bytes 196616 | tf_op jit(solution)/shard_map/ppermute | solution.py:238
  8.7 0.0 collective-permute-start.3
  8.7 0.8 %collective-permute-start.4 = (bf16[4,64,128]{2,1,0:T(8,128)(2,1)}, bf16[4,64,128]{2,1,0:T(8,128)(2,1)S(1)}, u32[]{:S(2)}, u32[]{:S(2)}) collective-permute-start(bf16[4,64,128]{2,1,0:T(8,128)(2,1)} %bitcast.27), channel_id=1, source_target_pairs={{0,8},{1,9},{2,10},{3,11},{4,12},{5,13},{6,14},{7,15},{8,0},{9,1},... | collective-permute-start | bytes 196616 | tf_op jit(solution)/shard_map/ppermute | solution.py:238
  9.5 1.1 %multiply_convert_fusion.v_ref.v_s = bf16[128,768]{1,0:T(8,128)(2,1)S(1)} fusion(s32[128,768]{1,0:T(8,128)} %param.7), kind=kLoop, calls=%fused_computation | loop fusion | flops 491520 | bytes 589824 | tf_op jit(solution)/shard_map/convert_element_type | solution.py:254
  10.6 0.0 copy-done.2
  10.6 0.0 collective-permute-done.rest_4_
  10.6 0.0 copy-done.1
  10.6 0.5 collective-permute-start.5
  11.1 0.1 pad_add_fusion.place
  11.2 0.1 broadcast_in_dim.4.mask_v
  11.2 0.0 copy-done
  11.2 1.1 %own_rows.1 = (bf16[128,1024]{1,0:T(8,128)(2,1)S(1)}, f32[1024,128]{1,0:T(8,128)S(1)}, f32[1024,128]{1,0:T(8,128)S(1)}, f32[1024,128]{1,0:T(8,128)S(1)}, f32[102...) custom-call(s32[2]{0:T(128)S(1)} %pad_add_fusion.place, ...), custom_call_target="tpu_custom_call" | custom-call | flops 10000000 | tf_op jit(solution)/shard_map/own_rows/pallas_call | solution.py:257
  12.3 0.0 collective-permute-done.1.rest_0_
  12.3 0.5 %collective-permute-done.2.rest_1_ = bf16[4,64,128]{2,1,0:T(8,128)(2,1)S(1)} collective-permute-done((bf16[4,64,128]{2,1,0:T(8,128)(2,1)}, bf16[4,64,128]{2,1,0:T(8,128)(2,1)S(1)}, u32[]{:S(2)}, u32[]{:S(2)}) %collective-permute-start.2) | collective-permute-done | bytes 65568 | tf_op jit(solution)/shard_map/ppermute | solution.py:238
  12.8 0.4 collective-permute-done.3.rest_2_
  13.2 0.9 %collective-permute-done.4.rest_3_ = bf16[4,64,128]{2,1,0:T(8,128)(2,1)S(1)} collective-permute-done((bf16[4,64,128]{2,1,0:T(8,128)(2,1)}, bf16[4,64,128]{2,1,0:T(8,128)(2,1)S(1)}, u32[]{:S(2)}, u32[]{:S(2)}) %collective-permute-start.4) | collective-permute-done | bytes 65568 | tf_op jit(solution)/shard_map/ppermute | solution.py:238
  14.1 1.5 %rows.1 = (bf16[128,1024]{1,0:T(8,128)(2,1)S(1)}, f32[1024,128]{1,0:T(8,128)S(1)}, f32[1024,128]{1,0:T(8,128)S(1)}, f32[1024,128]{1,0:T(8,128)S(1)}, f32[1024,12...) custom-call(s32[2]{0:T(128)S(1)} %pad_add_fusion.place, ...), custom_call_target="tpu_custom_call", output_to_operand_aliasing={{0}: (10, {}), {1}: (11, {}), {2}: (12, {}), {3}: (13, {}),... | custom-call | flops 10000000 | tf_op jit(solution)/shard_map/rows/pallas_call | solution.py:266
  15.6 0.0 collective-permute-done.5.late_ref
  15.6 5.7 %block.1 = (bf16[384,128]{1,0:T(8,128)(2,1)S(1)}, bf16[384,128]{1,0:T(8,128)(2,1)S(1)}, bf16[256,128]{1,0:T(8,128)(2,1)S(1)}, bf16[128,1024]{1,0:T(8,128)(2,1)S(...) custom-call(s32[2]{0:T(128)S(1)} %pad_add_fusion.place, ...), custom_call_target="tpu_custom_call", output_to_operand_aliasing={{3}: (11, {}), {4}: (12, {}), {5}: (13, {}), {6}: (14, {}),... | custom-call | flops 5000000000 | tf_op jit(solution)/shard_map/block/pallas_call | solution.py:276
  21.3 0.1 collective-permute-start.6
  21.3 1.3 %collective-permute-done.6 = bf16[384,128]{1,0:T(8,128)(2,1)S(1)} collective-permute-done((bf16[384,128]{1,0:T(8,128)(2,1)S(1)}, bf16[384,128]{1,0:T(8,128)(2,1)S(1)}, u32[]{:S(2)}, u32[]{:S(2)}) %collective-permute-start.6) | collective-permute-done | bytes 98336 | tf_op jit(solution)/shard_map/ppermute | solution.py:230
  22.7 1.1 %collective-permute-start.7 = (bf16[512,128]{1,0:T(8,128)(2,1)S(1)}, bf16[512,128]{1,0:T(8,128)(2,1)S(1)}, u32[]{:S(2)}, u32[]{:S(2)}) collective-permute-start(bf16[512,128]{1,0:T(8,128)(2,1)S(1)} %pad_maximum_fusion), channel_id=1, source_target_pairs={{0,1},{1,0},{2,3},{3,2},{4,5},{5,4},{6,7},{7,6},{8,9},{9,8},{10,11... | collective-permute-start | bytes 393224 | tf_op jit(solution)/shard_map/ppermute | solution.py:238
  23.7 4.0 %collective-permute-done.7 = bf16[512,128]{1,0:T(8,128)(2,1)S(1)} collective-permute-done((bf16[512,128]{1,0:T(8,128)(2,1)S(1)}, bf16[512,128]{1,0:T(8,128)(2,1)S(1)}, u32[]{:S(2)}, u32[]{:S(2)}) %collective-permute-start.7) | collective-permute-done | bytes 131104 | tf_op jit(solution)/shard_map/ppermute | solution.py:238
  27.8 1.6 %collective-permute-start.8 = (bf16[512,128]{1,0:T(8,128)(2,1)S(1)}, bf16[512,128]{1,0:T(8,128)(2,1)S(1)}, u32[]{:S(2)}, u32[]{:S(2)}) collective-permute-start(bf16[512,128]{1,0:T(8,128)(2,1)S(1)} %pad_maximum_fusion.1), channel_id=1, source_target_pairs={{0,2},{1,3},{2,0},{3,1},{4,6},{5,7},{6,4},{7,5},{8,10},{9,11},{10,... | collective-permute-start | bytes 393224 | tf_op jit(solution)/shard_map/ppermute | solution.py:238
  29.4 3.4 %collective-permute-done.8 = bf16[512,128]{1,0:T(8,128)(2,1)S(1)} collective-permute-done((bf16[512,128]{1,0:T(8,128)(2,1)S(1)}, bf16[512,128]{1,0:T(8,128)(2,1)S(1)}, u32[]{:S(2)}, u32[]{:S(2)}) %collective-permute-start.8) | collective-permute-done | bytes 131104 | tf_op jit(solution)/shard_map/ppermute | solution.py:238
  32.9 2.1 %collective-permute-start.9 = (bf16[384,128]{1,0:T(8,128)(2,1)S(1)}, bf16[384,128]{1,0:T(8,128)(2,1)S(1)}, u32[]{:S(2)}, u32[]{:S(2)}) collective-permute-start(bf16[384,128]{1,0:T(8,128)(2,1)S(1)} %add_convert_fusion.2), channel_id=1, source_target_pairs={{0,4},{1,5},{2,6},{3,7},{4,0},{5,1},{6,2},{7,3},{8,12},{9,13},{10,... | collective-permute-start | bytes 294920 | tf_op jit(solution)/shard_map/ppermute | solution.py:238
  35.0 1.3 %new_pair.1 = bf16[4,64,128]{2,1,0:T(8,128)(2,1)} custom-call(s32[2]{0:T(128)S(1)} %pad_add_fusion.place, bf16[4,64,128]{2,1,0:T(8,128)(2,1)S(1)} %bitcast.30, bf16[4,64,128]{2,1,0:T(8,128)(2,1)S(1)} %maximum_bitcast_fusion.1.y_ref), custom_call_target="tpu_custom_call" | custom-call | flops 500000000 | tf_op jit(solution)/shard_map/new_pair/pallas_call | solution.py:308
  36.3 1.4 %collective-permute-done.9 = bf16[384,128]{1,0:T(8,128)(2,1)S(1)} collective-permute-done((bf16[384,128]{1,0:T(8,128)(2,1)S(1)}, bf16[384,128]{1,0:T(8,128)(2,1)S(1)}, u32[]{:S(2)}, u32[]{:S(2)}) %collective-permute-start.9) | collective-permute-done | bytes 98336 | tf_op jit(solution)/shard_map/ppermute | solution.py:238
  37.7 1.4 %collective-permute-start.10 = (bf16[384,128]{1,0:T(8,128)(2,1)S(1)}, bf16[384,128]{1,0:T(8,128)(2,1)S(1)}, u32[]{:S(2)}, u32[]{:S(2)}) collective-permute-start(bf16[384,128]{1,0:T(8,128)(2,1)S(1)} %add_convert_fusion.1), channel_id=1, source_target_pairs={{0,8},{1,9},{2,10},{3,11},{4,12},{5,13},{6,14},{7,15},{8,0},{9,1},... | collective-permute-start | bytes 294920 | tf_op jit(solution)/shard_map/ppermute | solution.py:238
  39.1 4.2 %collective-permute-done.10 = bf16[384,128]{1,0:T(8,128)(2,1)S(1)} collective-permute-done((bf16[384,128]{1,0:T(8,128)(2,1)S(1)}, bf16[384,128]{1,0:T(8,128)(2,1)S(1)}, u32[]{:S(2)}, u32[]{:S(2)}) %collective-permute-start.10) | collective-permute-done | bytes 98336 | tf_op jit(solution)/shard_map/ppermute | solution.py:238
  43.3 0.1 collective-permute-start.11
  43.4 1.3 %collective-permute-done.11.other_ref = bf16[384,128]{1,0:T(8,128)(2,1)S(1)} collective-permute-done((bf16[384,128]{1,0:T(8,128)(2,1)S(1)}, bf16[384,128]{1,0:T(8,128)(2,1)S(1)}, u32[]{:S(2)}, u32[]{:S(2)}) %collective-permute-start.11) | collective-permute-done | bytes 98336 | tf_op jit(solution)/shard_map/ppermute | solution.py:230
  44.7 1.3 %halves.1 = f32[128,768]{1,0:T(8,128)} custom-call(s32[2]{0:T(128)S(1)} %pad_add_fusion.place, bf16[384,128]{1,0:T(8,128)(2,1)S(1)} %add_convert_fusion.mine_ref, bf16[384,128]{1,0:T(8,128)(2,1)S(1)} %collective-permute-done.11.other_ref), custom_call_target="tpu_custom_call" | custom-call | flops 500000000 | tf_op jit(solution)/shard_map/halves/pallas_call | solution.py:322
  (14 shorter events, 0.2 us)
Async XLA Ops:
  0.6 9.9 %copy-start.2 = (s32[1,64]{1,0:T(1,128)S(1)}, s32[1,64]{1,0:T(1,128)}, u32[]{:S(2)}) copy-start(s32[1,64]{1,0:T(1,128)} %mask_s.5) | copy-start | bytes 772
  0.6 10.0 %copy-start.1 = (bf16[1,4,64,128]{3,2,1,0:T(8,128)(2,1)S(1)}, bf16[1,4,64,128]{3,2,1,0:T(8,128)(2,1)}, u32[]{:S(2)}) copy-start(bf16[1,4,64,128]{3,2,1,0:T(8,128)(2,1)} %param.4) | copy-start | bytes 196612
  0.7 10.6 %copy-start = (bf16[128,768]{1,0:T(8,128)(2,1)S(1)}, bf16[128,768]{1,0:T(8,128)(2,1)}, u32[]{:S(2)}) copy-start(bf16[128,768]{1,0:T(8,128)(2,1)} %w_ref.5) | copy-start | bytes 589828
  0.7 9.9 %collective-permute-start = (bf16[4,64,128]{2,1,0:T(8,128)(2,1)}, bf16[4,64,128]{2,1,0:T(8,128)(2,1)S(1)}, u32[]{:S(2)}, u32[]{:S(2)}) collective-permute-start(bf16[4,64,128]{2,1,0:T(8,128)(2,1)} %bitcast.23), channel_id=1, source_target_pairs={{0,12},{1,13},{2,14},{3,15},{4,8},{5,9},{6,10},{7,11},{8,4},{9,5},... | collective-permute-start | bytes 196616 | tf_op jit(solution)/shard_map/ppermute | solution.py:238
  5.8 6.5 %collective-permute-start.1 = (bf16[4,64,128]{2,1,0:T(8,128)(2,1)}, bf16[4,64,128]{2,1,0:T(8,128)(2,1)S(1)}, u32[]{:S(2)}, u32[]{:S(2)}) collective-permute-start(bf16[4,64,128]{2,1,0:T(8,128)(2,1)} %bitcast.24), channel_id=1, source_target_pairs={{0,2},{1,3},{2,0},{3,1},{4,6},{5,7},{6,4},{7,5},{8,10},{9,11},{10,... | collective-permute-start | bytes 196616 | tf_op jit(solution)/shard_map/ppermute | solution.py:238
  7.3 5.5 %collective-permute-start.2 = (bf16[4,64,128]{2,1,0:T(8,128)(2,1)}, bf16[4,64,128]{2,1,0:T(8,128)(2,1)S(1)}, u32[]{:S(2)}, u32[]{:S(2)}) collective-permute-start(bf16[4,64,128]{2,1,0:T(8,128)(2,1)} %bitcast.25), channel_id=1, source_target_pairs={{0,3},{1,2},{2,1},{3,0},{4,7},{5,6},{6,5},{7,4},{8,11},{9,10},{10,... | collective-permute-start | bytes 196616 | tf_op jit(solution)/shard_map/ppermute | solution.py:238
  8.7 4.5 %collective-permute-start.3 = (bf16[4,64,128]{2,1,0:T(8,128)(2,1)}, bf16[4,64,128]{2,1,0:T(8,128)(2,1)S(1)}, u32[]{:S(2)}, u32[]{:S(2)}) collective-permute-start(bf16[4,64,128]{2,1,0:T(8,128)(2,1)} %bitcast.26), channel_id=1, source_target_pairs={{0,4},{1,5},{2,6},{3,7},{4,0},{5,1},{6,2},{7,3},{8,12},{9,13},{10,... | collective-permute-start | bytes 196616 | tf_op jit(solution)/shard_map/ppermute | solution.py:238
  8.7 5.4 %collective-permute-start.4 = (bf16[4,64,128]{2,1,0:T(8,128)(2,1)}, bf16[4,64,128]{2,1,0:T(8,128)(2,1)S(1)}, u32[]{:S(2)}, u32[]{:S(2)}) collective-permute-start(bf16[4,64,128]{2,1,0:T(8,128)(2,1)} %bitcast.27), channel_id=1, source_target_pairs={{0,8},{1,9},{2,10},{3,11},{4,12},{5,13},{6,14},{7,15},{8,0},{9,1},... | collective-permute-start | bytes 196616 | tf_op jit(solution)/shard_map/ppermute | solution.py:238
  10.6 4.9 %collective-permute-start.5 = (bf16[4,64,128]{2,1,0:T(8,128)(2,1)S(1)}, bf16[4,64,128]{2,1,0:T(8,128)(2,1)S(1)}, u32[]{:S(2)}, u32[]{:S(2)}) collective-permute-start(bf16[4,64,128]{2,1,0:T(8,128)(2,1)S(1)} %bitcast.28), channel_id=1, source_target_pairs={{0,1},{1,0},{2,3},{3,2},{4,5},{5,4},{6,7},{7,6},{8,9},{9,8},{10,11... | collective-permute-start | bytes 196616 | tf_op jit(solution)/shard_map/ppermute | solution.py:238
  21.3 1.4 %collective-permute-start.6 = (bf16[384,128]{1,0:T(8,128)(2,1)S(1)}, bf16[384,128]{1,0:T(8,128)(2,1)S(1)}, u32[]{:S(2)}, u32[]{:S(2)}) collective-permute-start(bf16[384,128]{1,0:T(8,128)(2,1)S(1)} %get-tuple-element.60), channel_id=1, source_target_pairs={{0,16},{16,0},{1,17},{17,1},{2,18},{18,2},{3,19},{19,3},{4,20},{20... | collective-permute-start | bytes 294920 | tf_op jit(solution)/shard_map/ppermute | solution.py:230
  22.7 5.0 %collective-permute-start.7 = (bf16[512,128]{1,0:T(8,128)(2,1)S(1)}, bf16[512,128]{1,0:T(8,128)(2,1)S(1)}, u32[]{:S(2)}, u32[]{:S(2)}) collective-permute-start(bf16[512,128]{1,0:T(8,128)(2,1)S(1)} %pad_maximum_fusion), channel_id=1, source_target_pairs={{0,1},{1,0},{2,3},{3,2},{4,5},{5,4},{6,7},{7,6},{8,9},{9,8},{10,11... | collective-permute-start | bytes 393224 | tf_op jit(solution)/shard_map/ppermute | solution.py:238
  27.8 5.0 %collective-permute-start.8 = (bf16[512,128]{1,0:T(8,128)(2,1)S(1)}, bf16[512,128]{1,0:T(8,128)(2,1)S(1)}, u32[]{:S(2)}, u32[]{:S(2)}) collective-permute-start(bf16[512,128]{1,0:T(8,128)(2,1)S(1)} %pad_maximum_fusion.1), channel_id=1, source_target_pairs={{0,2},{1,3},{2,0},{3,1},{4,6},{5,7},{6,4},{7,5},{8,10},{9,11},{10,... | collective-permute-start | bytes 393224 | tf_op jit(solution)/shard_map/ppermute | solution.py:238
  32.9 4.8 %collective-permute-start.9 = (bf16[384,128]{1,0:T(8,128)(2,1)S(1)}, bf16[384,128]{1,0:T(8,128)(2,1)S(1)}, u32[]{:S(2)}, u32[]{:S(2)}) collective-permute-start(bf16[384,128]{1,0:T(8,128)(2,1)S(1)} %add_convert_fusion.2), channel_id=1, source_target_pairs={{0,4},{1,5},{2,6},{3,7},{4,0},{5,1},{6,2},{7,3},{8,12},{9,13},{10,... | collective-permute-start | bytes 294920 | tf_op jit(solution)/shard_map/ppermute | solution.py:238
  37.7 5.6 %collective-permute-start.10 = (bf16[384,128]{1,0:T(8,128)(2,1)S(1)}, bf16[384,128]{1,0:T(8,128)(2,1)S(1)}, u32[]{:S(2)}, u32[]{:S(2)}) collective-permute-start(bf16[384,128]{1,0:T(8,128)(2,1)S(1)} %add_convert_fusion.1), channel_id=1, source_target_pairs={{0,8},{1,9},{2,10},{3,11},{4,12},{5,13},{6,14},{7,15},{8,0},{9,1},... | collective-permute-start | bytes 294920 | tf_op jit(solution)/shard_map/ppermute | solution.py:238
  43.3 1.4 %collective-permute-start.11 = (bf16[384,128]{1,0:T(8,128)(2,1)S(1)}, bf16[384,128]{1,0:T(8,128)(2,1)S(1)}, u32[]{:S(2)}, u32[]{:S(2)}) collective-permute-start(bf16[384,128]{1,0:T(8,128)(2,1)S(1)} %add_convert_fusion.mine_ref), channel_id=1, source_target_pairs={{0,16},{16,0},{1,17},{17,1},{2,18},{18,2},{3,19},{19,3},{4,20},{20... | collective-permute-start | bytes 294920 | tf_op jit(solution)/shard_map/ppermute | solution.py:230

commit v3 on v2

--- a/solution.py
+++ b/solution.py
@@ -11,6 +11,7 @@
 BF = jnp.bfloat16
 F32 = jnp.float32
 VMEM = pl.BlockSpec(memory_space=pltpu.VMEM)
+ANY = pl.BlockSpec(memory_space=pl.ANY)
 SMEM = pl.BlockSpec(memory_space=pltpu.SMEM)
 
 
@@ -91,31 +92,15 @@
     fill_side(cfg, place, mask_s, mask_v, w_ref, v_ref, [(0, own_ref)], g1, 2 * chans, outs[6:])
 
 
-def rows_kernel(cfg, place, mask_s, mask_v, w_ref, v_ref, *rest):
-    g1, g2, chans = cfg[0], cfg[1], cfg[4]
-    count = g1 + g2 - 3
-    refs, outs = rest[:count], rest[count + 11 :]
-    fill_side(cfg, place, mask_s, mask_v, w_ref, v_ref,
-              [(m + 1, refs[g1 - 2 + m]) for m in range(g2 - 1)], g1, 2 * chans, outs[6:])
-    fill_side(cfg, place, mask_s, mask_v, w_ref, v_ref,
-              [(m + 2, refs[m]) for m in range(g1 - 2)], 1, 0, outs[:6])
-
-
-def block_kernel(cfg, place, mask_s, mask_v, w_ref, v_s, zj_s, b_s, tb_s, sb_s, gb_s, late_ref, *rest):
-    g1, g2, rows, width, chans, total = cfg
-    (keep_ref, send_ref, y_ref, zi_s, a_s, ta_s, sa_s, ga_s, zp_s,
-     px_s, pt_s, x_s, tx_s, xb_s, d_s, g_s) = rest[6:]
-    n_i, n_j = g1 * rows, g2 * rows
-    blk = rows * width
-    core = place[1]
-    fill_side(cfg, place, mask_s, mask_v, w_ref, v_s, [(1, late_ref)], 1, 0,
-              (zi_s, a_s, ta_s, sa_s, ga_s, zp_s))
+def triangle(cfg, first, count, a_s, ta_s, b_s, tb_s, px_s, pt_s, x_ref, tx_ref):
+    _, g2, rows, width, chans, _ = cfg
+    n_j = g2 * rows
 
     def fold(value):
         return jnp.sum(value.reshape(width // 8, 8, chans), axis=0)
 
     def tri(i, carry):
-        at = pl.ds(pl.multiple_of(i * width, width), width)
+        at = pl.ds(pl.multiple_of((first + i) * width, width), width)
         a, ta = a_s[at, :].astype(F32), ta_s[at, :].astype(F32)
         for j in range(n_j):
             here = slice(j * width, (j + 1) * width)
@@ -125,10 +110,36 @@
             pt_s[to, :] = fold(ta * b + a * tb)
         return carry
 
-    lax.fori_loop(0, n_i, tri, 0)
+    lax.fori_loop(0, count, tri, 0, unroll=2 if width <= 64 else 1)
+    pairs = count * n_j
+    here = slice(first * n_j, (first + count) * n_j)
+    for part, out in ((px_s, x_ref), (pt_s, tx_ref)):
+        total = sum(part[pl.ds(s, pairs, stride=8), :] for s in range(8))
+        out[here, :] = total.astype(BF).astype(F32)
+
+
+def line_kernel(cfg, place, mask_s, mask_v, w_ref, v_ref, a_s, ta_s, *rest):
+    g1, g2, rows, width, chans, _ = cfg
+    refs, (*outs, x_ref, tx_ref, px_s, pt_s) = rest[: g2 - 1], rest[g2 + 4 :]
+    fill_side(cfg, place, mask_s, mask_v, w_ref, v_ref,
+              [(m + 1, refs[m]) for m in range(g2 - 1)], g1, 2 * chans, outs)
+    triangle(cfg, 0, rows, a_s, ta_s, outs[1], outs[2], px_s, pt_s, x_ref, tx_ref)
+
+
+def block_kernel(cfg, place, mask_s, mask_v, w_ref, v_s, zj_s, b_s, tb_s, sb_s, gb_s, x_in, tx_in, *rest):
+    g1, g2, rows, width, chans, total = cfg
+    refs = rest[: g1 - 1]
+    (keep_ref, send_ref, y_ref, zi_s, a_s, ta_s, sa_s, ga_s, zp_s,
+     px_s, pt_s, x_s, tx_s, xb_s, d_s, g_s) = rest[g1 + 5 :]
+    n_i, n_j = g1 * rows, g2 * rows
+    blk = rows * width
+    core = place[1]
+    fill_side(cfg, place, mask_s, mask_v, w_ref, v_s,
+              [(m, refs[m - 1]) for m in range(g1 - 1, 0, -1)], 1, 0, (zi_s, a_s, ta_s, sa_s, ga_s, zp_s))
+    x_s[: rows * n_j, :] = x_in[...]
+    tx_s[: rows * n_j, :] = tx_in[...]
+    triangle(cfg, rows, n_i - rows, a_s, ta_s, b_s, tb_s, px_s, pt_s, x_s, tx_s)
     pairs = n_i * n_j
-    x_s[...] = sum(px_s[pl.ds(s, pairs, stride=8), :] for s in range(8)).astype(BF).astype(F32)
-    tx_s[...] = sum(pt_s[pl.ds(s, pairs, stride=8), :] for s in range(8)).astype(BF).astype(F32)
 
     w_gate, w_out = w_ref[:, 4 * chans : 5 * chans], w_ref[:, 5 * chans :]
     v_gate, v_out = v_s[:, 4 * chans : 5 * chans], v_s[:, 5 * chans :]
@@ -166,22 +177,24 @@
 
     def back(count, others, row_of, val_s, sig_s, gate_s, z_s, spots):
         def one(m, carry):
-            bars = []
-            for r in range(rows):
-                for kc in range(0, width, chunk):
-                    acc = None
-                    for o in range(others):
-                        row = xb_s[pl.ds(row_of(m * rows + r, o), 1), :]
-                        term = row * val_s[o * width + kc : o * width + kc + chunk, :].astype(F32)
-                        acc = term if acc is None else acc + term
-                    bars.append(acc)
+            bars = [[] for _ in range(rows)]
+            for kc in range(0, width, chunk):
+                sums = [None] * rows
+                for o in range(others):
+                    val = val_s[o * width + kc : o * width + kc + chunk, :].astype(F32)
+                    for r in range(rows):
+                        term = xb_s[pl.ds(row_of(m * rows + r, o), 1), :] * val
+                        sums[r] = term if o == 0 else sums[r] + term
+                for r in range(rows):
+                    bars[r].append(sums[r])
+            bars = sum(bars, [])
             at = pl.ds(pl.multiple_of(m * blk, blk), blk)
             bar = jnp.concatenate(bars, axis=0)
             d_s[at, :chans] = (bar * sig_s[at, :].astype(F32)).astype(BF)
             d_s[at, chans:] = (bar * gate_s[at, :].astype(F32)).astype(BF)
             return carry
 
-        lax.fori_loop(0, count, one, 0)
+        lax.fori_loop(0, count, one, 0, unroll=width <= 64)
         part = dot(z_s[...], d_s[: count * blk, :])
         for n, (half, top) in enumerate(spots):
             g_s[half, top : top + chans, :] = part[:, n * chans : (n + 1) * chans]
@@ -207,16 +220,6 @@
         new_ref[r] = (pair_ref[r].astype(F32) + dot(put, y)).astype(BF)
 
 
-def last_kernel(cfg, place, mine_ref, other_ref, curv_ref, g_s):
-    chans = cfg[4]
-    core = place[1]
-    g_s[core] = mine_ref[...].astype(F32)
-    g_s[1 - core] = other_ref[...].astype(F32)
-    for b in range(6):
-        top = (b % 3) * chans
-        curv_ref[:, b * chans : (b + 1) * chans] = g_s[b // 3, top : top + chans, :]
-
-
 def shards(pair, crop_mask, weights, probe_signs):
     own = pair[0]
     rows, width, chans = own.shape
@@ -238,7 +241,6 @@
         return lax.ppermute(value, ("crop", "axial"), pairs)
 
     along = [swap(own, m, g1) for m in range(1, g2)]
-    plane = [swap(own, m, 1) for m in range(2, g1)]
     place = jnp.stack([lax.axis_index("axial"), lax.axis_index("crop") & 1]).astype(jnp.int32)
     mask_v = jnp.broadcast_to(crop_mask[0].astype(F32)[:, None], (width, chans))
     kept = F32 if width <= 64 else BF
@@ -252,8 +254,8 @@
 
     unit = 1.0 / np.sqrt(np.float32(chans))
     v = ((2 * probe_signs - 1).astype(F32) * unit).astype(BF)
-    later, along[-1], v = lax.optimization_barrier((own, along[-1], v))
-    late = swap(later, 1, 1)
+    later, v = lax.optimization_barrier((own, v))
+    plane = [swap(later, m, 1) for m in range(1, g1)]
     sides = pl.pallas_call(
         functools.partial(own_kernel, cfg),
         out_shape=side_a + side_b,
@@ -263,30 +265,34 @@
         cost_estimate=cost(0.01),
         name="own_rows",
     )(place, crop_mask, mask_v, weights, v, own)
-    sides = pl.pallas_call(
-        functools.partial(rows_kernel, cfg),
-        out_shape=side_a + side_b,
-        in_specs=[SMEM, SMEM] + [VMEM] * (3 + g1 + g2 - 3 + 11),
-        out_specs=[VMEM] * 11,
-        input_output_aliases={2 + g1 + g2 + i: i for i in range(11)},
+    own_pairs = shape((rows * n_j, chans), F32)
+    part = pltpu.VMEM((rows * n_j * 8, chans), F32)
+    *line, x, tx = pl.pallas_call(
+        functools.partial(line_kernel, cfg),
+        out_shape=side_b + [own_pairs, own_pairs],
+        in_specs=[SMEM, SMEM] + [VMEM] * (5 + g2 - 1 + 5),
+        out_specs=[VMEM] * 7,
+        input_output_aliases={6 + g2 + i: i for i in range(5)},
+        scratch_shapes=[part, part],
         compiler_params=params(),
         cost_estimate=cost(0.01),
-        name="rows",
-    )(place, crop_mask, mask_v, weights, v, *plane, *along, *sides)
+        name="line",
+    )(place, crop_mask, mask_v, weights, v, sides[1], sides[2], *along, *sides[6:])
+    part = pltpu.VMEM(((n_i - rows) * n_j * 8, chans), F32)
     keep, send, y, *_ = pl.pallas_call(
         functools.partial(block_kernel, cfg),
         out_shape=[half, half, shape(pairs, BF)] + side_a,
-        in_specs=[SMEM, SMEM] + [VMEM] * 15,
+        in_specs=[SMEM, SMEM] + [VMEM] * (10 + g1 - 1 + 6),
         out_specs=[VMEM] * 9,
-        input_output_aliases={11 + i: 3 + i for i in range(6)},
-        scratch_shapes=[pltpu.VMEM((pairs[0] * 8, chans), F32)] * 2
+        input_output_aliases={11 + g1 + i: 3 + i for i in range(6)},
+        scratch_shapes=[part, part]
         + [pltpu.VMEM(pairs, F32)] * 3
         + [pltpu.VMEM((max(n_i, n_j) * width, 2 * chans), BF)]
         + [pltpu.VMEM((2, 3 * chans, chans), F32)],
         compiler_params=params(),
         cost_estimate=cost(5.0),
         name="block",
-    )(place, crop_mask, mask_v, weights, v, *sides[6:], late, *sides[:6])
+    )(place, crop_mask, mask_v, weights, v, *line, x, tx, *plane, *sides[:6])
 
     def plus(one, two):
         return (one.astype(F32) + two.astype(F32)).astype(BF)
@@ -319,16 +325,10 @@
         g = plus(g, swap(g, bit, g1, False))
         g, new_pair = lax.optimization_barrier((g, new_pair))
         bit *= 2
-    curvature = pl.pallas_call(
-        functools.partial(last_kernel, cfg),
-        out_shape=shape(weights.shape, F32),
-        in_specs=[SMEM] + [VMEM] * 2,
-        out_specs=VMEM,
-        scratch_shapes=[pltpu.VMEM((2, 3 * chans, chans), F32)],
-        compiler_params=params(),
-        cost_estimate=cost(0.5),
-        name="halves",
-    )(place, g, crop_swap(g, 1))
+    other = crop_swap(g, 1)
+    first = place[1] == 0
+    low, high = jnp.where(first, g, other), jnp.where(first, other, g)
+    curvature = jnp.concatenate([p[n * chans : (n + 1) * chans].astype(F32) for p in (low, high) for n in range(3)], axis=1)
     return (new_pair[None], curvature)
 
 

time: 46.2 us -> 45.5 us (0.985)
  Pallas kernels: 10.9 us -> 9.28 us
  other arithmetic: 1.32 us -> 2.11 us
    pallas_call x2 -> x1, Pallas kernels: 2.79 us -> 1.77 us  [shards(): pl.pallas_call(functools.partial(line_kernel, cfg), out_shape=side_b + [o...]
    concatenate x0 -> x1, other arithmetic: none -> 0.77 us  [shards(): jnp.concatenate([p[n * chans:(n + 1) * chans].astype(F32) for p in (low,...]
    pallas_call x1, Pallas kernels: 5.67 us -> 5.12 us  [shards(): pl.pallas_call(functools.partial(block_kernel, cfg), out_shape=[half, hal...]
  transfers between devices with their start and end apart: 12 -> 12, of which waited for: 9 -> 8; matrix products, arithmetic and copies ran while one was open for 3% -> 3% of each run, Pallas kernels for 8% -> 9%
where the time goes in v3:
time: 45.5 us; the launch traced here: 45.4 us
  waiting for transfers between devices  17.4 us (38%)
  starting transfers between devices  15.6 us (34%)
  Pallas kernels  9.28 us (20%)
  other arithmetic  2.11 us (5%)
  between operations  0.84 us (2%)
    ppermute x10, starting transfers between devices, swap(): return lax.ppermute(value, ('crop', 'axial'), pairs)  15.4 us
    ppermute x10, waiting for transfers between devices, swap(): return lax.ppermute(value, ('crop', 'axial'), pairs)  14.9 us
    pallas_call x1, Pallas kernels, shards(): pl.pallas_call(functools.partial(block_kernel, cfg), out_shape=[half, hal...  5.12 us
    ppermute x2, waiting for transfers between devices, crop_swap(): return lax.ppermute(value, 'crop', [(i, i ^ bit) for i in range(n_crop)])  2.56 us
    pallas_call x1, Pallas kernels, shards(): pl.pallas_call(functools.partial(line_kernel, cfg), out_shape=side_b + [o...  1.77 us
    pallas_call x1, Pallas kernels, shards(): pl.pallas_call(functools.partial(pair_kernel, cfg), out_shape=shape(own.s...  1.32 us
    pallas_call x1, Pallas kernels, shards(): pl.pallas_call(functools.partial(own_kernel, cfg), out_shape=side_a + sid...  1.07 us
    convert_element_type x1, other arithmetic, shards(): v = ((2 * probe_signs - 1).astype(F32) * unit).astype(BF)  1.05 us
  transfers between devices with their start and end apart: 12, of which 8 were waited for; matrix products, arithmetic and copies ran while one was open for 3% of the time, Pallas kernels for 9%

profile of v3, /device:TPU:0, one launch (start us, length us, event | category | flops | bytes accessed | tf_op | source)
XLA Modules:
  0.0 45.4 jit_solution(14599453253763832392)
XLA Ops:
  0.6 0.0 copy-start.1
  0.6 0.0 copy-start.2
  0.7 0.0 copy-start
  0.7 5.1 %collective-permute-start.2 = (bf16[4,64,128]{2,1,0:T(8,128)(2,1)}, bf16[4,64,128]{2,1,0:T(8,128)(2,1)S(1)}, u32[]{:S(2)}, u32[]{:S(2)}) collective-permute-start(bf16[4,64,128]{2,1,0:T(8,128)(2,1)} %bitcast.21), channel_id=1, source_target_pairs={{0,12},{1,13},{2,14},{3,15},{4,8},{5,9},{6,10},{7,11},{8,4},{9,5},... | collective-permute-start | bytes 196616 | tf_op jit(solution)/shard_map/ppermute | solution.py:241
  5.8 0.0 collective-permute-start.1
  5.8 0.6 %collective-permute-start = (bf16[4,64,128]{2,1,0:T(8,128)(2,1)}, bf16[4,64,128]{2,1,0:T(8,128)(2,1)S(1)}, u32[]{:S(2)}, u32[]{:S(2)}) collective-permute-start(bf16[4,64,128]{2,1,0:T(8,128)(2,1)} %bitcast.23), channel_id=1, source_target_pairs={{0,4},{1,5},{2,6},{3,7},{4,0},{5,1},{6,2},{7,3},{8,12},{9,13},{10,... | collective-permute-start | bytes 196616 | tf_op jit(solution)/shard_map/ppermute | solution.py:241
  6.4 1.1 %multiply_convert_fusion.v_ref.v_s = bf16[128,768]{1,0:T(8,128)(2,1)S(1)} fusion(s32[128,768]{1,0:T(8,128)} %param.7), kind=kLoop, calls=%fused_computation | loop fusion | flops 491520 | bytes 589824 | tf_op jit(solution)/shard_map/convert_element_type | solution.py:256
  7.5 0.0 copy-done.1
  7.5 2.7 %collective-permute-start.5 = (bf16[4,64,128]{2,1,0:T(8,128)(2,1)S(1)}, bf16[4,64,128]{2,1,0:T(8,128)(2,1)S(1)}, u32[]{:S(2)}, u32[]{:S(2)}) collective-permute-start(bf16[4,64,128]{2,1,0:T(8,128)(2,1)S(1)} %bitcast.24), channel_id=1, source_target_pairs={{0,3},{1,2},{2,1},{3,0},{4,7},{5,6},{6,5},{7,4},{8,11},{9,10},{10,... | collective-permute-start | bytes 196616 | tf_op jit(solution)/shard_map/ppermute | solution.py:241
  10.1 0.5 %collective-permute-start.4 = (bf16[4,64,128]{2,1,0:T(8,128)(2,1)S(1)}, bf16[4,64,128]{2,1,0:T(8,128)(2,1)S(1)}, u32[]{:S(2)}, u32[]{:S(2)}) collective-permute-start(bf16[4,64,128]{2,1,0:T(8,128)(2,1)S(1)} %bitcast.25), channel_id=1, source_target_pairs={{0,2},{1,3},{2,0},{3,1},{4,6},{5,7},{6,4},{7,5},{8,10},{9,11},{10,... | collective-permute-start | bytes 196616 | tf_op jit(solution)/shard_map/ppermute | solution.py:241
  10.6 0.0 copy-done.2
  10.7 0.0 collective-permute-done.2.rest_2_
  10.7 0.5 %collective-permute-start.3 = (bf16[4,64,128]{2,1,0:T(8,128)(2,1)S(1)}, bf16[4,64,128]{2,1,0:T(8,128)(2,1)S(1)}, u32[]{:S(2)}, u32[]{:S(2)}) collective-permute-start(bf16[4,64,128]{2,1,0:T(8,128)(2,1)S(1)} %bitcast.26), channel_id=1, source_target_pairs={{0,1},{1,0},{2,3},{3,2},{4,5},{5,4},{6,7},{7,6},{8,9},{9,8},{10,11... | collective-permute-start | bytes 196616 | tf_op jit(solution)/shard_map/ppermute | solution.py:241
  11.1 0.1 pad_add_fusion.place
  11.2 0.1 broadcast_in_dim.4.mask_v
  11.3 0.0 copy-done
  11.3 1.1 %own_rows.1 = (bf16[128,1024]{1,0:T(8,128)(2,1)S(1)}, f32[1024,128]{1,0:T(8,128)S(1)}, f32[1024,128]{1,0:T(8,128)S(1)}, f32[1024,128]{1,0:T(8,128)S(1)}, f32[102...) custom-call(s32[2]{0:T(128)S(1)} %pad_add_fusion.place, ...), custom_call_target="tpu_custom_call" | custom-call | flops 10000000 | tf_op jit(solution)/shard_map/own_rows/pallas_call | solution.py:259
  12.3 0.0 collective-permute-done.1.rest_1_
  12.4 0.0 collective-permute-done.rest_0_
  12.4 1.8 %line.1 = (bf16[128,1024]{1,0:T(8,128)(2,1)S(1)}, f32[1024,128]{1,0:T(8,128)S(1)}, f32[1024,128]{1,0:T(8,128)S(1)}, f32[1024,128]{1,0:T(8,128)S(1)}, f32[1024,12...) custom-call(s32[2]{0:T(128)S(1)} %pad_add_fusion.place, ...), custom_call_target="tpu_custom_call", output_to_operand_aliasing={{0}: (10, {}), {1}: (11, {}), {2}: (12, {}), {3}: (13, {}),... | custom-call | flops 10000000 | tf_op jit(solution)/shard_map/line/pallas_call | solution.py:270
  14.1 0.0 collective-permute-done.5.rest_2_
  14.1 0.3 collective-permute-done.4.rest_1_
  14.4 0.6 %collective-permute-done.3.rest_0_ = bf16[4,64,128]{2,1,0:T(8,128)(2,1)S(1)} collective-permute-done((bf16[4,64,128]{2,1,0:T(8,128)(2,1)S(1)}, bf16[4,64,128]{2,1,0:T(8,128)(2,1)S(1)}, u32[]{:S(2)}, u32[]{:S(2)}) %collective-permute-start.3) | collective-permute-done | bytes 65568 | tf_op jit(solution)/shard_map/ppermute | solution.py:241
  15.0 5.1 %block.1 = (bf16[384,128]{1,0:T(8,128)(2,1)S(1)}, bf16[384,128]{1,0:T(8,128)(2,1)S(1)}, bf16[256,128]{1,0:T(8,128)(2,1)S(1)}, bf16[128,1024]{1,0:T(8,128)(2,1)S(...) custom-call(s32[2]{0:T(128)S(1)} %pad_add_fusion.place, ...), custom_call_target="tpu_custom_call", output_to_operand_aliasing={{3}: (15, {}), {4}: (16, {}), {5}: (17, {}), {6}: (18, {}),... | custom-call | flops 5000000000 | tf_op jit(solution)/shard_map/block/pallas_call | solution.py:282
  20.1 0.1 collective-permute-start.6
  20.2 1.3 %collective-permute-done.6 = bf16[384,128]{1,0:T(8,128)(2,1)S(1)} collective-permute-done((bf16[384,128]{1,0:T(8,128)(2,1)S(1)}, bf16[384,128]{1,0:T(8,128)(2,1)S(1)}, u32[]{:S(2)}, u32[]{:S(2)}) %collective-permute-start.6) | collective-permute-done | bytes 98336 | tf_op jit(solution)/shard_map/ppermute | solution.py:233
  21.5 0.9 %collective-permute-start.7 = (bf16[512,128]{1,0:T(8,128)(2,1)S(1)}, bf16[512,128]{1,0:T(8,128)(2,1)S(1)}, u32[]{:S(2)}, u32[]{:S(2)}) collective-permute-start(bf16[512,128]{1,0:T(8,128)(2,1)S(1)} %pad_maximum_fusion), channel_id=1, source_target_pairs={{0,1},{1,0},{2,3},{3,2},{4,5},{5,4},{6,7},{7,6},{8,9},{9,8},{10,11... | collective-permute-start | bytes 393224 | tf_op jit(solution)/shard_map/ppermute | solution.py:241
  22.4 4.1 %collective-permute-done.7 = bf16[512,128]{1,0:T(8,128)(2,1)S(1)} collective-permute-done((bf16[512,128]{1,0:T(8,128)(2,1)S(1)}, bf16[512,128]{1,0:T(8,128)(2,1)S(1)}, u32[]{:S(2)}, u32[]{:S(2)}) %collective-permute-start.7) | collective-permute-done | bytes 131104 | tf_op jit(solution)/shard_map/ppermute | solution.py:241
  26.7 1.6 %collective-permute-start.8 = (bf16[512,128]{1,0:T(8,128)(2,1)S(1)}, bf16[512,128]{1,0:T(8,128)(2,1)S(1)}, u32[]{:S(2)}, u32[]{:S(2)}) collective-permute-start(bf16[512,128]{1,0:T(8,128)(2,1)S(1)} %pad_maximum_fusion.1), channel_id=1, source_target_pairs={{0,2},{1,3},{2,0},{3,1},{4,6},{5,7},{6,4},{7,5},{8,10},{9,11},{10,... | collective-permute-start | bytes 393224 | tf_op jit(solution)/shard_map/ppermute | solution.py:241
  28.2 3.4 %collective-permute-done.8 = bf16[512,128]{1,0:T(8,128)(2,1)S(1)} collective-permute-done((bf16[512,128]{1,0:T(8,128)(2,1)S(1)}, bf16[512,128]{1,0:T(8,128)(2,1)S(1)}, u32[]{:S(2)}, u32[]{:S(2)}) %collective-permute-start.8) | collective-permute-done | bytes 131104 | tf_op jit(solution)/shard_map/ppermute | solution.py:241
  31.7 1.3 %collective-permute-start.9 = (bf16[384,128]{1,0:T(8,128)(2,1)S(1)}, bf16[384,128]{1,0:T(8,128)(2,1)S(1)}, u32[]{:S(2)}, u32[]{:S(2)}) collective-permute-start(bf16[384,128]{1,0:T(8,128)(2,1)S(1)} %add_convert_fusion.2), channel_id=1, source_target_pairs={{0,4},{1,5},{2,6},{3,7},{4,0},{5,1},{6,2},{7,3},{8,12},{9,13},{10,... | collective-permute-start | bytes 294920 | tf_op jit(solution)/shard_map/ppermute | solution.py:241
  33.0 1.3 %new_pair.1 = bf16[4,64,128]{2,1,0:T(8,128)(2,1)} custom-call(s32[2]{0:T(128)S(1)} %pad_add_fusion.place, bf16[4,64,128]{2,1,0:T(8,128)(2,1)S(1)} %bitcast.28, bf16[4,64,128]{2,1,0:T(8,128)(2,1)S(1)} %maximum_bitcast_fusion.1.y_ref), custom_call_target="tpu_custom_call" | custom-call | flops 500000000 | tf_op jit(solution)/shard_map/new_pair/pallas_call | solution.py:314
  34.4 2.0 %collective-permute-done.9 = bf16[384,128]{1,0:T(8,128)(2,1)S(1)} collective-permute-done((bf16[384,128]{1,0:T(8,128)(2,1)S(1)}, bf16[384,128]{1,0:T(8,128)(2,1)S(1)}, u32[]{:S(2)}, u32[]{:S(2)}) %collective-permute-start.9) | collective-permute-done | bytes 98336 | tf_op jit(solution)/shard_map/ppermute | solution.py:241
  36.4 2.2 %collective-permute-start.10 = (bf16[384,128]{1,0:T(8,128)(2,1)S(1)}, bf16[384,128]{1,0:T(8,128)(2,1)S(1)}, u32[]{:S(2)}, u32[]{:S(2)}) collective-permute-start(bf16[384,128]{1,0:T(8,128)(2,1)S(1)} %add_convert_fusion.1), channel_id=1, source_target_pairs={{0,8},{1,9},{2,10},{3,11},{4,12},{5,13},{6,14},{7,15},{8,0},{9,1},... | collective-permute-start | bytes 294920 | tf_op jit(solution)/shard_map/ppermute | solution.py:241
  38.7 4.4 %collective-permute-done.10 = bf16[384,128]{1,0:T(8,128)(2,1)S(1)} collective-permute-done((bf16[384,128]{1,0:T(8,128)(2,1)S(1)}, bf16[384,128]{1,0:T(8,128)(2,1)S(1)}, u32[]{:S(2)}, u32[]{:S(2)}) %collective-permute-start.10) | collective-permute-done | bytes 98336 | tf_op jit(solution)/shard_map/ppermute | solution.py:241
  43.1 0.1 collective-permute-start.11
  43.2 1.3 %collective-permute-done.11 = bf16[384,128]{1,0:T(8,128)(2,1)S(1)} collective-permute-done((bf16[384,128]{1,0:T(8,128)(2,1)S(1)}, bf16[384,128]{1,0:T(8,128)(2,1)S(1)}, u32[]{:S(2)}, u32[]{:S(2)}) %collective-permute-start.11) | collective-permute-done | bytes 98336 | tf_op jit(solution)/shard_map/ppermute | solution.py:233
  44.6 0.8 %concatenate.23 = f32[128,768]{1,0:T(8,128)} convert(bf16[128,768]{1,0:T(8,128)(2,1)S(1)} %slice_dynamic-update-slice_fusion) | non-fusion elementwise | flops 98304 | bytes 589824 | tf_op jit(solution)/shard_map/concatenate | solution.py:331
  (21 shorter events, 0.3 us)
Async XLA Ops:
  0.6 6.8 %copy-start.1 = (bf16[1,4,64,128]{3,2,1,0:T(8,128)(2,1)S(1)}, bf16[1,4,64,128]{3,2,1,0:T(8,128)(2,1)}, u32[]{:S(2)}) copy-start(bf16[1,4,64,128]{3,2,1,0:T(8,128)(2,1)} %param.4) | copy-start | bytes 196612
  0.6 10.0 %copy-start.2 = (s32[1,64]{1,0:T(1,128)S(1)}, s32[1,64]{1,0:T(1,128)}, u32[]{:S(2)}) copy-start(s32[1,64]{1,0:T(1,128)} %mask_s.5) | copy-start | bytes 772
  0.7 10.6 %copy-start = (bf16[128,768]{1,0:T(8,128)(2,1)S(1)}, bf16[128,768]{1,0:T(8,128)(2,1)}, u32[]{:S(2)}) copy-start(bf16[128,768]{1,0:T(8,128)(2,1)} %w_ref.5) | copy-start | bytes 589828
  0.7 10.0 %collective-permute-start.2 = (bf16[4,64,128]{2,1,0:T(8,128)(2,1)}, bf16[4,64,128]{2,1,0:T(8,128)(2,1)S(1)}, u32[]{:S(2)}, u32[]{:S(2)}) collective-permute-start(bf16[4,64,128]{2,1,0:T(8,128)(2,1)} %bitcast.21), channel_id=1, source_target_pairs={{0,12},{1,13},{2,14},{3,15},{4,8},{5,9},{6,10},{7,11},{8,4},{9,5},... | collective-permute-start | bytes 196616 | tf_op jit(solution)/shard_map/ppermute | solution.py:241
  5.8 6.6 %collective-permute-start.1 = (bf16[4,64,128]{2,1,0:T(8,128)(2,1)}, bf16[4,64,128]{2,1,0:T(8,128)(2,1)S(1)}, u32[]{:S(2)}, u32[]{:S(2)}) collective-permute-start(bf16[4,64,128]{2,1,0:T(8,128)(2,1)} %bitcast.22), channel_id=1, source_target_pairs={{0,8},{1,9},{2,10},{3,11},{4,12},{5,13},{6,14},{7,15},{8,0},{9,1},... | collective-permute-start | bytes 196616 | tf_op jit(solution)/shard_map/ppermute | solution.py:241
  5.8 6.6 %collective-permute-start = (bf16[4,64,128]{2,1,0:T(8,128)(2,1)}, bf16[4,64,128]{2,1,0:T(8,128)(2,1)S(1)}, u32[]{:S(2)}, u32[]{:S(2)}) collective-permute-start(bf16[4,64,128]{2,1,0:T(8,128)(2,1)} %bitcast.23), channel_id=1, source_target_pairs={{0,4},{1,5},{2,6},{3,7},{4,0},{5,1},{6,2},{7,3},{8,12},{9,13},{10,... | collective-permute-start | bytes 196616 | tf_op jit(solution)/shard_map/ppermute | solution.py:241
  7.5 6.7 %collective-permute-start.5 = (bf16[4,64,128]{2,1,0:T(8,128)(2,1)S(1)}, bf16[4,64,128]{2,1,0:T(8,128)(2,1)S(1)}, u32[]{:S(2)}, u32[]{:S(2)}) collective-permute-start(bf16[4,64,128]{2,1,0:T(8,128)(2,1)S(1)} %bitcast.24), channel_id=1, source_target_pairs={{0,3},{1,2},{2,1},{3,0},{4,7},{5,6},{6,5},{7,4},{8,11},{9,10},{10,... | collective-permute-start | bytes 196616 | tf_op jit(solution)/shard_map/ppermute | solution.py:241
  10.1 4.3 %collective-permute-start.4 = (bf16[4,64,128]{2,1,0:T(8,128)(2,1)S(1)}, bf16[4,64,128]{2,1,0:T(8,128)(2,1)S(1)}, u32[]{:S(2)}, u32[]{:S(2)}) collective-permute-start(bf16[4,64,128]{2,1,0:T(8,128)(2,1)S(1)} %bitcast.25), channel_id=1, source_target_pairs={{0,2},{1,3},{2,0},{3,1},{4,6},{5,7},{6,4},{7,5},{8,10},{9,11},{10,... | collective-permute-start | bytes 196616 | tf_op jit(solution)/shard_map/ppermute | solution.py:241
  10.7 4.3 %collective-permute-start.3 = (bf16[4,64,128]{2,1,0:T(8,128)(2,1)S(1)}, bf16[4,64,128]{2,1,0:T(8,128)(2,1)S(1)}, u32[]{:S(2)}, u32[]{:S(2)}) collective-permute-start(bf16[4,64,128]{2,1,0:T(8,128)(2,1)S(1)} %bitcast.26), channel_id=1, source_target_pairs={{0,1},{1,0},{2,3},{3,2},{4,5},{5,4},{6,7},{7,6},{8,9},{9,8},{10,11... | collective-permute-start | bytes 196616 | tf_op jit(solution)/shard_map/ppermute | solution.py:241
  20.1 1.4 %collective-permute-start.6 = (bf16[384,128]{1,0:T(8,128)(2,1)S(1)}, bf16[384,128]{1,0:T(8,128)(2,1)S(1)}, u32[]{:S(2)}, u32[]{:S(2)}) collective-permute-start(bf16[384,128]{1,0:T(8,128)(2,1)S(1)} %get-tuple-element.50), channel_id=1, source_target_pairs={{0,16},{16,0},{1,17},{17,1},{2,18},{18,2},{3,19},{19,3},{4,20},{20... | collective-permute-start | bytes 294920 | tf_op jit(solution)/shard_map/ppermute | solution.py:233
  21.5 5.0 %collective-permute-start.7 = (bf16[512,128]{1,0:T(8,128)(2,1)S(1)}, bf16[512,128]{1,0:T(8,128)(2,1)S(1)}, u32[]{:S(2)}, u32[]{:S(2)}) collective-permute-start(bf16[512,128]{1,0:T(8,128)(2,1)S(1)} %pad_maximum_fusion), channel_id=1, source_target_pairs={{0,1},{1,0},{2,3},{3,2},{4,5},{5,4},{6,7},{7,6},{8,9},{9,8},{10,11... | collective-permute-start | bytes 393224 | tf_op jit(solution)/shard_map/ppermute | solution.py:241
  26.7 5.0 %collective-permute-start.8 = (bf16[512,128]{1,0:T(8,128)(2,1)S(1)}, bf16[512,128]{1,0:T(8,128)(2,1)S(1)}, u32[]{:S(2)}, u32[]{:S(2)}) collective-permute-start(bf16[512,128]{1,0:T(8,128)(2,1)S(1)} %pad_maximum_fusion.1), channel_id=1, source_target_pairs={{0,2},{1,3},{2,0},{3,1},{4,6},{5,7},{6,4},{7,5},{8,10},{9,11},{10,... | collective-permute-start | bytes 393224 | tf_op jit(solution)/shard_map/ppermute | solution.py:241
  31.7 4.7 %collective-permute-start.9 = (bf16[384,128]{1,0:T(8,128)(2,1)S(1)}, bf16[384,128]{1,0:T(8,128)(2,1)S(1)}, u32[]{:S(2)}, u32[]{:S(2)}) collective-permute-start(bf16[384,128]{1,0:T(8,128)(2,1)S(1)} %add_convert_fusion.2), channel_id=1, source_target_pairs={{0,4},{1,5},{2,6},{3,7},{4,0},{5,1},{6,2},{7,3},{8,12},{9,13},{10,... | collective-permute-start | bytes 294920 | tf_op jit(solution)/shard_map/ppermute | solution.py:241
  36.4 6.6 %collective-permute-start.10 = (bf16[384,128]{1,0:T(8,128)(2,1)S(1)}, bf16[384,128]{1,0:T(8,128)(2,1)S(1)}, u32[]{:S(2)}, u32[]{:S(2)}) collective-permute-start(bf16[384,128]{1,0:T(8,128)(2,1)S(1)} %add_convert_fusion.1), channel_id=1, source_target_pairs={{0,8},{1,9},{2,10},{3,11},{4,12},{5,13},{6,14},{7,15},{8,0},{9,1},... | collective-permute-start | bytes 294920 | tf_op jit(solution)/shard_map/ppermute | solution.py:241
  43.1 1.4 %collective-permute-start.11 = (bf16[384,128]{1,0:T(8,128)(2,1)S(1)}, bf16[384,128]{1,0:T(8,128)(2,1)S(1)}, u32[]{:S(2)}, u32[]{:S(2)}) collective-permute-start(bf16[384,128]{1,0:T(8,128)(2,1)S(1)} %add_convert_fusion), channel_id=1, source_target_pairs={{0,16},{16,0},{1,17},{17,1},{2,18},{18,2},{3,19},{19,3},{4,20},{20... | collective-permute-start | bytes 294920 | tf_op jit(solution)/shard_map/ppermute | solution.py:233

commit v4 on v3

--- a/solution.py
+++ b/solution.py
@@ -86,9 +86,9 @@
         gate_s[here, :] = gate.astype(gate_s.dtype)
 
 
-def own_kernel(cfg, place, mask_s, mask_v, w_ref, v_ref, own_ref, *outs):
+def own_kernel(cfg, place, mask_s, mask_v, w_ref, v_ref, own_ref, far_ref, *outs):
     g1, chans = cfg[0], cfg[4]
-    fill_side(cfg, place, mask_s, mask_v, w_ref, v_ref, [(0, own_ref)], 1, 0, outs[:6])
+    fill_side(cfg, place, mask_s, mask_v, w_ref, v_ref, [(0, own_ref), (g1 - 1, far_ref)], 1, 0, outs[:6])
     fill_side(cfg, place, mask_s, mask_v, w_ref, v_ref, [(0, own_ref)], g1, 2 * chans, outs[6:])
 
 
@@ -110,7 +110,7 @@
             pt_s[to, :] = fold(ta * b + a * tb)
         return carry
 
-    lax.fori_loop(0, count, tri, 0, unroll=2 if width <= 64 else 1)
+    lax.fori_loop(0, count, tri, 0, unroll=4 if width <= 64 else 1)
     pairs = count * n_j
     here = slice(first * n_j, (first + count) * n_j)
     for part, out in ((px_s, x_ref), (pt_s, tx_ref)):
@@ -128,14 +128,14 @@
 
 def block_kernel(cfg, place, mask_s, mask_v, w_ref, v_s, zj_s, b_s, tb_s, sb_s, gb_s, x_in, tx_in, *rest):
     g1, g2, rows, width, chans, total = cfg
-    refs = rest[: g1 - 1]
+    refs = rest[: g1 - 2]
     (keep_ref, send_ref, y_ref, zi_s, a_s, ta_s, sa_s, ga_s, zp_s,
-     px_s, pt_s, x_s, tx_s, xb_s, d_s, g_s) = rest[g1 + 5 :]
+     px_s, pt_s, x_s, tx_s, xb_s, d_s, g_s) = rest[g1 + 4 :]
     n_i, n_j = g1 * rows, g2 * rows
     blk = rows * width
     core = place[1]
     fill_side(cfg, place, mask_s, mask_v, w_ref, v_s,
-              [(m, refs[m - 1]) for m in range(g1 - 1, 0, -1)], 1, 0, (zi_s, a_s, ta_s, sa_s, ga_s, zp_s))
+              [(m, refs[m - 1]) for m in range(g1 - 2, 0, -1)], 1, 0, (zi_s, a_s, ta_s, sa_s, ga_s, zp_s))
     x_s[: rows * n_j, :] = x_in[...]
     tx_s[: rows * n_j, :] = tx_in[...]
     triangle(cfg, rows, n_i - rows, a_s, ta_s, b_s, tb_s, px_s, pt_s, x_s, tx_s)
@@ -143,7 +143,7 @@
 
     w_gate, w_out = w_ref[:, 4 * chans : 5 * chans], w_ref[:, 5 * chans :]
     v_gate, v_out = v_s[:, 4 * chans : 5 * chans], v_s[:, 5 * chans :]
-    step = min(pairs, 256)
+    step = min(pairs, 128)
     for at in range(0, pairs, step):
         here = slice(at, at + step)
         zp = zp_s[here, :]
@@ -255,16 +255,18 @@
     unit = 1.0 / np.sqrt(np.float32(chans))
     v = ((2 * probe_signs - 1).astype(F32) * unit).astype(BF)
     later, v = lax.optimization_barrier((own, v))
-    plane = [swap(later, m, 1) for m in range(1, g1)]
+    last, along[-1] = lax.optimization_barrier((later, along[-1]))
+    starts = [last] + [later] * (g1 - 3) + [own]
+    plane = [swap(starts[m - 1], m, 1) for m in range(1, g1)]
     sides = pl.pallas_call(
         functools.partial(own_kernel, cfg),
         out_shape=side_a + side_b,
-        in_specs=[SMEM, SMEM] + [VMEM] * 4,
+        in_specs=[SMEM, SMEM] + [VMEM] * 5,
         out_specs=[VMEM] * 11,
         compiler_params=params(),
         cost_estimate=cost(0.01),
         name="own_rows",
-    )(place, crop_mask, mask_v, weights, v, own)
+    )(place, crop_mask, mask_v, weights, v, own, plane[-1])
     own_pairs = shape((rows * n_j, chans), F32)
     part = pltpu.VMEM((rows * n_j * 8, chans), F32)
     *line, x, tx = pl.pallas_call(
@@ -282,9 +284,9 @@
     keep, send, y, *_ = pl.pallas_call(
         functools.partial(block_kernel, cfg),
         out_shape=[half, half, shape(pairs, BF)] + side_a,
-        in_specs=[SMEM, SMEM] + [VMEM] * (10 + g1 - 1 + 6),
+        in_specs=[SMEM, SMEM] + [VMEM] * (10 + g1 - 2 + 6),
         out_specs=[VMEM] * 9,
-        input_output_aliases={11 + g1 + i: 3 + i for i in range(6)},
+        input_output_aliases={10 + g1 + i: 3 + i for i in range(6)},
         scratch_shapes=[part, part]
         + [pltpu.VMEM(pairs, F32)] * 3
         + [pltpu.VMEM((max(n_i, n_j) * width, 2 * chans), BF)]
@@ -292,7 +294,7 @@
         compiler_params=params(),
         cost_estimate=cost(5.0),
         name="block",
-    )(place, crop_mask, mask_v, weights, v, *line, x, tx, *plane, *sides[:6])
+    )(place, crop_mask, mask_v, weights, v, *line, x, tx, *plane[:-1], *sides[:6])
 
     def plus(one, two):
         return (one.astype(F32) + two.astype(F32)).astype(BF)

time: 45.5 us -> 44.6 us (0.980)
  waiting for transfers between devices: 17.4 us -> 15.3 us
  starting transfers between devices: 15.6 us -> 16.7 us
    ppermute x10, waiting for transfers between devices: 14.9 us -> 12.7 us  [swap(): return lax.ppermute(value, ('crop', 'axial'), pairs)]
    ppermute x10, starting transfers between devices: 15.4 us -> 16.6 us  [swap(): return lax.ppermute(value, ('crop', 'axial'), pairs)]
  transfers between devices with their start and end apart: 12 -> 12, of which waited for: 8 -> 7; matrix products, arithmetic and copies ran while one was open for 3% -> 3% of each run, Pallas kernels for 9% -> 9%
where the time goes in v4:
time: 44.6 us; the launch traced here: 44.3 us
  starting transfers between devices  16.7 us (37%)
  waiting for transfers between devices  15.3 us (34%)
  Pallas kernels  9.15 us (21%)
  other arithmetic  2.11 us (5%)
  between operations  0.85 us (2%)
    ppermute x10, starting transfers between devices, swap(): return lax.ppermute(value, ('crop', 'axial'), pairs)  16.6 us
    ppermute x10, waiting for transfers between devices, swap(): return lax.ppermute(value, ('crop', 'axial'), pairs)  12.7 us
    pallas_call x1, Pallas kernels, shards(): pl.pallas_call(functools.partial(block_kernel, cfg), out_shape=[half, hal...  4.96 us
    ppermute x2, waiting for transfers between devices, crop_swap(): return lax.ppermute(value, 'crop', [(i, i ^ bit) for i in range(n_crop)])  2.56 us
    pallas_call x1, Pallas kernels, shards(): pl.pallas_call(functools.partial(line_kernel, cfg), out_shape=side_b + [o...  1.68 us
    pallas_call x1, Pallas kernels, shards(): pl.pallas_call(functools.partial(pair_kernel, cfg), out_shape=shape(own.s...  1.32 us
    pallas_call x1, Pallas kernels, shards(): pl.pallas_call(functools.partial(own_kernel, cfg), out_shape=side_a + sid...  1.19 us
    convert_element_type x1, other arithmetic, shards(): v = ((2 * probe_signs - 1).astype(F32) * unit).astype(BF)  1.05 us
  transfers between devices with their start and end apart: 12, of which 7 were waited for; matrix products, arithmetic and copies ran while one was open for 3% of the time, Pallas kernels for 9%

profile of v4, /device:TPU:0, one launch (start us, length us, event | category | flops | bytes accessed | tf_op | source)
XLA Modules:
  0.0 44.3 jit_solution(1040222432892001532)
XLA Ops:
  0.6 0.0 copy-start.1
  0.6 0.0 copy-start.2
  0.7 0.0 copy-start
  0.7 5.1 %collective-permute-start.3 = (bf16[4,64,128]{2,1,0:T(8,128)(2,1)}, bf16[4,64,128]{2,1,0:T(8,128)(2,1)S(1)}, u32[]{:S(2)}, u32[]{:S(2)}) collective-permute-start(bf16[4,64,128]{2,1,0:T(8,128)(2,1)} %bitcast.21), channel_id=1, source_target_pairs={{0,12},{1,13},{2,14},{3,15},{4,8},{5,9},{6,10},{7,11},{8,4},{9,5},... | collective-permute-start | bytes 196616 | tf_op jit(solution)/shard_map/ppermute | solution.py:241
  5.8 0.0 collective-permute-start.2
  5.8 0.6 %collective-permute-start.1 = (bf16[4,64,128]{2,1,0:T(8,128)(2,1)}, bf16[4,64,128]{2,1,0:T(8,128)(2,1)S(1)}, u32[]{:S(2)}, u32[]{:S(2)}) collective-permute-start(bf16[4,64,128]{2,1,0:T(8,128)(2,1)} %bitcast.23), channel_id=1, source_target_pairs={{0,4},{1,5},{2,6},{3,7},{4,0},{5,1},{6,2},{7,3},{8,12},{9,13},{10,... | collective-permute-start | bytes 196616 | tf_op jit(solution)/shard_map/ppermute | solution.py:241
  6.4 2.6 %collective-permute-start = (bf16[4,64,128]{2,1,0:T(8,128)(2,1)}, bf16[4,64,128]{2,1,0:T(8,128)(2,1)S(1)}, u32[]{:S(2)}, u32[]{:S(2)}) collective-permute-start(bf16[4,64,128]{2,1,0:T(8,128)(2,1)} %bitcast.24), channel_id=1, source_target_pairs={{0,3},{1,2},{2,1},{3,0},{4,7},{5,6},{6,5},{7,4},{8,11},{9,10},{10,... | collective-permute-start | bytes 196616 | tf_op jit(solution)/shard_map/ppermute | solution.py:241
  9.0 1.1 %multiply_convert_fusion.v_ref.v_s = bf16[128,768]{1,0:T(8,128)(2,1)S(1)} fusion(s32[128,768]{1,0:T(8,128)} %param.7), kind=kLoop, calls=%fused_computation | loop fusion | flops 491520 | bytes 589824 | tf_op jit(solution)/shard_map/convert_element_type | solution.py:256
  10.1 0.0 copy-done.1
  10.1 0.6 %collective-permute-start.5 = (bf16[4,64,128]{2,1,0:T(8,128)(2,1)S(1)}, bf16[4,64,128]{2,1,0:T(8,128)(2,1)S(1)}, u32[]{:S(2)}, u32[]{:S(2)}) collective-permute-start(bf16[4,64,128]{2,1,0:T(8,128)(2,1)S(1)} %bitcast.25), channel_id=1, source_target_pairs={{0,2},{1,3},{2,0},{3,1},{4,6},{5,7},{6,4},{7,5},{8,10},{9,11},{10,... | collective-permute-start | bytes 196616 | tf_op jit(solution)/shard_map/ppermute | solution.py:241
  10.6 0.0 copy-done.2
  10.7 0.0 collective-permute-done.3.rest_2_
  10.7 0.5 %collective-permute-start.4 = (bf16[4,64,128]{2,1,0:T(8,128)(2,1)S(1)}, bf16[4,64,128]{2,1,0:T(8,128)(2,1)S(1)}, u32[]{:S(2)}, u32[]{:S(2)}) collective-permute-start(bf16[4,64,128]{2,1,0:T(8,128)(2,1)S(1)} %bitcast.26), channel_id=1, source_target_pairs={{0,1},{1,0},{2,3},{3,2},{4,5},{5,4},{6,7},{7,6},{8,9},{9,8},{10,11... | collective-permute-start | bytes 196616 | tf_op jit(solution)/shard_map/ppermute | solution.py:241
  11.1 0.1 pad_add_fusion.place
  11.2 0.9 %collective-permute-done.far_ref = bf16[4,64,128]{2,1,0:T(8,128)(2,1)S(1)} collective-permute-done((bf16[4,64,128]{2,1,0:T(8,128)(2,1)}, bf16[4,64,128]{2,1,0:T(8,128)(2,1)S(1)}, u32[]{:S(2)}, u32[]{:S(2)}) %collective-permute-start) | collective-permute-done | bytes 65568 | tf_op jit(solution)/shard_map/ppermute | solution.py:241
  12.1 0.1 broadcast_in_dim.4.mask_v
  12.2 0.0 copy-done
  12.2 1.2 %own_rows.1 = (bf16[128,1024]{1,0:T(8,128)(2,1)S(1)}, f32[1024,128]{1,0:T(8,128)S(1)}, f32[1024,128]{1,0:T(8,128)S(1)}, f32[1024,128]{1,0:T(8,128)S(1)}, f32[102...) custom-call(s32[2]{0:T(128)S(1)} %pad_add_fusion.place, ...), custom_call_target="tpu_custom_call" | custom-call | flops 10000000 | tf_op jit(solution)/shard_map/own_rows/pallas_call | solution.py:261
  13.4 0.0 collective-permute-done.2.rest_1_
  13.4 0.0 collective-permute-done.1.rest_0_
  13.4 1.7 %line.1 = (bf16[128,1024]{1,0:T(8,128)(2,1)S(1)}, f32[1024,128]{1,0:T(8,128)S(1)}, f32[1024,128]{1,0:T(8,128)S(1)}, f32[1024,128]{1,0:T(8,128)S(1)}, f32[1024,12...) custom-call(s32[2]{0:T(128)S(1)} %pad_add_fusion.place, ...), custom_call_target="tpu_custom_call", output_to_operand_aliasing={{0}: (10, {}), {1}: (11, {}), {2}: (12, {}), {3}: (13, {}),... | custom-call | flops 10000000 | tf_op jit(solution)/shard_map/line/pallas_call | solution.py:272
  15.1 0.0 collective-permute-done.5.rest_1_
  15.1 0.0 collective-permute-done.4.rest_0_
  15.1 5.0 %block.1 = (bf16[384,128]{1,0:T(8,128)(2,1)S(1)}, bf16[384,128]{1,0:T(8,128)(2,1)S(1)}, bf16[256,128]{1,0:T(8,128)(2,1)S(1)}, bf16[128,1024]{1,0:T(8,128)(2,1)S(...) custom-call(s32[2]{0:T(128)S(1)} %pad_add_fusion.place, ...), custom_call_target="tpu_custom_call", output_to_operand_aliasing={{3}: (14, {}), {4}: (15, {}), {5}: (16, {}), {6}: (17, {}),... | custom-call | flops 5000000000 | tf_op jit(solution)/shard_map/block/pallas_call | solution.py:284
  20.1 0.1 collective-permute-start.6
  20.2 1.3 %collective-permute-done.6 = bf16[384,128]{1,0:T(8,128)(2,1)S(1)} collective-permute-done((bf16[384,128]{1,0:T(8,128)(2,1)S(1)}, bf16[384,128]{1,0:T(8,128)(2,1)S(1)}, u32[]{:S(2)}, u32[]{:S(2)}) %collective-permute-start.6) | collective-permute-done | bytes 98336 | tf_op jit(solution)/shard_map/ppermute | solution.py:233
  21.5 1.4 %collective-permute-start.7 = (bf16[512,128]{1,0:T(8,128)(2,1)S(1)}, bf16[512,128]{1,0:T(8,128)(2,1)S(1)}, u32[]{:S(2)}, u32[]{:S(2)}) collective-permute-start(bf16[512,128]{1,0:T(8,128)(2,1)S(1)} %pad_maximum_fusion), channel_id=1, source_target_pairs={{0,1},{1,0},{2,3},{3,2},{4,5},{5,4},{6,7},{7,6},{8,9},{9,8},{10,11... | collective-permute-start | bytes 393224 | tf_op jit(solution)/shard_map/ppermute | solution.py:241
  22.9 3.6 %collective-permute-done.7 = bf16[512,128]{1,0:T(8,128)(2,1)S(1)} collective-permute-done((bf16[512,128]{1,0:T(8,128)(2,1)S(1)}, bf16[512,128]{1,0:T(8,128)(2,1)S(1)}, u32[]{:S(2)}, u32[]{:S(2)}) %collective-permute-start.7) | collective-permute-done | bytes 131104 | tf_op jit(solution)/shard_map/ppermute | solution.py:241
  26.6 1.8 %collective-permute-start.8 = (bf16[512,128]{1,0:T(8,128)(2,1)S(1)}, bf16[512,128]{1,0:T(8,128)(2,1)S(1)}, u32[]{:S(2)}, u32[]{:S(2)}) collective-permute-start(bf16[512,128]{1,0:T(8,128)(2,1)S(1)} %pad_maximum_fusion.1), channel_id=1, source_target_pairs={{0,2},{1,3},{2,0},{3,1},{4,6},{5,7},{6,4},{7,5},{8,10},{9,11},{10,... | collective-permute-start | bytes 393224 | tf_op jit(solution)/shard_map/ppermute | solution.py:241
  28.4 3.2 %collective-permute-done.8 = bf16[512,128]{1,0:T(8,128)(2,1)S(1)} collective-permute-done((bf16[512,128]{1,0:T(8,128)(2,1)S(1)}, bf16[512,128]{1,0:T(8,128)(2,1)S(1)}, u32[]{:S(2)}, u32[]{:S(2)}) %collective-permute-start.8) | collective-permute-done | bytes 131104 | tf_op jit(solution)/shard_map/ppermute | solution.py:241
  31.7 1.4 %collective-permute-start.9 = (bf16[384,128]{1,0:T(8,128)(2,1)S(1)}, bf16[384,128]{1,0:T(8,128)(2,1)S(1)}, u32[]{:S(2)}, u32[]{:S(2)}) collective-permute-start(bf16[384,128]{1,0:T(8,128)(2,1)S(1)} %add_convert_fusion.2), channel_id=1, source_target_pairs={{0,4},{1,5},{2,6},{3,7},{4,0},{5,1},{6,2},{7,3},{8,12},{9,13},{10,... | collective-permute-start | bytes 294920 | tf_op jit(solution)/shard_map/ppermute | solution.py:241
  33.2 1.3 %new_pair.1 = bf16[4,64,128]{2,1,0:T(8,128)(2,1)} custom-call(s32[2]{0:T(128)S(1)} %pad_add_fusion.place, bf16[4,64,128]{2,1,0:T(8,128)(2,1)S(1)} %bitcast.28, bf16[4,64,128]{2,1,0:T(8,128)(2,1)S(1)} %maximum_bitcast_fusion.1.y_ref), custom_call_target="tpu_custom_call" | custom-call | flops 500000000 | tf_op jit(solution)/shard_map/new_pair/pallas_call | solution.py:316
  34.5 1.9 %collective-permute-done.9 = bf16[384,128]{1,0:T(8,128)(2,1)S(1)} collective-permute-done((bf16[384,128]{1,0:T(8,128)(2,1)S(1)}, bf16[384,128]{1,0:T(8,128)(2,1)S(1)}, u32[]{:S(2)}, u32[]{:S(2)}) %collective-permute-start.9) | collective-permute-done | bytes 98336 | tf_op jit(solution)/shard_map/ppermute | solution.py:241
  36.4 2.6 %collective-permute-start.10 = (bf16[384,128]{1,0:T(8,128)(2,1)S(1)}, bf16[384,128]{1,0:T(8,128)(2,1)S(1)}, u32[]{:S(2)}, u32[]{:S(2)}) collective-permute-start(bf16[384,128]{1,0:T(8,128)(2,1)S(1)} %add_convert_fusion.1), channel_id=1, source_target_pairs={{0,8},{1,9},{2,10},{3,11},{4,12},{5,13},{6,14},{7,15},{8,0},{9,1},... | collective-permute-start | bytes 294920 | tf_op jit(solution)/shard_map/ppermute | solution.py:241
  39.0 3.0 %collective-permute-done.10 = bf16[384,128]{1,0:T(8,128)(2,1)S(1)} collective-permute-done((bf16[384,128]{1,0:T(8,128)(2,1)S(1)}, bf16[384,128]{1,0:T(8,128)(2,1)S(1)}, u32[]{:S(2)}, u32[]{:S(2)}) %collective-permute-start.10) | collective-permute-done | bytes 98336 | tf_op jit(solution)/shard_map/ppermute | solution.py:241
  42.1 0.1 collective-permute-start.11
  42.1 1.3 %collective-permute-done.11 = bf16[384,128]{1,0:T(8,128)(2,1)S(1)} collective-permute-done((bf16[384,128]{1,0:T(8,128)(2,1)S(1)}, bf16[384,128]{1,0:T(8,128)(2,1)S(1)}, u32[]{:S(2)}, u32[]{:S(2)}) %collective-permute-start.11) | collective-permute-done | bytes 98336 | tf_op jit(solution)/shard_map/ppermute | solution.py:233
  43.5 0.8 %concatenate.23 = f32[128,768]{1,0:T(8,128)} convert(bf16[128,768]{1,0:T(8,128)(2,1)S(1)} %slice_dynamic-update-slice_fusion) | non-fusion elementwise | flops 98304 | bytes 589824 | tf_op jit(solution)/shard_map/concatenate | solution.py:333
  (21 shorter events, 0.3 us)
Async XLA Ops:
  0.6 9.4 %copy-start.1 = (bf16[1,4,64,128]{3,2,1,0:T(8,128)(2,1)S(1)}, bf16[1,4,64,128]{3,2,1,0:T(8,128)(2,1)}, u32[]{:S(2)}) copy-start(bf16[1,4,64,128]{3,2,1,0:T(8,128)(2,1)} %param.4) | copy-start | bytes 196612
  0.6 10.0 %copy-start.2 = (s32[1,64]{1,0:T(1,128)S(1)}, s32[1,64]{1,0:T(1,128)}, u32[]{:S(2)}) copy-start(s32[1,64]{1,0:T(1,128)} %mask_s.5) | copy-start | bytes 772
  0.7 11.6 %copy-start = (bf16[128,768]{1,0:T(8,128)(2,1)S(1)}, bf16[128,768]{1,0:T(8,128)(2,1)}, u32[]{:S(2)}) copy-start(bf16[128,768]{1,0:T(8,128)(2,1)} %w_ref.5) | copy-start | bytes 589828
  0.7 10.0 %collective-permute-start.3 = (bf16[4,64,128]{2,1,0:T(8,128)(2,1)}, bf16[4,64,128]{2,1,0:T(8,128)(2,1)S(1)}, u32[]{:S(2)}, u32[]{:S(2)}) collective-permute-start(bf16[4,64,128]{2,1,0:T(8,128)(2,1)} %bitcast.21), channel_id=1, source_target_pairs={{0,12},{1,13},{2,14},{3,15},{4,8},{5,9},{6,10},{7,11},{8,4},{9,5},... | collective-permute-start | bytes 196616 | tf_op jit(solution)/shard_map/ppermute | solution.py:241
  5.8 7.6 %collective-permute-start.2 = (bf16[4,64,128]{2,1,0:T(8,128)(2,1)}, bf16[4,64,128]{2,1,0:T(8,128)(2,1)S(1)}, u32[]{:S(2)}, u32[]{:S(2)}) collective-permute-start(bf16[4,64,128]{2,1,0:T(8,128)(2,1)} %bitcast.22), channel_id=1, source_target_pairs={{0,8},{1,9},{2,10},{3,11},{4,12},{5,13},{6,14},{7,15},{8,0},{9,1},... | collective-permute-start | bytes 196616 | tf_op jit(solution)/shard_map/ppermute | solution.py:241
  5.8 7.6 %collective-permute-start.1 = (bf16[4,64,128]{2,1,0:T(8,128)(2,1)}, bf16[4,64,128]{2,1,0:T(8,128)(2,1)S(1)}, u32[]{:S(2)}, u32[]{:S(2)}) collective-permute-start(bf16[4,64,128]{2,1,0:T(8,128)(2,1)} %bitcast.23), channel_id=1, source_target_pairs={{0,4},{1,5},{2,6},{3,7},{4,0},{5,1},{6,2},{7,3},{8,12},{9,13},{10,... | collective-permute-start | bytes 196616 | tf_op jit(solution)/shard_map/ppermute | solution.py:241
  6.4 5.7 %collective-permute-start = (bf16[4,64,128]{2,1,0:T(8,128)(2,1)}, bf16[4,64,128]{2,1,0:T(8,128)(2,1)S(1)}, u32[]{:S(2)}, u32[]{:S(2)}) collective-permute-start(bf16[4,64,128]{2,1,0:T(8,128)(2,1)} %bitcast.24), channel_id=1, source_target_pairs={{0,3},{1,2},{2,1},{3,0},{4,7},{5,6},{6,5},{7,4},{8,11},{9,10},{10,... | collective-permute-start | bytes 196616 | tf_op jit(solution)/shard_map/ppermute | solution.py:241
  10.1 5.0 %collective-permute-start.5 = (bf16[4,64,128]{2,1,0:T(8,128)(2,1)S(1)}, bf16[4,64,128]{2,1,0:T(8,128)(2,1)S(1)}, u32[]{:S(2)}, u32[]{:S(2)}) collective-permute-start(bf16[4,64,128]{2,1,0:T(8,128)(2,1)S(1)} %bitcast.25), channel_id=1, source_target_pairs={{0,2},{1,3},{2,0},{3,1},{4,6},{5,7},{6,4},{7,5},{8,10},{9,11},{10,... | collective-permute-start | bytes 196616 | tf_op jit(solution)/shard_map/ppermute | solution.py:241
  10.7 4.5 %collective-permute-start.4 = (bf16[4,64,128]{2,1,0:T(8,128)(2,1)S(1)}, bf16[4,64,128]{2,1,0:T(8,128)(2,1)S(1)}, u32[]{:S(2)}, u32[]{:S(2)}) collective-permute-start(bf16[4,64,128]{2,1,0:T(8,128)(2,1)S(1)} %bitcast.26), channel_id=1, source_target_pairs={{0,1},{1,0},{2,3},{3,2},{4,5},{5,4},{6,7},{7,6},{8,9},{9,8},{10,11... | collective-permute-start | bytes 196616 | tf_op jit(solution)/shard_map/ppermute | solution.py:241
  20.1 1.4 %collective-permute-start.6 = (bf16[384,128]{1,0:T(8,128)(2,1)S(1)}, bf16[384,128]{1,0:T(8,128)(2,1)S(1)}, u32[]{:S(2)}, u32[]{:S(2)}) collective-permute-start(bf16[384,128]{1,0:T(8,128)(2,1)S(1)} %get-tuple-element.54), channel_id=1, source_target_pairs={{0,16},{16,0},{1,17},{17,1},{2,18},{18,2},{3,19},{19,3},{4,20},{20... | collective-permute-start | bytes 294920 | tf_op jit(solution)/shard_map/ppermute | solution.py:233
  21.5 5.0 %collective-permute-start.7 = (bf16[512,128]{1,0:T(8,128)(2,1)S(1)}, bf16[512,128]{1,0:T(8,128)(2,1)S(1)}, u32[]{:S(2)}, u32[]{:S(2)}) collective-permute-start(bf16[512,128]{1,0:T(8,128)(2,1)S(1)} %pad_maximum_fusion), channel_id=1, source_target_pairs={{0,1},{1,0},{2,3},{3,2},{4,5},{5,4},{6,7},{7,6},{8,9},{9,8},{10,11... | collective-permute-start | bytes 393224 | tf_op jit(solution)/shard_map/ppermute | solution.py:241
  26.6 5.0 %collective-permute-start.8 = (bf16[512,128]{1,0:T(8,128)(2,1)S(1)}, bf16[512,128]{1,0:T(8,128)(2,1)S(1)}, u32[]{:S(2)}, u32[]{:S(2)}) collective-permute-start(bf16[512,128]{1,0:T(8,128)(2,1)S(1)} %pad_maximum_fusion.1), channel_id=1, source_target_pairs={{0,2},{1,3},{2,0},{3,1},{4,6},{5,7},{6,4},{7,5},{8,10},{9,11},{10,... | collective-permute-start | bytes 393224 | tf_op jit(solution)/shard_map/ppermute | solution.py:241
  31.7 4.7 %collective-permute-start.9 = (bf16[384,128]{1,0:T(8,128)(2,1)S(1)}, bf16[384,128]{1,0:T(8,128)(2,1)S(1)}, u32[]{:S(2)}, u32[]{:S(2)}) collective-permute-start(bf16[384,128]{1,0:T(8,128)(2,1)S(1)} %add_convert_fusion.2), channel_id=1, source_target_pairs={{0,4},{1,5},{2,6},{3,7},{4,0},{5,1},{6,2},{7,3},{8,12},{9,13},{10,... | collective-permute-start | bytes 294920 | tf_op jit(solution)/shard_map/ppermute | solution.py:241
  36.4 5.6 %collective-permute-start.10 = (bf16[384,128]{1,0:T(8,128)(2,1)S(1)}, bf16[384,128]{1,0:T(8,128)(2,1)S(1)}, u32[]{:S(2)}, u32[]{:S(2)}) collective-permute-start(bf16[384,128]{1,0:T(8,128)(2,1)S(1)} %add_convert_fusion.1), channel_id=1, source_target_pairs={{0,8},{1,9},{2,10},{3,11},{4,12},{5,13},{6,14},{7,15},{8,0},{9,1},... | collective-permute-start | bytes 294920 | tf_op jit(solution)/shard_map/ppermute | solution.py:241
  42.1 1.4 %collective-permute-start.11 = (bf16[384,128]{1,0:T(8,128)(2,1)S(1)}, bf16[384,128]{1,0:T(8,128)(2,1)S(1)}, u32[]{:S(2)}, u32[]{:S(2)}) collective-permute-start(bf16[384,128]{1,0:T(8,128)(2,1)S(1)} %add_convert_fusion), channel_id=1, source_target_pairs={{0,16},{16,0},{1,17},{17,1},{2,18},{18,2},{3,19},{19,3},{4,20},{20... | collective-permute-start | bytes 294920 | tf_op jit(solution)/shard_map/ppermute | solution.py:233

commit v5 on v4

--- a/solution.py
+++ b/solution.py
@@ -268,7 +268,7 @@
         name="own_rows",
     )(place, crop_mask, mask_v, weights, v, own, plane[-1])
     own_pairs = shape((rows * n_j, chans), F32)
-    part = pltpu.VMEM((rows * n_j * 8, chans), F32)
+    part = pltpu.VMEM((rows * n_j * 8 + 8, chans), F32)
     *line, x, tx = pl.pallas_call(
         functools.partial(line_kernel, cfg),
         out_shape=side_b + [own_pairs, own_pairs],
@@ -280,7 +280,7 @@
         cost_estimate=cost(0.01),
         name="line",
     )(place, crop_mask, mask_v, weights, v, sides[1], sides[2], *along, *sides[6:])
-    part = pltpu.VMEM(((n_i - rows) * n_j * 8, chans), F32)
+    part = pltpu.VMEM(((n_i - rows) * n_j * 8 + 8, chans), F32)
     keep, send, y, *_ = pl.pallas_call(
         functools.partial(block_kernel, cfg),
         out_shape=[half, half, shape(pairs, BF)] + side_a,

time: 44.6 us -> 44.5 us (level)
  no operation moved by 1% of the time
where the time goes in v5:
time: 44.5 us; the launch traced here: 44.3 us
  starting transfers between devices  16.7 us (38%)
  waiting for transfers between devices  15.3 us (34%)
  Pallas kernels  9.1 us (20%)
  other arithmetic  2.11 us (5%)
  between operations  0.85 us (2%)
    ppermute x10, starting transfers between devices, swap(): return lax.ppermute(value, ('crop', 'axial'), pairs)  16.6 us
    ppermute x10, waiting for transfers between devices, swap(): return lax.ppermute(value, ('crop', 'axial'), pairs)  12.7 us
    pallas_call x1, Pallas kernels, shards(): pl.pallas_call(functools.partial(block_kernel, cfg), out_shape=[half, hal...  4.92 us
    ppermute x2, waiting for transfers between devices, crop_swap(): return lax.ppermute(value, 'crop', [(i, i ^ bit) for i in range(n_crop)])  2.56 us
    pallas_call x1, Pallas kernels, shards(): pl.pallas_call(functools.partial(line_kernel, cfg), out_shape=side_b + [o...  1.68 us
    pallas_call x1, Pallas kernels, shards(): pl.pallas_call(functools.partial(pair_kernel, cfg), out_shape=shape(own.s...  1.32 us
    pallas_call x1, Pallas kernels, shards(): pl.pallas_call(functools.partial(own_kernel, cfg), out_shape=side_a + sid...  1.19 us
    convert_element_type x1, other arithmetic, shards(): v = ((2 * probe_signs - 1).astype(F32) * unit).astype(BF)  1.05 us
  transfers between devices with their start and end apart: 12, of which 7 were waited for; matrix products, arithmetic and copies ran while one was open for 3% of the time, Pallas kernels for 9%

profile of v5, /device:TPU:0, one launch (start us, length us, event | category | flops | bytes accessed | tf_op | source)
XLA Modules:
  0.0 44.3 jit_solution(6876549514336080940)
XLA Ops:
  0.6 0.0 copy-start.1
  0.6 0.0 copy-start.2
  0.7 0.0 copy-start
  0.7 5.1 %collective-permute-start.3 = (bf16[4,64,128]{2,1,0:T(8,128)(2,1)}, bf16[4,64,128]{2,1,0:T(8,128)(2,1)S(1)}, u32[]{:S(2)}, u32[]{:S(2)}) collective-permute-start(bf16[4,64,128]{2,1,0:T(8,128)(2,1)} %bitcast.21), channel_id=1, source_target_pairs={{0,12},{1,13},{2,14},{3,15},{4,8},{5,9},{6,10},{7,11},{8,4},{9,5},... | collective-permute-start | bytes 196616 | tf_op jit(solution)/shard_map/ppermute | solution.py:241
  5.8 0.0 collective-permute-start.2
  5.8 0.6 %collective-permute-start.1 = (bf16[4,64,128]{2,1,0:T(8,128)(2,1)}, bf16[4,64,128]{2,1,0:T(8,128)(2,1)S(1)}, u32[]{:S(2)}, u32[]{:S(2)}) collective-permute-start(bf16[4,64,128]{2,1,0:T(8,128)(2,1)} %bitcast.23), channel_id=1, source_target_pairs={{0,4},{1,5},{2,6},{3,7},{4,0},{5,1},{6,2},{7,3},{8,12},{9,13},{10,... | collective-permute-start | bytes 196616 | tf_op jit(solution)/shard_map/ppermute | solution.py:241
  6.4 2.6 %collective-permute-start = (bf16[4,64,128]{2,1,0:T(8,128)(2,1)}, bf16[4,64,128]{2,1,0:T(8,128)(2,1)S(1)}, u32[]{:S(2)}, u32[]{:S(2)}) collective-permute-start(bf16[4,64,128]{2,1,0:T(8,128)(2,1)} %bitcast.24), channel_id=1, source_target_pairs={{0,3},{1,2},{2,1},{3,0},{4,7},{5,6},{6,5},{7,4},{8,11},{9,10},{10,... | collective-permute-start | bytes 196616 | tf_op jit(solution)/shard_map/ppermute | solution.py:241
  9.0 1.1 %multiply_convert_fusion.v_ref.v_s = bf16[128,768]{1,0:T(8,128)(2,1)S(1)} fusion(s32[128,768]{1,0:T(8,128)} %param.7), kind=kLoop, calls=%fused_computation | loop fusion | flops 491520 | bytes 589824 | tf_op jit(solution)/shard_map/convert_element_type | solution.py:256
  10.1 0.0 copy-done.1
  10.1 0.6 %collective-permute-start.5 = (bf16[4,64,128]{2,1,0:T(8,128)(2,1)S(1)}, bf16[4,64,128]{2,1,0:T(8,128)(2,1)S(1)}, u32[]{:S(2)}, u32[]{:S(2)}) collective-permute-start(bf16[4,64,128]{2,1,0:T(8,128)(2,1)S(1)} %bitcast.25), channel_id=1, source_target_pairs={{0,2},{1,3},{2,0},{3,1},{4,6},{5,7},{6,4},{7,5},{8,10},{9,11},{10,... | collective-permute-start | bytes 196616 | tf_op jit(solution)/shard_map/ppermute | solution.py:241
  10.6 0.0 copy-done.2
  10.7 0.0 collective-permute-done.3.rest_2_
  10.7 0.5 %collective-permute-start.4 = (bf16[4,64,128]{2,1,0:T(8,128)(2,1)S(1)}, bf16[4,64,128]{2,1,0:T(8,128)(2,1)S(1)}, u32[]{:S(2)}, u32[]{:S(2)}) collective-permute-start(bf16[4,64,128]{2,1,0:T(8,128)(2,1)S(1)} %bitcast.26), channel_id=1, source_target_pairs={{0,1},{1,0},{2,3},{3,2},{4,5},{5,4},{6,7},{7,6},{8,9},{9,8},{10,11... | collective-permute-start | bytes 196616 | tf_op jit(solution)/shard_map/ppermute | solution.py:241
  11.1 0.1 pad_add_fusion.place
  11.2 0.9 %collective-permute-done.far_ref = bf16[4,64,128]{2,1,0:T(8,128)(2,1)S(1)} collective-permute-done((bf16[4,64,128]{2,1,0:T(8,128)(2,1)}, bf16[4,64,128]{2,1,0:T(8,128)(2,1)S(1)}, u32[]{:S(2)}, u32[]{:S(2)}) %collective-permute-start) | collective-permute-done | bytes 65568 | tf_op jit(solution)/shard_map/ppermute | solution.py:241
  12.1 0.1 broadcast_in_dim.4.mask_v
  12.2 0.0 copy-done
  12.2 1.2 %own_rows.1 = (bf16[128,1024]{1,0:T(8,128)(2,1)S(1)}, f32[1024,128]{1,0:T(8,128)S(1)}, f32[1024,128]{1,0:T(8,128)S(1)}, f32[1024,128]{1,0:T(8,128)S(1)}, f32[102...) custom-call(s32[2]{0:T(128)S(1)} %pad_add_fusion.place, ...), custom_call_target="tpu_custom_call" | custom-call | flops 10000000 | tf_op jit(solution)/shard_map/own_rows/pallas_call | solution.py:261
  13.4 0.0 collective-permute-done.2.rest_1_
  13.4 0.0 collective-permute-done.1.rest_0_
  13.4 1.7 %line.1 = (bf16[128,1024]{1,0:T(8,128)(2,1)S(1)}, f32[1024,128]{1,0:T(8,128)S(1)}, f32[1024,128]{1,0:T(8,128)S(1)}, f32[1024,128]{1,0:T(8,128)S(1)}, f32[1024,12...) custom-call(s32[2]{0:T(128)S(1)} %pad_add_fusion.place, ...), custom_call_target="tpu_custom_call", output_to_operand_aliasing={{0}: (10, {}), {1}: (11, {}), {2}: (12, {}), {3}: (13, {}),... | custom-call | flops 10000000 | tf_op jit(solution)/shard_map/line/pallas_call | solution.py:272
  15.1 0.0 collective-permute-done.5.rest_1_
  15.1 0.0 collective-permute-done.4.rest_0_
  15.1 4.9 %block.1 = (bf16[384,128]{1,0:T(8,128)(2,1)S(1)}, bf16[384,128]{1,0:T(8,128)(2,1)S(1)}, bf16[256,128]{1,0:T(8,128)(2,1)S(1)}, bf16[128,1024]{1,0:T(8,128)(2,1)S(...) custom-call(s32[2]{0:T(128)S(1)} %pad_add_fusion.place, ...), custom_call_target="tpu_custom_call", output_to_operand_aliasing={{3}: (14, {}), {4}: (15, {}), {5}: (16, {}), {6}: (17, {}),... | custom-call | flops 5000000000 | tf_op jit(solution)/shard_map/block/pallas_call | solution.py:284
  20.1 0.1 collective-permute-start.6
  20.2 1.3 %collective-permute-done.6 = bf16[384,128]{1,0:T(8,128)(2,1)S(1)} collective-permute-done((bf16[384,128]{1,0:T(8,128)(2,1)S(1)}, bf16[384,128]{1,0:T(8,128)(2,1)S(1)}, u32[]{:S(2)}, u32[]{:S(2)}) %collective-permute-start.6) | collective-permute-done | bytes 98336 | tf_op jit(solution)/shard_map/ppermute | solution.py:233
  21.5 1.4 %collective-permute-start.7 = (bf16[512,128]{1,0:T(8,128)(2,1)S(1)}, bf16[512,128]{1,0:T(8,128)(2,1)S(1)}, u32[]{:S(2)}, u32[]{:S(2)}) collective-permute-start(bf16[512,128]{1,0:T(8,128)(2,1)S(1)} %pad_maximum_fusion), channel_id=1, source_target_pairs={{0,1},{1,0},{2,3},{3,2},{4,5},{5,4},{6,7},{7,6},{8,9},{9,8},{10,11... | collective-permute-start | bytes 393224 | tf_op jit(solution)/shard_map/ppermute | solution.py:241
  22.9 3.6 %collective-permute-done.7 = bf16[512,128]{1,0:T(8,128)(2,1)S(1)} collective-permute-done((bf16[512,128]{1,0:T(8,128)(2,1)S(1)}, bf16[512,128]{1,0:T(8,128)(2,1)S(1)}, u32[]{:S(2)}, u32[]{:S(2)}) %collective-permute-start.7) | collective-permute-done | bytes 131104 | tf_op jit(solution)/shard_map/ppermute | solution.py:241
  26.6 1.8 %collective-permute-start.8 = (bf16[512,128]{1,0:T(8,128)(2,1)S(1)}, bf16[512,128]{1,0:T(8,128)(2,1)S(1)}, u32[]{:S(2)}, u32[]{:S(2)}) collective-permute-start(bf16[512,128]{1,0:T(8,128)(2,1)S(1)} %pad_maximum_fusion.1), channel_id=1, source_target_pairs={{0,2},{1,3},{2,0},{3,1},{4,6},{5,7},{6,4},{7,5},{8,10},{9,11},{10,... | collective-permute-start | bytes 393224 | tf_op jit(solution)/shard_map/ppermute | solution.py:241
  28.4 3.2 %collective-permute-done.8 = bf16[512,128]{1,0:T(8,128)(2,1)S(1)} collective-permute-done((bf16[512,128]{1,0:T(8,128)(2,1)S(1)}, bf16[512,128]{1,0:T(8,128)(2,1)S(1)}, u32[]{:S(2)}, u32[]{:S(2)}) %collective-permute-start.8) | collective-permute-done | bytes 131104 | tf_op jit(solution)/shard_map/ppermute | solution.py:241
  31.7 1.5 %collective-permute-start.9 = (bf16[384,128]{1,0:T(8,128)(2,1)S(1)}, bf16[384,128]{1,0:T(8,128)(2,1)S(1)}, u32[]{:S(2)}, u32[]{:S(2)}) collective-permute-start(bf16[384,128]{1,0:T(8,128)(2,1)S(1)} %add_convert_fusion.2), channel_id=1, source_target_pairs={{0,4},{1,5},{2,6},{3,7},{4,0},{5,1},{6,2},{7,3},{8,12},{9,13},{10,... | collective-permute-start | bytes 294920 | tf_op jit(solution)/shard_map/ppermute | solution.py:241
  33.1 1.3 %new_pair.1 = bf16[4,64,128]{2,1,0:T(8,128)(2,1)} custom-call(s32[2]{0:T(128)S(1)} %pad_add_fusion.place, bf16[4,64,128]{2,1,0:T(8,128)(2,1)S(1)} %bitcast.28, bf16[4,64,128]{2,1,0:T(8,128)(2,1)S(1)} %maximum_bitcast_fusion.1.y_ref), custom_call_target="tpu_custom_call" | custom-call | flops 500000000 | tf_op jit(solution)/shard_map/new_pair/pallas_call | solution.py:316
  34.5 1.9 %collective-permute-done.9 = bf16[384,128]{1,0:T(8,128)(2,1)S(1)} collective-permute-done((bf16[384,128]{1,0:T(8,128)(2,1)S(1)}, bf16[384,128]{1,0:T(8,128)(2,1)S(1)}, u32[]{:S(2)}, u32[]{:S(2)}) %collective-permute-start.9) | collective-permute-done | bytes 98336 | tf_op jit(solution)/shard_map/ppermute | solution.py:241
  36.4 2.6 %collective-permute-start.10 = (bf16[384,128]{1,0:T(8,128)(2,1)S(1)}, bf16[384,128]{1,0:T(8,128)(2,1)S(1)}, u32[]{:S(2)}, u32[]{:S(2)}) collective-permute-start(bf16[384,128]{1,0:T(8,128)(2,1)S(1)} %add_convert_fusion.1), channel_id=1, source_target_pairs={{0,8},{1,9},{2,10},{3,11},{4,12},{5,13},{6,14},{7,15},{8,0},{9,1},... | collective-permute-start | bytes 294920 | tf_op jit(solution)/shard_map/ppermute | solution.py:241
  39.0 3.0 %collective-permute-done.10 = bf16[384,128]{1,0:T(8,128)(2,1)S(1)} collective-permute-done((bf16[384,128]{1,0:T(8,128)(2,1)S(1)}, bf16[384,128]{1,0:T(8,128)(2,1)S(1)}, u32[]{:S(2)}, u32[]{:S(2)}) %collective-permute-start.10) | collective-permute-done | bytes 98336 | tf_op jit(solution)/shard_map/ppermute | solution.py:241
  42.0 0.1 collective-permute-start.11
  42.1 1.3 %collective-permute-done.11 = bf16[384,128]{1,0:T(8,128)(2,1)S(1)} collective-permute-done((bf16[384,128]{1,0:T(8,128)(2,1)S(1)}, bf16[384,128]{1,0:T(8,128)(2,1)S(1)}, u32[]{:S(2)}, u32[]{:S(2)}) %collective-permute-start.11) | collective-permute-done | bytes 98336 | tf_op jit(solution)/shard_map/ppermute | solution.py:233
  43.5 0.8 %concatenate.23 = f32[128,768]{1,0:T(8,128)} convert(bf16[128,768]{1,0:T(8,128)(2,1)S(1)} %slice_dynamic-update-slice_fusion) | non-fusion elementwise | flops 98304 | bytes 589824 | tf_op jit(solution)/shard_map/concatenate | solution.py:333
  (21 shorter events, 0.3 us)
Async XLA Ops:
  0.6 9.4 %copy-start.1 = (bf16[1,4,64,128]{3,2,1,0:T(8,128)(2,1)S(1)}, bf16[1,4,64,128]{3,2,1,0:T(8,128)(2,1)}, u32[]{:S(2)}) copy-start(bf16[1,4,64,128]{3,2,1,0:T(8,128)(2,1)} %param.4) | copy-start | bytes 196612
  0.6 10.0 %copy-start.2 = (s32[1,64]{1,0:T(1,128)S(1)}, s32[1,64]{1,0:T(1,128)}, u32[]{:S(2)}) copy-start(s32[1,64]{1,0:T(1,128)} %mask_s.5) | copy-start | bytes 772
  0.7 11.6 %copy-start = (bf16[128,768]{1,0:T(8,128)(2,1)S(1)}, bf16[128,768]{1,0:T(8,128)(2,1)}, u32[]{:S(2)}) copy-start(bf16[128,768]{1,0:T(8,128)(2,1)} %w_ref.5) | copy-start | bytes 589828
  0.7 10.0 %collective-permute-start.3 = (bf16[4,64,128]{2,1,0:T(8,128)(2,1)}, bf16[4,64,128]{2,1,0:T(8,128)(2,1)S(1)}, u32[]{:S(2)}, u32[]{:S(2)}) collective-permute-start(bf16[4,64,128]{2,1,0:T(8,128)(2,1)} %bitcast.21), channel_id=1, source_target_pairs={{0,12},{1,13},{2,14},{3,15},{4,8},{5,9},{6,10},{7,11},{8,4},{9,5},... | collective-permute-start | bytes 196616 | tf_op jit(solution)/shard_map/ppermute | solution.py:241
  5.8 7.6 %collective-permute-start.2 = (bf16[4,64,128]{2,1,0:T(8,128)(2,1)}, bf16[4,64,128]{2,1,0:T(8,128)(2,1)S(1)}, u32[]{:S(2)}, u32[]{:S(2)}) collective-permute-start(bf16[4,64,128]{2,1,0:T(8,128)(2,1)} %bitcast.22), channel_id=1, source_target_pairs={{0,8},{1,9},{2,10},{3,11},{4,12},{5,13},{6,14},{7,15},{8,0},{9,1},... | collective-permute-start | bytes 196616 | tf_op jit(solution)/shard_map/ppermute | solution.py:241
  5.8 7.6 %collective-permute-start.1 = (bf16[4,64,128]{2,1,0:T(8,128)(2,1)}, bf16[4,64,128]{2,1,0:T(8,128)(2,1)S(1)}, u32[]{:S(2)}, u32[]{:S(2)}) collective-permute-start(bf16[4,64,128]{2,1,0:T(8,128)(2,1)} %bitcast.23), channel_id=1, source_target_pairs={{0,4},{1,5},{2,6},{3,7},{4,0},{5,1},{6,2},{7,3},{8,12},{9,13},{10,... | collective-permute-start | bytes 196616 | tf_op jit(solution)/shard_map/ppermute | solution.py:241
  6.4 5.7 %collective-permute-start = (bf16[4,64,128]{2,1,0:T(8,128)(2,1)}, bf16[4,64,128]{2,1,0:T(8,128)(2,1)S(1)}, u32[]{:S(2)}, u32[]{:S(2)}) collective-permute-start(bf16[4,64,128]{2,1,0:T(8,128)(2,1)} %bitcast.24), channel_id=1, source_target_pairs={{0,3},{1,2},{2,1},{3,0},{4,7},{5,6},{6,5},{7,4},{8,11},{9,10},{10,... | collective-permute-start | bytes 196616 | tf_op jit(solution)/shard_map/ppermute | solution.py:241
  10.1 5.0 %collective-permute-start.5 = (bf16[4,64,128]{2,1,0:T(8,128)(2,1)S(1)}, bf16[4,64,128]{2,1,0:T(8,128)(2,1)S(1)}, u32[]{:S(2)}, u32[]{:S(2)}) collective-permute-start(bf16[4,64,128]{2,1,0:T(8,128)(2,1)S(1)} %bitcast.25), channel_id=1, source_target_pairs={{0,2},{1,3},{2,0},{3,1},{4,6},{5,7},{6,4},{7,5},{8,10},{9,11},{10,... | collective-permute-start | bytes 196616 | tf_op jit(solution)/shard_map/ppermute | solution.py:241
  10.7 4.5 %collective-permute-start.4 = (bf16[4,64,128]{2,1,0:T(8,128)(2,1)S(1)}, bf16[4,64,128]{2,1,0:T(8,128)(2,1)S(1)}, u32[]{:S(2)}, u32[]{:S(2)}) collective-permute-start(bf16[4,64,128]{2,1,0:T(8,128)(2,1)S(1)} %bitcast.26), channel_id=1, source_target_pairs={{0,1},{1,0},{2,3},{3,2},{4,5},{5,4},{6,7},{7,6},{8,9},{9,8},{10,11... | collective-permute-start | bytes 196616 | tf_op jit(solution)/shard_map/ppermute | solution.py:241
  20.1 1.4 %collective-permute-start.6 = (bf16[384,128]{1,0:T(8,128)(2,1)S(1)}, bf16[384,128]{1,0:T(8,128)(2,1)S(1)}, u32[]{:S(2)}, u32[]{:S(2)}) collective-permute-start(bf16[384,128]{1,0:T(8,128)(2,1)S(1)} %get-tuple-element.54), channel_id=1, source_target_pairs={{0,16},{16,0},{1,17},{17,1},{2,18},{18,2},{3,19},{19,3},{4,20},{20... | collective-permute-start | bytes 294920 | tf_op jit(solution)/shard_map/ppermute | solution.py:233
  21.5 5.0 %collective-permute-start.7 = (bf16[512,128]{1,0:T(8,128)(2,1)S(1)}, bf16[512,128]{1,0:T(8,128)(2,1)S(1)}, u32[]{:S(2)}, u32[]{:S(2)}) collective-permute-start(bf16[512,128]{1,0:T(8,128)(2,1)S(1)} %pad_maximum_fusion), channel_id=1, source_target_pairs={{0,1},{1,0},{2,3},{3,2},{4,5},{5,4},{6,7},{7,6},{8,9},{9,8},{10,11... | collective-permute-start | bytes 393224 | tf_op jit(solution)/shard_map/ppermute | solution.py:241
  26.6 5.0 %collective-permute-start.8 = (bf16[512,128]{1,0:T(8,128)(2,1)S(1)}, bf16[512,128]{1,0:T(8,128)(2,1)S(1)}, u32[]{:S(2)}, u32[]{:S(2)}) collective-permute-start(bf16[512,128]{1,0:T(8,128)(2,1)S(1)} %pad_maximum_fusion.1), channel_id=1, source_target_pairs={{0,2},{1,3},{2,0},{3,1},{4,6},{5,7},{6,4},{7,5},{8,10},{9,11},{10,... | collective-permute-start | bytes 393224 | tf_op jit(solution)/shard_map/ppermute | solution.py:241
  31.7 4.7 %collective-permute-start.9 = (bf16[384,128]{1,0:T(8,128)(2,1)S(1)}, bf16[384,128]{1,0:T(8,128)(2,1)S(1)}, u32[]{:S(2)}, u32[]{:S(2)}) collective-permute-start(bf16[384,128]{1,0:T(8,128)(2,1)S(1)} %add_convert_fusion.2), channel_id=1, source_target_pairs={{0,4},{1,5},{2,6},{3,7},{4,0},{5,1},{6,2},{7,3},{8,12},{9,13},{10,... | collective-permute-start | bytes 294920 | tf_op jit(solution)/shard_map/ppermute | solution.py:241
  36.4 5.6 %collective-permute-start.10 = (bf16[384,128]{1,0:T(8,128)(2,1)S(1)}, bf16[384,128]{1,0:T(8,128)(2,1)S(1)}, u32[]{:S(2)}, u32[]{:S(2)}) collective-permute-start(bf16[384,128]{1,0:T(8,128)(2,1)S(1)} %add_convert_fusion.1), channel_id=1, source_target_pairs={{0,8},{1,9},{2,10},{3,11},{4,12},{5,13},{6,14},{7,15},{8,0},{9,1},... | collective-permute-start | bytes 294920 | tf_op jit(solution)/shard_map/ppermute | solution.py:241
  42.0 1.4 %collective-permute-start.11 = (bf16[384,128]{1,0:T(8,128)(2,1)S(1)}, bf16[384,128]{1,0:T(8,128)(2,1)S(1)}, u32[]{:S(2)}, u32[]{:S(2)}) collective-permute-start(bf16[384,128]{1,0:T(8,128)(2,1)S(1)} %add_convert_fusion), channel_id=1, source_target_pairs={{0,16},{16,0},{1,17},{17,1},{2,18},{18,2},{3,19},{19,3},{4,20},{20... | collective-permute-start | bytes 294920 | tf_op jit(solution)/shard_map/ppermute | solution.py:233

commit v6 on v5

--- a/solution.py
+++ b/solution.py
@@ -86,9 +86,9 @@
         gate_s[here, :] = gate.astype(gate_s.dtype)
 
 
-def own_kernel(cfg, place, mask_s, mask_v, w_ref, v_ref, own_ref, far_ref, *outs):
+def own_kernel(cfg, place, mask_s, mask_v, w_ref, v_ref, own_ref, *outs):
     g1, chans = cfg[0], cfg[4]
-    fill_side(cfg, place, mask_s, mask_v, w_ref, v_ref, [(0, own_ref), (g1 - 1, far_ref)], 1, 0, outs[:6])
+    fill_side(cfg, place, mask_s, mask_v, w_ref, v_ref, [(0, own_ref)], 1, 0, outs[:6])
     fill_side(cfg, place, mask_s, mask_v, w_ref, v_ref, [(0, own_ref)], g1, 2 * chans, outs[6:])
 
 
@@ -118,12 +118,13 @@
         out[here, :] = total.astype(BF).astype(F32)
 
 
-def line_kernel(cfg, place, mask_s, mask_v, w_ref, v_ref, a_s, ta_s, *rest):
+def line_kernel(cfg, place, mask_s, mask_v, w_ref, v_ref, *rest):
     g1, g2, rows, width, chans, _ = cfg
-    refs, (*outs, x_ref, tx_ref, px_s, pt_s) = rest[: g2 - 1], rest[g2 + 4 :]
+    refs, (*outs, x_ref, tx_ref, px_s, pt_s) = rest[:g2], rest[g2 + 11 :]
     fill_side(cfg, place, mask_s, mask_v, w_ref, v_ref,
-              [(m + 1, refs[m]) for m in range(g2 - 1)], g1, 2 * chans, outs)
-    triangle(cfg, 0, rows, a_s, ta_s, outs[1], outs[2], px_s, pt_s, x_ref, tx_ref)
+              [(m + 1, refs[m]) for m in range(g2 - 1)], g1, 2 * chans, outs[6:])
+    triangle(cfg, 0, rows, outs[1], outs[2], outs[7], outs[8], px_s, pt_s, x_ref, tx_ref)
+    fill_side(cfg, place, mask_s, mask_v, w_ref, v_ref, [(g1 - 1, refs[g2 - 1])], 1, 0, outs[:6])
 
 
 def block_kernel(cfg, place, mask_s, mask_v, w_ref, v_s, zj_s, b_s, tb_s, sb_s, gb_s, x_in, tx_in, *rest):
@@ -261,25 +262,25 @@
     sides = pl.pallas_call(
         functools.partial(own_kernel, cfg),
         out_shape=side_a + side_b,
-        in_specs=[SMEM, SMEM] + [VMEM] * 5,
+        in_specs=[SMEM, SMEM] + [VMEM] * 4,
         out_specs=[VMEM] * 11,
         compiler_params=params(),
         cost_estimate=cost(0.01),
         name="own_rows",
-    )(place, crop_mask, mask_v, weights, v, own, plane[-1])
+    )(place, crop_mask, mask_v, weights, v, own)
     own_pairs = shape((rows * n_j, chans), F32)
     part = pltpu.VMEM((rows * n_j * 8 + 8, chans), F32)
-    *line, x, tx = pl.pallas_call(
+    *sides, x, tx = pl.pallas_call(
         functools.partial(line_kernel, cfg),
-        out_shape=side_b + [own_pairs, own_pairs],
-        in_specs=[SMEM, SMEM] + [VMEM] * (5 + g2 - 1 + 5),
-        out_specs=[VMEM] * 7,
-        input_output_aliases={6 + g2 + i: i for i in range(5)},
+        out_shape=side_a + side_b + [own_pairs, own_pairs],
+        in_specs=[SMEM, SMEM] + [VMEM] * (3 + g2 + 11),
+        out_specs=[VMEM] * 13,
+        input_output_aliases={5 + g2 + i: i for i in range(11)},
         scratch_shapes=[part, part],
         compiler_params=params(),
         cost_estimate=cost(0.01),
         name="line",
-    )(place, crop_mask, mask_v, weights, v, sides[1], sides[2], *along, *sides[6:])
+    )(place, crop_mask, mask_v, weights, v, *along, plane[-1], *sides)
     part = pltpu.VMEM(((n_i - rows) * n_j * 8 + 8, chans), F32)
     keep, send, y, *_ = pl.pallas_call(
         functools.partial(block_kernel, cfg),
@@ -294,7 +295,7 @@
         compiler_params=params(),
         cost_estimate=cost(5.0),
         name="block",
-    )(place, crop_mask, mask_v, weights, v, *line, x, tx, *plane[:-1], *sides[:6])
+    )(place, crop_mask, mask_v, weights, v, *sides[6:], x, tx, *plane[:-1], *sides[:6])
 
     def plus(one, two):
         return (one.astype(F32) + two.astype(F32)).astype(BF)
@@ -324,7 +325,7 @@
     )(place, own, y[0])
     bit = 1
     while bit < g2:
-        g = plus(g, swap(g, bit, g1, False))
+        g = plus(g, swap(g, bit, g1))
         g, new_pair = lax.optimization_barrier((g, new_pair))
         bit *= 2
     other = crop_swap(g, 1)

time: 44.5 us -> 45.3 us (1.018)
  waiting for transfers between devices: 15.3 us -> 17.4 us
  starting transfers between devices: 16.7 us -> 15.6 us
    ppermute x10, waiting for transfers between devices: 12.7 us -> 14.8 us  [swap(): return lax.ppermute(value, ('crop', 'axial'), pairs)]
    ppermute x10, starting transfers between devices: 16.6 us -> 15.4 us  [swap(): return lax.ppermute(value, ('crop', 'axial'), pairs)]
  transfers between devices with their start and end apart: 12 -> 12, of which waited for: 7 -> 8; matrix products, arithmetic and copies ran while one was open for 3% -> 3% of each run, Pallas kernels for 9% -> 9%
where the time goes in v6:
time: 45.3 us; the launch traced here: 45.1 us
  waiting for transfers between devices  17.4 us (38%)
  starting transfers between devices  15.6 us (34%)
  Pallas kernels  9.05 us (20%)
  other arithmetic  2.11 us (5%)
  between operations  0.84 us (2%)
    ppermute x10, starting transfers between devices, swap(): return lax.ppermute(value, ('crop', 'axial'), pairs)  15.4 us
    ppermute x10, waiting for transfers between devices, swap(): return lax.ppermute(value, ('crop', 'axial'), pairs)  14.8 us
    pallas_call x1, Pallas kernels, shards(): pl.pallas_call(functools.partial(block_kernel, cfg), out_shape=[half, hal...  4.85 us
    ppermute x2, waiting for transfers between devices, crop_swap(): return lax.ppermute(value, 'crop', [(i, i ^ bit) for i in range(n_crop)])  2.56 us
    pallas_call x1, Pallas kernels, shards(): pl.pallas_call(functools.partial(line_kernel, cfg), out_shape=side_a + si...  1.81 us
    pallas_call x1, Pallas kernels, shards(): pl.pallas_call(functools.partial(pair_kernel, cfg), out_shape=shape(own.s...  1.32 us
    pallas_call x1, Pallas kernels, shards(): pl.pallas_call(functools.partial(own_kernel, cfg), out_shape=side_a + sid...  1.07 us
    convert_element_type x1, other arithmetic, shards(): v = ((2 * probe_signs - 1).astype(F32) * unit).astype(BF)  1.05 us
  transfers between devices with their start and end apart: 12, of which 8 were waited for; matrix products, arithmetic and copies ran while one was open for 3% of the time, Pallas kernels for 9%

profile of v6, /device:TPU:0, one launch (start us, length us, event | category | flops | bytes accessed | tf_op | source)
XLA Modules:
  0.0 45.1 jit_solution(3585775430850745620)
XLA Ops:
  0.6 0.0 copy-start.1
  0.6 0.0 copy-start.2
  0.7 0.0 copy-start
  0.7 5.1 %collective-permute-start.2 = (bf16[4,64,128]{2,1,0:T(8,128)(2,1)}, bf16[4,64,128]{2,1,0:T(8,128)(2,1)S(1)}, u32[]{:S(2)}, u32[]{:S(2)}) collective-permute-start(bf16[4,64,128]{2,1,0:T(8,128)(2,1)} %bitcast.21), channel_id=1, source_target_pairs={{0,12},{1,13},{2,14},{3,15},{4,8},{5,9},{6,10},{7,11},{8,4},{9,5},... | collective-permute-start | bytes 196616 | tf_op jit(solution)/shard_map/ppermute | solution.py:242
  5.8 0.0 collective-permute-start
  5.8 0.6 %collective-permute-start.1 = (bf16[4,64,128]{2,1,0:T(8,128)(2,1)}, bf16[4,64,128]{2,1,0:T(8,128)(2,1)S(1)}, u32[]{:S(2)}, u32[]{:S(2)}) collective-permute-start(bf16[4,64,128]{2,1,0:T(8,128)(2,1)} %bitcast.23), channel_id=1, source_target_pairs={{0,8},{1,9},{2,10},{3,11},{4,12},{5,13},{6,14},{7,15},{8,0},{9,1},... | collective-permute-start | bytes 196616 | tf_op jit(solution)/shard_map/ppermute | solution.py:242
  6.4 2.6 %collective-permute-start.3 = (bf16[4,64,128]{2,1,0:T(8,128)(2,1)}, bf16[4,64,128]{2,1,0:T(8,128)(2,1)S(1)}, u32[]{:S(2)}, u32[]{:S(2)}) collective-permute-start(bf16[4,64,128]{2,1,0:T(8,128)(2,1)} %bitcast.24), channel_id=1, source_target_pairs={{0,3},{1,2},{2,1},{3,0},{4,7},{5,6},{6,5},{7,4},{8,11},{9,10},{10,... | collective-permute-start | bytes 196616 | tf_op jit(solution)/shard_map/ppermute | solution.py:242
  9.0 1.1 %multiply_convert_fusion.v_ref.v_s = bf16[128,768]{1,0:T(8,128)(2,1)S(1)} fusion(s32[128,768]{1,0:T(8,128)} %param.7), kind=kLoop, calls=%fused_computation | loop fusion | flops 491520 | bytes 589824 | tf_op jit(solution)/shard_map/convert_element_type | solution.py:257
  10.1 0.0 copy-done.1
  10.1 0.6 %collective-permute-start.5 = (bf16[4,64,128]{2,1,0:T(8,128)(2,1)S(1)}, bf16[4,64,128]{2,1,0:T(8,128)(2,1)S(1)}, u32[]{:S(2)}, u32[]{:S(2)}) collective-permute-start(bf16[4,64,128]{2,1,0:T(8,128)(2,1)S(1)} %bitcast.25), channel_id=1, source_target_pairs={{0,2},{1,3},{2,0},{3,1},{4,6},{5,7},{6,4},{7,5},{8,10},{9,11},{10,... | collective-permute-start | bytes 196616 | tf_op jit(solution)/shard_map/ppermute | solution.py:242
  10.6 0.0 copy-done.2
  10.7 0.0 collective-permute-done.2.rest_2_
  10.7 0.5 %collective-permute-start.4 = (bf16[4,64,128]{2,1,0:T(8,128)(2,1)S(1)}, bf16[4,64,128]{2,1,0:T(8,128)(2,1)S(1)}, u32[]{:S(2)}, u32[]{:S(2)}) collective-permute-start(bf16[4,64,128]{2,1,0:T(8,128)(2,1)S(1)} %bitcast.26), channel_id=1, source_target_pairs={{0,1},{1,0},{2,3},{3,2},{4,5},{5,4},{6,7},{7,6},{8,9},{9,8},{10,11... | collective-permute-start | bytes 196616 | tf_op jit(solution)/shard_map/ppermute | solution.py:242
  11.1 0.1 pad_add_fusion.place
  11.2 0.1 broadcast_in_dim.4.mask_v
  11.3 0.0 copy-done
  11.3 1.1 %own_rows.1 = (bf16[128,1024]{1,0:T(8,128)(2,1)S(1)}, f32[1024,128]{1,0:T(8,128)S(1)}, f32[1024,128]{1,0:T(8,128)S(1)}, f32[1024,128]{1,0:T(8,128)S(1)}, f32[102...) custom-call(s32[2]{0:T(128)S(1)} %pad_add_fusion.place, ...), custom_call_target="tpu_custom_call" | custom-call | flops 10000000 | tf_op jit(solution)/shard_map/own_rows/pallas_call | solution.py:262
  12.3 0.0 collective-permute-done.rest_0_
  12.4 0.0 collective-permute-done.1.rest_1_
  12.4 0.0 collective-permute-done.3.rest_3_
  12.4 1.8 %line.1 = (bf16[128,1024]{1,0:T(8,128)(2,1)S(1)}, f32[1024,128]{1,0:T(8,128)S(1)}, f32[1024,128]{1,0:T(8,128)S(1)}, f32[1024,128]{1,0:T(8,128)S(1)}, f32[1024,12...) custom-call(s32[2]{0:T(128)S(1)} %pad_add_fusion.place, ...), custom_call_target="tpu_custom_call", output_to_operand_aliasing={{0}: (9, {}), {1}: (10, {}), {2}: (11, {}), {3}: (12, {}), ... | custom-call | flops 10000000 | tf_op jit(solution)/shard_map/line/pallas_call | solution.py:273
  14.2 0.2 collective-permute-done.5.rest_1_
  14.4 0.6 %collective-permute-done.4.rest_0_ = bf16[4,64,128]{2,1,0:T(8,128)(2,1)S(1)} collective-permute-done((bf16[4,64,128]{2,1,0:T(8,128)(2,1)S(1)}, bf16[4,64,128]{2,1,0:T(8,128)(2,1)S(1)}, u32[]{:S(2)}, u32[]{:S(2)}) %collective-permute-start.4) | collective-permute-done | bytes 65568 | tf_op jit(solution)/shard_map/ppermute | solution.py:242
  15.0 4.9 %block.1 = (bf16[384,128]{1,0:T(8,128)(2,1)S(1)}, bf16[384,128]{1,0:T(8,128)(2,1)S(1)}, bf16[256,128]{1,0:T(8,128)(2,1)S(1)}, bf16[128,1024]{1,0:T(8,128)(2,1)S(...) custom-call(s32[2]{0:T(128)S(1)} %pad_add_fusion.place, ...), custom_call_target="tpu_custom_call", output_to_operand_aliasing={{3}: (14, {}), {4}: (15, {}), {5}: (16, {}), {6}: (17, {}),... | custom-call | flops 5000000000 | tf_op jit(solution)/shard_map/block/pallas_call | solution.py:285
  19.9 0.1 collective-permute-start.6
  19.9 1.3 %collective-permute-done.6 = bf16[384,128]{1,0:T(8,128)(2,1)S(1)} collective-permute-done((bf16[384,128]{1,0:T(8,128)(2,1)S(1)}, bf16[384,128]{1,0:T(8,128)(2,1)S(1)}, u32[]{:S(2)}, u32[]{:S(2)}) %collective-permute-start.6) | collective-permute-done | bytes 98336 | tf_op jit(solution)/shard_map/ppermute | solution.py:234
  21.3 0.9 %collective-permute-start.7 = (bf16[512,128]{1,0:T(8,128)(2,1)S(1)}, bf16[512,128]{1,0:T(8,128)(2,1)S(1)}, u32[]{:S(2)}, u32[]{:S(2)}) collective-permute-start(bf16[512,128]{1,0:T(8,128)(2,1)S(1)} %pad_maximum_fusion), channel_id=1, source_target_pairs={{0,1},{1,0},{2,3},{3,2},{4,5},{5,4},{6,7},{7,6},{8,9},{9,8},{10,11... | collective-permute-start | bytes 393224 | tf_op jit(solution)/shard_map/ppermute | solution.py:242
  22.2 4.1 %collective-permute-done.7 = bf16[512,128]{1,0:T(8,128)(2,1)S(1)} collective-permute-done((bf16[512,128]{1,0:T(8,128)(2,1)S(1)}, bf16[512,128]{1,0:T(8,128)(2,1)S(1)}, u32[]{:S(2)}, u32[]{:S(2)}) %collective-permute-start.7) | collective-permute-done | bytes 131104 | tf_op jit(solution)/shard_map/ppermute | solution.py:242
  26.4 1.6 %collective-permute-start.8 = (bf16[512,128]{1,0:T(8,128)(2,1)S(1)}, bf16[512,128]{1,0:T(8,128)(2,1)S(1)}, u32[]{:S(2)}, u32[]{:S(2)}) collective-permute-start(bf16[512,128]{1,0:T(8,128)(2,1)S(1)} %pad_maximum_fusion.1), channel_id=1, source_target_pairs={{0,2},{1,3},{2,0},{3,1},{4,6},{5,7},{6,4},{7,5},{8,10},{9,11},{10,... | collective-permute-start | bytes 393224 | tf_op jit(solution)/shard_map/ppermute | solution.py:242
  28.0 3.4 %collective-permute-done.8 = bf16[512,128]{1,0:T(8,128)(2,1)S(1)} collective-permute-done((bf16[512,128]{1,0:T(8,128)(2,1)S(1)}, bf16[512,128]{1,0:T(8,128)(2,1)S(1)}, u32[]{:S(2)}, u32[]{:S(2)}) %collective-permute-start.8) | collective-permute-done | bytes 131104 | tf_op jit(solution)/shard_map/ppermute | solution.py:242
  31.5 1.3 %collective-permute-start.9 = (bf16[384,128]{1,0:T(8,128)(2,1)S(1)}, bf16[384,128]{1,0:T(8,128)(2,1)S(1)}, u32[]{:S(2)}, u32[]{:S(2)}) collective-permute-start(bf16[384,128]{1,0:T(8,128)(2,1)S(1)} %add_convert_fusion.2), channel_id=1, source_target_pairs={{0,4},{1,5},{2,6},{3,7},{4,0},{5,1},{6,2},{7,3},{8,12},{9,13},{10,... | collective-permute-start | bytes 294920 | tf_op jit(solution)/shard_map/ppermute | solution.py:242
  32.8 1.3 %new_pair.1 = bf16[4,64,128]{2,1,0:T(8,128)(2,1)} custom-call(s32[2]{0:T(128)S(1)} %pad_add_fusion.place, bf16[4,64,128]{2,1,0:T(8,128)(2,1)S(1)} %bitcast.28, bf16[4,64,128]{2,1,0:T(8,128)(2,1)S(1)} %maximum_bitcast_fusion.1.y_ref), custom_call_target="tpu_custom_call" | custom-call | flops 500000000 | tf_op jit(solution)/shard_map/new_pair/pallas_call | solution.py:317
  34.1 2.0 %collective-permute-done.9 = bf16[384,128]{1,0:T(8,128)(2,1)S(1)} collective-permute-done((bf16[384,128]{1,0:T(8,128)(2,1)S(1)}, bf16[384,128]{1,0:T(8,128)(2,1)S(1)}, u32[]{:S(2)}, u32[]{:S(2)}) %collective-permute-start.9) | collective-permute-done | bytes 98336 | tf_op jit(solution)/shard_map/ppermute | solution.py:242
  36.2 2.2 %collective-permute-start.10 = (bf16[384,128]{1,0:T(8,128)(2,1)S(1)}, bf16[384,128]{1,0:T(8,128)(2,1)S(1)}, u32[]{:S(2)}, u32[]{:S(2)}) collective-permute-start(bf16[384,128]{1,0:T(8,128)(2,1)S(1)} %add_convert_fusion.1), channel_id=1, source_target_pairs={{0,8},{1,9},{2,10},{3,11},{4,12},{5,13},{6,14},{7,15},{8,0},{9,1},... | collective-permute-start | bytes 294920 | tf_op jit(solution)/shard_map/ppermute | solution.py:242
  38.4 4.4 %collective-permute-done.10 = bf16[384,128]{1,0:T(8,128)(2,1)S(1)} collective-permute-done((bf16[384,128]{1,0:T(8,128)(2,1)S(1)}, bf16[384,128]{1,0:T(8,128)(2,1)S(1)}, u32[]{:S(2)}, u32[]{:S(2)}) %collective-permute-start.10) | collective-permute-done | bytes 98336 | tf_op jit(solution)/shard_map/ppermute | solution.py:242
  42.8 0.1 collective-permute-start.11
  42.9 1.3 %collective-permute-done.11 = bf16[384,128]{1,0:T(8,128)(2,1)S(1)} collective-permute-done((bf16[384,128]{1,0:T(8,128)(2,1)S(1)}, bf16[384,128]{1,0:T(8,128)(2,1)S(1)}, u32[]{:S(2)}, u32[]{:S(2)}) %collective-permute-start.11) | collective-permute-done | bytes 98336 | tf_op jit(solution)/shard_map/ppermute | solution.py:234
  44.3 0.8 %concatenate.23 = f32[128,768]{1,0:T(8,128)} convert(bf16[128,768]{1,0:T(8,128)(2,1)S(1)} %slice_dynamic-update-slice_fusion) | non-fusion elementwise | flops 98304 | bytes 589824 | tf_op jit(solution)/shard_map/concatenate | solution.py:334
  (21 shorter events, 0.3 us)
Async XLA Ops:
  0.6 9.4 %copy-start.1 = (bf16[1,4,64,128]{3,2,1,0:T(8,128)(2,1)S(1)}, bf16[1,4,64,128]{3,2,1,0:T(8,128)(2,1)}, u32[]{:S(2)}) copy-start(bf16[1,4,64,128]{3,2,1,0:T(8,128)(2,1)} %param.4) | copy-start | bytes 196612
  0.6 10.0 %copy-start.2 = (s32[1,64]{1,0:T(1,128)S(1)}, s32[1,64]{1,0:T(1,128)}, u32[]{:S(2)}) copy-start(s32[1,64]{1,0:T(1,128)} %mask_s.5) | copy-start | bytes 772
  0.7 10.6 %copy-start = (bf16[128,768]{1,0:T(8,128)(2,1)S(1)}, bf16[128,768]{1,0:T(8,128)(2,1)}, u32[]{:S(2)}) copy-start(bf16[128,768]{1,0:T(8,128)(2,1)} %w_ref.5) | copy-start | bytes 589828
  0.7 10.0 %collective-permute-start.2 = (bf16[4,64,128]{2,1,0:T(8,128)(2,1)}, bf16[4,64,128]{2,1,0:T(8,128)(2,1)S(1)}, u32[]{:S(2)}, u32[]{:S(2)}) collective-permute-start(bf16[4,64,128]{2,1,0:T(8,128)(2,1)} %bitcast.21), channel_id=1, source_target_pairs={{0,12},{1,13},{2,14},{3,15},{4,8},{5,9},{6,10},{7,11},{8,4},{9,5},... | collective-permute-start | bytes 196616 | tf_op jit(solution)/shard_map/ppermute | solution.py:242
  5.8 6.6 %collective-permute-start = (bf16[4,64,128]{2,1,0:T(8,128)(2,1)}, bf16[4,64,128]{2,1,0:T(8,128)(2,1)S(1)}, u32[]{:S(2)}, u32[]{:S(2)}) collective-permute-start(bf16[4,64,128]{2,1,0:T(8,128)(2,1)} %bitcast.22), channel_id=1, source_target_pairs={{0,4},{1,5},{2,6},{3,7},{4,0},{5,1},{6,2},{7,3},{8,12},{9,13},{10,... | collective-permute-start | bytes 196616 | tf_op jit(solution)/shard_map/ppermute | solution.py:242
  5.8 6.6 %collective-permute-start.1 = (bf16[4,64,128]{2,1,0:T(8,128)(2,1)}, bf16[4,64,128]{2,1,0:T(8,128)(2,1)S(1)}, u32[]{:S(2)}, u32[]{:S(2)}) collective-permute-start(bf16[4,64,128]{2,1,0:T(8,128)(2,1)} %bitcast.23), channel_id=1, source_target_pairs={{0,8},{1,9},{2,10},{3,11},{4,12},{5,13},{6,14},{7,15},{8,0},{9,1},... | collective-permute-start | bytes 196616 | tf_op jit(solution)/shard_map/ppermute | solution.py:242
  6.4 5.9 %collective-permute-start.3 = (bf16[4,64,128]{2,1,0:T(8,128)(2,1)}, bf16[4,64,128]{2,1,0:T(8,128)(2,1)S(1)}, u32[]{:S(2)}, u32[]{:S(2)}) collective-permute-start(bf16[4,64,128]{2,1,0:T(8,128)(2,1)} %bitcast.24), channel_id=1, source_target_pairs={{0,3},{1,2},{2,1},{3,0},{4,7},{5,6},{6,5},{7,4},{8,11},{9,10},{10,... | collective-permute-start | bytes 196616 | tf_op jit(solution)/shard_map/ppermute | solution.py:242
  10.1 4.3 %collective-permute-start.5 = (bf16[4,64,128]{2,1,0:T(8,128)(2,1)S(1)}, bf16[4,64,128]{2,1,0:T(8,128)(2,1)S(1)}, u32[]{:S(2)}, u32[]{:S(2)}) collective-permute-start(bf16[4,64,128]{2,1,0:T(8,128)(2,1)S(1)} %bitcast.25), channel_id=1, source_target_pairs={{0,2},{1,3},{2,0},{3,1},{4,6},{5,7},{6,4},{7,5},{8,10},{9,11},{10,... | collective-permute-start | bytes 196616 | tf_op jit(solution)/shard_map/ppermute | solution.py:242
  10.7 4.3 %collective-permute-start.4 = (bf16[4,64,128]{2,1,0:T(8,128)(2,1)S(1)}, bf16[4,64,128]{2,1,0:T(8,128)(2,1)S(1)}, u32[]{:S(2)}, u32[]{:S(2)}) collective-permute-start(bf16[4,64,128]{2,1,0:T(8,128)(2,1)S(1)} %bitcast.26), channel_id=1, source_target_pairs={{0,1},{1,0},{2,3},{3,2},{4,5},{5,4},{6,7},{7,6},{8,9},{9,8},{10,11... | collective-permute-start | bytes 196616 | tf_op jit(solution)/shard_map/ppermute | solution.py:242
  19.9 1.4 %collective-permute-start.6 = (bf16[384,128]{1,0:T(8,128)(2,1)S(1)}, bf16[384,128]{1,0:T(8,128)(2,1)S(1)}, u32[]{:S(2)}, u32[]{:S(2)}) collective-permute-start(bf16[384,128]{1,0:T(8,128)(2,1)S(1)} %get-tuple-element.66), channel_id=1, source_target_pairs={{0,16},{16,0},{1,17},{17,1},{2,18},{18,2},{3,19},{19,3},{4,20},{20... | collective-permute-start | bytes 294920 | tf_op jit(solution)/shard_map/ppermute | solution.py:234
  21.3 5.0 %collective-permute-start.7 = (bf16[512,128]{1,0:T(8,128)(2,1)S(1)}, bf16[512,128]{1,0:T(8,128)(2,1)S(1)}, u32[]{:S(2)}, u32[]{:S(2)}) collective-permute-start(bf16[512,128]{1,0:T(8,128)(2,1)S(1)} %pad_maximum_fusion), channel_id=1, source_target_pairs={{0,1},{1,0},{2,3},{3,2},{4,5},{5,4},{6,7},{7,6},{8,9},{9,8},{10,11... | collective-permute-start | bytes 393224 | tf_op jit(solution)/shard_map/ppermute | solution.py:242
  26.4 5.0 %collective-permute-start.8 = (bf16[512,128]{1,0:T(8,128)(2,1)S(1)}, bf16[512,128]{1,0:T(8,128)(2,1)S(1)}, u32[]{:S(2)}, u32[]{:S(2)}) collective-permute-start(bf16[512,128]{1,0:T(8,128)(2,1)S(1)} %pad_maximum_fusion.1), channel_id=1, source_target_pairs={{0,2},{1,3},{2,0},{3,1},{4,6},{5,7},{6,4},{7,5},{8,10},{9,11},{10,... | collective-permute-start | bytes 393224 | tf_op jit(solution)/shard_map/ppermute | solution.py:242
  31.5 4.7 %collective-permute-start.9 = (bf16[384,128]{1,0:T(8,128)(2,1)S(1)}, bf16[384,128]{1,0:T(8,128)(2,1)S(1)}, u32[]{:S(2)}, u32[]{:S(2)}) collective-permute-start(bf16[384,128]{1,0:T(8,128)(2,1)S(1)} %add_convert_fusion.2), channel_id=1, source_target_pairs={{0,4},{1,5},{2,6},{3,7},{4,0},{5,1},{6,2},{7,3},{8,12},{9,13},{10,... | collective-permute-start | bytes 294920 | tf_op jit(solution)/shard_map/ppermute | solution.py:242
  36.2 6.6 %collective-permute-start.10 = (bf16[384,128]{1,0:T(8,128)(2,1)S(1)}, bf16[384,128]{1,0:T(8,128)(2,1)S(1)}, u32[]{:S(2)}, u32[]{:S(2)}) collective-permute-start(bf16[384,128]{1,0:T(8,128)(2,1)S(1)} %add_convert_fusion.1), channel_id=1, source_target_pairs={{0,8},{1,9},{2,10},{3,11},{4,12},{5,13},{6,14},{7,15},{8,0},{9,1},... | collective-permute-start | bytes 294920 | tf_op jit(solution)/shard_map/ppermute | solution.py:242
  42.8 1.4 %collective-permute-start.11 = (bf16[384,128]{1,0:T(8,128)(2,1)S(1)}, bf16[384,128]{1,0:T(8,128)(2,1)S(1)}, u32[]{:S(2)}, u32[]{:S(2)}) collective-permute-start(bf16[384,128]{1,0:T(8,128)(2,1)S(1)} %add_convert_fusion), channel_id=1, source_target_pairs={{0,16},{16,0},{1,17},{17,1},{2,18},{18,2},{3,19},{19,3},{4,20},{20... | collective-permute-start | bytes 294920 | tf_op jit(solution)/shard_map/ppermute | solution.py:234

commit v7 on v5

--- a/solution.py
+++ b/solution.py
@@ -163,15 +163,14 @@
         d_gate = (bar * slope).astype(BF)
         part_gate = dot(zp, d_gate, ((0,), (0,)))
         part_out = dot(xn, d_out, ((0,), (0,)))
-        if at == 0:
-            g_s[1, chans : 2 * chans, :] = part_gate
-            g_s[1, 2 * chans :, :] = part_out
-        else:
-            g_s[1, chans : 2 * chans, :] += part_gate
-            g_s[1, 2 * chans :, :] += part_out
+        g_gate = part_gate if at == 0 else g_gate + part_gate
+        g_out = part_out if at == 0 else g_out + part_out
         dxn = dot(d_out, w_out, ((1,), (1,)))
         dc = centre(dxn)
         xb_s[here, :] = inv * (dc - xhat * jnp.mean(xhat * dxn, axis=1, keepdims=True))
+
+    g_s[1, chans : 2 * chans, :] = g_gate.astype(BF)
+    g_s[1, 2 * chans :, :] = g_out.astype(BF)
 
     chunk = min(width, 64)
 
@@ -197,12 +196,12 @@
         lax.fori_loop(0, count, one, 0, unroll=width <= 64)
         part = dot(z_s[...], d_s[: count * blk, :])
         for n, (half, top) in enumerate(spots):
-            g_s[half, top : top + chans, :] = part[:, n * chans : (n + 1) * chans]
+            g_s[half, top : top + chans, :] = part[:, n * chans : (n + 1) * chans].astype(BF)
 
     back(g1, n_j, lambda i, j: i * n_j + j, b_s, sa_s, ga_s, zi_s, ((0, 0), (0, chans)))
     back(g2, n_i, lambda j, i: i * n_j + j, a_s, sb_s, gb_s, zj_s, ((0, 2 * chans), (1, 0)))
-    keep_ref[...] = g_s[core].astype(BF)
-    send_ref[...] = g_s[1 - core].astype(BF)
+    keep_ref[...] = g_s[core]
+    send_ref[...] = g_s[1 - core]
 
 
 def pair_kernel(cfg, place, pair_ref, y_ref, new_ref):
@@ -290,7 +289,7 @@
         scratch_shapes=[part, part]
         + [pltpu.VMEM(pairs, F32)] * 3
         + [pltpu.VMEM((max(n_i, n_j) * width, 2 * chans), BF)]
-        + [pltpu.VMEM((2, 3 * chans, chans), F32)],
+        + [pltpu.VMEM((2, 3 * chans, chans), BF)],
         compiler_params=params(),
         cost_estimate=cost(5.0),
         name="block",

time: 44.5 us -> 44.5 us (level)
  no operation moved by 1% of the time
where the time goes in v7:
time: 44.5 us; the launch traced here: 44.2 us
  starting transfers between devices  16.7 us (38%)
  waiting for transfers between devices  15.3 us (34%)
  Pallas kernels  9.07 us (20%)
  other arithmetic  2.11 us (5%)
  between operations  0.85 us (2%)
    ppermute x10, starting transfers between devices, swap(): return lax.ppermute(value, ('crop', 'axial'), pairs)  16.6 us
    ppermute x10, waiting for transfers between devices, swap(): return lax.ppermute(value, ('crop', 'axial'), pairs)  12.7 us
    pallas_call x1, Pallas kernels, shards(): pl.pallas_call(functools.partial(block_kernel, cfg), out_shape=[half, hal...  4.88 us
    ppermute x2, waiting for transfers between devices, crop_swap(): return lax.ppermute(value, 'crop', [(i, i ^ bit) for i in range(n_crop)])  2.56 us
    pallas_call x1, Pallas kernels, shards(): pl.pallas_call(functools.partial(line_kernel, cfg), out_shape=side_b + [o...  1.68 us
    pallas_call x1, Pallas kernels, shards(): pl.pallas_call(functools.partial(pair_kernel, cfg), out_shape=shape(own.s...  1.32 us
    pallas_call x1, Pallas kernels, shards(): pl.pallas_call(functools.partial(own_kernel, cfg), out_shape=side_a + sid...  1.19 us
    convert_element_type x1, other arithmetic, shards(): v = ((2 * probe_signs - 1).astype(F32) * unit).astype(BF)  1.05 us
  transfers between devices with their start and end apart: 12, of which 7 were waited for; matrix products, arithmetic and copies ran while one was open for 3% of the time, Pallas kernels for 9%

profile of v7, /device:TPU:0, one launch (start us, length us, event | category | flops | bytes accessed | tf_op | source)
XLA Modules:
  0.0 44.2 jit_solution(13402675149392203868)
XLA Ops:
  0.6 0.0 copy-start.1
  0.6 0.0 copy-start.2
  0.7 0.0 copy-start
  0.7 5.1 %collective-permute-start.3 = (bf16[4,64,128]{2,1,0:T(8,128)(2,1)}, bf16[4,64,128]{2,1,0:T(8,128)(2,1)S(1)}, u32[]{:S(2)}, u32[]{:S(2)}) collective-permute-start(bf16[4,64,128]{2,1,0:T(8,128)(2,1)} %bitcast.21), channel_id=1, source_target_pairs={{0,12},{1,13},{2,14},{3,15},{4,8},{5,9},{6,10},{7,11},{8,4},{9,5},... | collective-permute-start | bytes 196616 | tf_op jit(solution)/shard_map/ppermute | solution.py:240
  5.8 0.0 collective-permute-start.2
  5.8 0.6 %collective-permute-start.1 = (bf16[4,64,128]{2,1,0:T(8,128)(2,1)}, bf16[4,64,128]{2,1,0:T(8,128)(2,1)S(1)}, u32[]{:S(2)}, u32[]{:S(2)}) collective-permute-start(bf16[4,64,128]{2,1,0:T(8,128)(2,1)} %bitcast.23), channel_id=1, source_target_pairs={{0,4},{1,5},{2,6},{3,7},{4,0},{5,1},{6,2},{7,3},{8,12},{9,13},{10,... | collective-permute-start | bytes 196616 | tf_op jit(solution)/shard_map/ppermute | solution.py:240
  6.4 2.6 %collective-permute-start = (bf16[4,64,128]{2,1,0:T(8,128)(2,1)}, bf16[4,64,128]{2,1,0:T(8,128)(2,1)S(1)}, u32[]{:S(2)}, u32[]{:S(2)}) collective-permute-start(bf16[4,64,128]{2,1,0:T(8,128)(2,1)} %bitcast.24), channel_id=1, source_target_pairs={{0,3},{1,2},{2,1},{3,0},{4,7},{5,6},{6,5},{7,4},{8,11},{9,10},{10,... | collective-permute-start | bytes 196616 | tf_op jit(solution)/shard_map/ppermute | solution.py:240
  9.0 1.1 %multiply_convert_fusion.v_ref.v_s = bf16[128,768]{1,0:T(8,128)(2,1)S(1)} fusion(s32[128,768]{1,0:T(8,128)} %param.7), kind=kLoop, calls=%fused_computation | loop fusion | flops 491520 | bytes 589824 | tf_op jit(solution)/shard_map/convert_element_type | solution.py:255
  10.1 0.0 copy-done.1
  10.1 0.6 %collective-permute-start.5 = (bf16[4,64,128]{2,1,0:T(8,128)(2,1)S(1)}, bf16[4,64,128]{2,1,0:T(8,128)(2,1)S(1)}, u32[]{:S(2)}, u32[]{:S(2)}) collective-permute-start(bf16[4,64,128]{2,1,0:T(8,128)(2,1)S(1)} %bitcast.25), channel_id=1, source_target_pairs={{0,2},{1,3},{2,0},{3,1},{4,6},{5,7},{6,4},{7,5},{8,10},{9,11},{10,... | collective-permute-start | bytes 196616 | tf_op jit(solution)/shard_map/ppermute | solution.py:240
  10.6 0.0 copy-done.2
  10.7 0.0 collective-permute-done.3.rest_2_
  10.7 0.5 %collective-permute-start.4 = (bf16[4,64,128]{2,1,0:T(8,128)(2,1)S(1)}, bf16[4,64,128]{2,1,0:T(8,128)(2,1)S(1)}, u32[]{:S(2)}, u32[]{:S(2)}) collective-permute-start(bf16[4,64,128]{2,1,0:T(8,128)(2,1)S(1)} %bitcast.26), channel_id=1, source_target_pairs={{0,1},{1,0},{2,3},{3,2},{4,5},{5,4},{6,7},{7,6},{8,9},{9,8},{10,11... | collective-permute-start | bytes 196616 | tf_op jit(solution)/shard_map/ppermute | solution.py:240
  11.1 0.1 pad_add_fusion.place
  11.2 0.9 %collective-permute-done.far_ref = bf16[4,64,128]{2,1,0:T(8,128)(2,1)S(1)} collective-permute-done((bf16[4,64,128]{2,1,0:T(8,128)(2,1)}, bf16[4,64,128]{2,1,0:T(8,128)(2,1)S(1)}, u32[]{:S(2)}, u32[]{:S(2)}) %collective-permute-start) | collective-permute-done | bytes 65568 | tf_op jit(solution)/shard_map/ppermute | solution.py:240
  12.1 0.1 broadcast_in_dim.4.mask_v
  12.2 0.0 copy-done
  12.2 1.2 %own_rows.1 = (bf16[128,1024]{1,0:T(8,128)(2,1)S(1)}, f32[1024,128]{1,0:T(8,128)S(1)}, f32[1024,128]{1,0:T(8,128)S(1)}, f32[1024,128]{1,0:T(8,128)S(1)}, f32[102...) custom-call(s32[2]{0:T(128)S(1)} %pad_add_fusion.place, ...), custom_call_target="tpu_custom_call" | custom-call | flops 10000000 | tf_op jit(solution)/shard_map/own_rows/pallas_call | solution.py:260
  13.4 0.0 collective-permute-done.2.rest_1_
  13.4 0.0 collective-permute-done.1.rest_0_
  13.4 1.7 %line.1 = (bf16[128,1024]{1,0:T(8,128)(2,1)S(1)}, f32[1024,128]{1,0:T(8,128)S(1)}, f32[1024,128]{1,0:T(8,128)S(1)}, f32[1024,128]{1,0:T(8,128)S(1)}, f32[1024,12...) custom-call(s32[2]{0:T(128)S(1)} %pad_add_fusion.place, ...), custom_call_target="tpu_custom_call", output_to_operand_aliasing={{0}: (10, {}), {1}: (11, {}), {2}: (12, {}), {3}: (13, {}),... | custom-call | flops 10000000 | tf_op jit(solution)/shard_map/line/pallas_call | solution.py:271
  15.1 0.0 collective-permute-done.5.rest_1_
  15.1 0.0 collective-permute-done.4.rest_0_
  15.1 4.9 %block.1 = (bf16[384,128]{1,0:T(8,128)(2,1)S(1)}, bf16[384,128]{1,0:T(8,128)(2,1)S(1)}, bf16[256,128]{1,0:T(8,128)(2,1)S(1)}, bf16[128,1024]{1,0:T(8,128)(2,1)S(...) custom-call(s32[2]{0:T(128)S(1)} %pad_add_fusion.place, ...), custom_call_target="tpu_custom_call", output_to_operand_aliasing={{3}: (14, {}), {4}: (15, {}), {5}: (16, {}), {6}: (17, {}),... | custom-call | flops 5000000000 | tf_op jit(solution)/shard_map/block/pallas_call | solution.py:283
  20.0 0.1 collective-permute-start.6
  20.1 1.3 %collective-permute-done.6 = bf16[384,128]{1,0:T(8,128)(2,1)S(1)} collective-permute-done((bf16[384,128]{1,0:T(8,128)(2,1)S(1)}, bf16[384,128]{1,0:T(8,128)(2,1)S(1)}, u32[]{:S(2)}, u32[]{:S(2)}) %collective-permute-start.6) | collective-permute-done | bytes 98336 | tf_op jit(solution)/shard_map/ppermute | solution.py:232
  21.4 1.4 %collective-permute-start.7 = (bf16[512,128]{1,0:T(8,128)(2,1)S(1)}, bf16[512,128]{1,0:T(8,128)(2,1)S(1)}, u32[]{:S(2)}, u32[]{:S(2)}) collective-permute-start(bf16[512,128]{1,0:T(8,128)(2,1)S(1)} %pad_maximum_fusion), channel_id=1, source_target_pairs={{0,1},{1,0},{2,3},{3,2},{4,5},{5,4},{6,7},{7,6},{8,9},{9,8},{10,11... | collective-permute-start | bytes 393224 | tf_op jit(solution)/shard_map/ppermute | solution.py:240
  22.8 3.6 %collective-permute-done.7 = bf16[512,128]{1,0:T(8,128)(2,1)S(1)} collective-permute-done((bf16[512,128]{1,0:T(8,128)(2,1)S(1)}, bf16[512,128]{1,0:T(8,128)(2,1)S(1)}, u32[]{:S(2)}, u32[]{:S(2)}) %collective-permute-start.7) | collective-permute-done | bytes 131104 | tf_op jit(solution)/shard_map/ppermute | solution.py:240
  26.6 1.8 %collective-permute-start.8 = (bf16[512,128]{1,0:T(8,128)(2,1)S(1)}, bf16[512,128]{1,0:T(8,128)(2,1)S(1)}, u32[]{:S(2)}, u32[]{:S(2)}) collective-permute-start(bf16[512,128]{1,0:T(8,128)(2,1)S(1)} %pad_maximum_fusion.1), channel_id=1, source_target_pairs={{0,2},{1,3},{2,0},{3,1},{4,6},{5,7},{6,4},{7,5},{8,10},{9,11},{10,... | collective-permute-start | bytes 393224 | tf_op jit(solution)/shard_map/ppermute | solution.py:240
  28.4 3.2 %collective-permute-done.8 = bf16[512,128]{1,0:T(8,128)(2,1)S(1)} collective-permute-done((bf16[512,128]{1,0:T(8,128)(2,1)S(1)}, bf16[512,128]{1,0:T(8,128)(2,1)S(1)}, u32[]{:S(2)}, u32[]{:S(2)}) %collective-permute-start.8) | collective-permute-done | bytes 131104 | tf_op jit(solution)/shard_map/ppermute | solution.py:240
  31.6 1.5 %collective-permute-start.9 = (bf16[384,128]{1,0:T(8,128)(2,1)S(1)}, bf16[384,128]{1,0:T(8,128)(2,1)S(1)}, u32[]{:S(2)}, u32[]{:S(2)}) collective-permute-start(bf16[384,128]{1,0:T(8,128)(2,1)S(1)} %add_convert_fusion.2), channel_id=1, source_target_pairs={{0,4},{1,5},{2,6},{3,7},{4,0},{5,1},{6,2},{7,3},{8,12},{9,13},{10,... | collective-permute-start | bytes 294920 | tf_op jit(solution)/shard_map/ppermute | solution.py:240
  33.1 1.3 %new_pair.1 = bf16[4,64,128]{2,1,0:T(8,128)(2,1)} custom-call(s32[2]{0:T(128)S(1)} %pad_add_fusion.place, bf16[4,64,128]{2,1,0:T(8,128)(2,1)S(1)} %bitcast.28, bf16[4,64,128]{2,1,0:T(8,128)(2,1)S(1)} %maximum_bitcast_fusion.1.y_ref), custom_call_target="tpu_custom_call" | custom-call | flops 500000000 | tf_op jit(solution)/shard_map/new_pair/pallas_call | solution.py:315
  34.4 1.9 %collective-permute-done.9 = bf16[384,128]{1,0:T(8,128)(2,1)S(1)} collective-permute-done((bf16[384,128]{1,0:T(8,128)(2,1)S(1)}, bf16[384,128]{1,0:T(8,128)(2,1)S(1)}, u32[]{:S(2)}, u32[]{:S(2)}) %collective-permute-start.9) | collective-permute-done | bytes 98336 | tf_op jit(solution)/shard_map/ppermute | solution.py:240
  36.3 2.6 %collective-permute-start.10 = (bf16[384,128]{1,0:T(8,128)(2,1)S(1)}, bf16[384,128]{1,0:T(8,128)(2,1)S(1)}, u32[]{:S(2)}, u32[]{:S(2)}) collective-permute-start(bf16[384,128]{1,0:T(8,128)(2,1)S(1)} %add_convert_fusion.1), channel_id=1, source_target_pairs={{0,8},{1,9},{2,10},{3,11},{4,12},{5,13},{6,14},{7,15},{8,0},{9,1},... | collective-permute-start | bytes 294920 | tf_op jit(solution)/shard_map/ppermute | solution.py:240
  38.9 3.0 %collective-permute-done.10 = bf16[384,128]{1,0:T(8,128)(2,1)S(1)} collective-permute-done((bf16[384,128]{1,0:T(8,128)(2,1)S(1)}, bf16[384,128]{1,0:T(8,128)(2,1)S(1)}, u32[]{:S(2)}, u32[]{:S(2)}) %collective-permute-start.10) | collective-permute-done | bytes 98336 | tf_op jit(solution)/shard_map/ppermute | solution.py:240
  42.0 0.1 collective-permute-start.11
  42.1 1.3 %collective-permute-done.11 = bf16[384,128]{1,0:T(8,128)(2,1)S(1)} collective-permute-done((bf16[384,128]{1,0:T(8,128)(2,1)S(1)}, bf16[384,128]{1,0:T(8,128)(2,1)S(1)}, u32[]{:S(2)}, u32[]{:S(2)}) %collective-permute-start.11) | collective-permute-done | bytes 98336 | tf_op jit(solution)/shard_map/ppermute | solution.py:232
  43.5 0.8 %concatenate.23 = f32[128,768]{1,0:T(8,128)} convert(bf16[128,768]{1,0:T(8,128)(2,1)S(1)} %slice_dynamic-update-slice_fusion) | non-fusion elementwise | flops 98304 | bytes 589824 | tf_op jit(solution)/shard_map/concatenate | solution.py:332
  (21 shorter events, 0.3 us)
Async XLA Ops:
  0.6 9.4 %copy-start.1 = (bf16[1,4,64,128]{3,2,1,0:T(8,128)(2,1)S(1)}, bf16[1,4,64,128]{3,2,1,0:T(8,128)(2,1)}, u32[]{:S(2)}) copy-start(bf16[1,4,64,128]{3,2,1,0:T(8,128)(2,1)} %param.4) | copy-start | bytes 196612
  0.6 10.0 %copy-start.2 = (s32[1,64]{1,0:T(1,128)S(1)}, s32[1,64]{1,0:T(1,128)}, u32[]{:S(2)}) copy-start(s32[1,64]{1,0:T(1,128)} %mask_s.5) | copy-start | bytes 772
  0.7 11.6 %copy-start = (bf16[128,768]{1,0:T(8,128)(2,1)S(1)}, bf16[128,768]{1,0:T(8,128)(2,1)}, u32[]{:S(2)}) copy-start(bf16[128,768]{1,0:T(8,128)(2,1)} %w_ref.5) | copy-start | bytes 589828
  0.7 10.0 %collective-permute-start.3 = (bf16[4,64,128]{2,1,0:T(8,128)(2,1)}, bf16[4,64,128]{2,1,0:T(8,128)(2,1)S(1)}, u32[]{:S(2)}, u32[]{:S(2)}) collective-permute-start(bf16[4,64,128]{2,1,0:T(8,128)(2,1)} %bitcast.21), channel_id=1, source_target_pairs={{0,12},{1,13},{2,14},{3,15},{4,8},{5,9},{6,10},{7,11},{8,4},{9,5},... | collective-permute-start | bytes 196616 | tf_op jit(solution)/shard_map/ppermute | solution.py:240
  5.8 7.6 %collective-permute-start.2 = (bf16[4,64,128]{2,1,0:T(8,128)(2,1)}, bf16[4,64,128]{2,1,0:T(8,128)(2,1)S(1)}, u32[]{:S(2)}, u32[]{:S(2)}) collective-permute-start(bf16[4,64,128]{2,1,0:T(8,128)(2,1)} %bitcast.22), channel_id=1, source_target_pairs={{0,8},{1,9},{2,10},{3,11},{4,12},{5,13},{6,14},{7,15},{8,0},{9,1},... | collective-permute-start | bytes 196616 | tf_op jit(solution)/shard_map/ppermute | solution.py:240
  5.8 7.6 %collective-permute-start.1 = (bf16[4,64,128]{2,1,0:T(8,128)(2,1)}, bf16[4,64,128]{2,1,0:T(8,128)(2,1)S(1)}, u32[]{:S(2)}, u32[]{:S(2)}) collective-permute-start(bf16[4,64,128]{2,1,0:T(8,128)(2,1)} %bitcast.23), channel_id=1, source_target_pairs={{0,4},{1,5},{2,6},{3,7},{4,0},{5,1},{6,2},{7,3},{8,12},{9,13},{10,... | collective-permute-start | bytes 196616 | tf_op jit(solution)/shard_map/ppermute | solution.py:240
  6.4 5.7 %collective-permute-start = (bf16[4,64,128]{2,1,0:T(8,128)(2,1)}, bf16[4,64,128]{2,1,0:T(8,128)(2,1)S(1)}, u32[]{:S(2)}, u32[]{:S(2)}) collective-permute-start(bf16[4,64,128]{2,1,0:T(8,128)(2,1)} %bitcast.24), channel_id=1, source_target_pairs={{0,3},{1,2},{2,1},{3,0},{4,7},{5,6},{6,5},{7,4},{8,11},{9,10},{10,... | collective-permute-start | bytes 196616 | tf_op jit(solution)/shard_map/ppermute | solution.py:240
  10.1 5.0 %collective-permute-start.5 = (bf16[4,64,128]{2,1,0:T(8,128)(2,1)S(1)}, bf16[4,64,128]{2,1,0:T(8,128)(2,1)S(1)}, u32[]{:S(2)}, u32[]{:S(2)}) collective-permute-start(bf16[4,64,128]{2,1,0:T(8,128)(2,1)S(1)} %bitcast.25), channel_id=1, source_target_pairs={{0,2},{1,3},{2,0},{3,1},{4,6},{5,7},{6,4},{7,5},{8,10},{9,11},{10,... | collective-permute-start | bytes 196616 | tf_op jit(solution)/shard_map/ppermute | solution.py:240
  10.7 4.5 %collective-permute-start.4 = (bf16[4,64,128]{2,1,0:T(8,128)(2,1)S(1)}, bf16[4,64,128]{2,1,0:T(8,128)(2,1)S(1)}, u32[]{:S(2)}, u32[]{:S(2)}) collective-permute-start(bf16[4,64,128]{2,1,0:T(8,128)(2,1)S(1)} %bitcast.26), channel_id=1, source_target_pairs={{0,1},{1,0},{2,3},{3,2},{4,5},{5,4},{6,7},{7,6},{8,9},{9,8},{10,11... | collective-permute-start | bytes 196616 | tf_op jit(solution)/shard_map/ppermute | solution.py:240
  20.0 1.4 %collective-permute-start.6 = (bf16[384,128]{1,0:T(8,128)(2,1)S(1)}, bf16[384,128]{1,0:T(8,128)(2,1)S(1)}, u32[]{:S(2)}, u32[]{:S(2)}) collective-permute-start(bf16[384,128]{1,0:T(8,128)(2,1)S(1)} %get-tuple-element.54), channel_id=1, source_target_pairs={{0,16},{16,0},{1,17},{17,1},{2,18},{18,2},{3,19},{19,3},{4,20},{20... | collective-permute-start | bytes 294920 | tf_op jit(solution)/shard_map/ppermute | solution.py:232
  21.4 5.0 %collective-permute-start.7 = (bf16[512,128]{1,0:T(8,128)(2,1)S(1)}, bf16[512,128]{1,0:T(8,128)(2,1)S(1)}, u32[]{:S(2)}, u32[]{:S(2)}) collective-permute-start(bf16[512,128]{1,0:T(8,128)(2,1)S(1)} %pad_maximum_fusion), channel_id=1, source_target_pairs={{0,1},{1,0},{2,3},{3,2},{4,5},{5,4},{6,7},{7,6},{8,9},{9,8},{10,11... | collective-permute-start | bytes 393224 | tf_op jit(solution)/shard_map/ppermute | solution.py:240
  26.6 5.0 %collective-permute-start.8 = (bf16[512,128]{1,0:T(8,128)(2,1)S(1)}, bf16[512,128]{1,0:T(8,128)(2,1)S(1)}, u32[]{:S(2)}, u32[]{:S(2)}) collective-permute-start(bf16[512,128]{1,0:T(8,128)(2,1)S(1)} %pad_maximum_fusion.1), channel_id=1, source_target_pairs={{0,2},{1,3},{2,0},{3,1},{4,6},{5,7},{6,4},{7,5},{8,10},{9,11},{10,... | collective-permute-start | bytes 393224 | tf_op jit(solution)/shard_map/ppermute | solution.py:240
  31.6 4.7 %collective-permute-start.9 = (bf16[384,128]{1,0:T(8,128)(2,1)S(1)}, bf16[384,128]{1,0:T(8,128)(2,1)S(1)}, u32[]{:S(2)}, u32[]{:S(2)}) collective-permute-start(bf16[384,128]{1,0:T(8,128)(2,1)S(1)} %add_convert_fusion.2), channel_id=1, source_target_pairs={{0,4},{1,5},{2,6},{3,7},{4,0},{5,1},{6,2},{7,3},{8,12},{9,13},{10,... | collective-permute-start | bytes 294920 | tf_op jit(solution)/shard_map/ppermute | solution.py:240
  36.3 5.6 %collective-permute-start.10 = (bf16[384,128]{1,0:T(8,128)(2,1)S(1)}, bf16[384,128]{1,0:T(8,128)(2,1)S(1)}, u32[]{:S(2)}, u32[]{:S(2)}) collective-permute-start(bf16[384,128]{1,0:T(8,128)(2,1)S(1)} %add_convert_fusion.1), channel_id=1, source_target_pairs={{0,8},{1,9},{2,10},{3,11},{4,12},{5,13},{6,14},{7,15},{8,0},{9,1},... | collective-permute-start | bytes 294920 | tf_op jit(solution)/shard_map/ppermute | solution.py:240
  42.0 1.4 %collective-permute-start.11 = (bf16[384,128]{1,0:T(8,128)(2,1)S(1)}, bf16[384,128]{1,0:T(8,128)(2,1)S(1)}, u32[]{:S(2)}, u32[]{:S(2)}) collective-permute-start(bf16[384,128]{1,0:T(8,128)(2,1)S(1)} %add_convert_fusion), channel_id=1, source_target_pairs={{0,16},{16,0},{1,17},{17,1},{2,18},{18,2},{3,19},{19,3},{4,20},{20... | collective-permute-start | bytes 294920 | tf_op jit(solution)/shard_map/ppermute | solution.py:232
